TPU v7x, 512 devices: a whole 4x4x16 slice. The times are simulated.
512 devices in a mesh: db: 128 (over x, z, core), pb: 4 (over y).
Axes of the slice: x: 4, y: 4, z: 16, core: 2. Of those that a mesh axis runs over, the one named last changes fastest.
Arguments:
- keys: float32 [13312, 384], P(('db', 'pb')), may hold values from -6 to 6
- slab: float32 [12288, 384], P('db'), may hold values from -6 to 6
- neighbour_ids: int32 [13312, 2], P(('db', 'pb')), may hold values from 0 to 12287, as said below
- group_acts: bfloat16 [13312, 4, 896], P(('db', 'pb')), may hold values from -48 to 48
- table: bfloat16 [12288, 4, 896], P('db'), may hold values from -6 to 6
- norm_gain: float32 [896], replicated, may hold values from 0.1 to 1.9
- w_query: bfloat16 [896, 448], P('pb'), may hold values from -0.1875 to 0.1875
- w_key: bfloat16 [896, 448], P('pb'), may hold values from -0.1875 to 0.1875
- w_value: bfloat16 [896, 448], P('pb'), may hold values from -0.1875 to 0.1875
- w_out: bfloat16 [448, 896], P('pb'), may hold values from -0.25 to 0.25
Outputs:
- best: float32 [13312, 2], P(('db', 'pb'))
- encoded: bfloat16 [13312, 2, 4, 896], P(('db', 'pb'))
Inputs may be any that keep to these rules, and one draw needn't show every extreme that they name: `neighbour_ids`: the owner of a neighbour is its id // 96. Among the 52 neighbours in the rows of one device (aligned blocks of 26 rows, devices in the order db+pb), no owner appears more than 2 times and some owner exactly 2 times; a group's two neighbours differ.
All inputs are finite; a program needn't handle non-finite values.
Results may differ from a plain program's by a relative error of at most 0.012.
Values may be sent and summed in bfloat16 or wider, within the bound.
No kernel may reach another device: no remote copies, remote signals or barrier semaphores. Data moves between devices by JAX's collectives and lax.ppermute only.
A program may use at most 64 MiB of HBM per device.

v0:
```python
import math

import jax
import jax.numpy as jnp
from jax import lax
from jax.sharding import Mesh
from jax.sharding import PartitionSpec as P

HEADS = 7
CAP = 2
DB = ("db_0", "db_1", "db_2")
DB_PB = ("db_0", "db_1", "db_2", "pb")


def sent_together(arrays, axis, dim, along):
    both = jnp.concatenate(arrays, axis=along)
    whole, at, done = (lax.all_gather(both, axis, axis=dim, tiled=True), 0, [])
    for a in arrays:
        done.append(lax.slice_in_dim(whole, at, at + a.shape[along], axis=along))
        at += a.shape[along]
    return tuple(done)


def cut_along(array, dim, size):
    shape = array.shape
    blocks = array.reshape(*shape[:dim], size, shape[dim] // size, *shape[dim + 1 :])
    return jnp.moveaxis(blocks, dim, 0)


def in_order(blocks, dim):
    shape = list(blocks.shape[1:])
    shape[dim] *= blocks.shape[0]
    return jnp.moveaxis(blocks, 0, dim).reshape(shape)


def turned_blocks(blocks, axes, order):
    shape = [lax.axis_size(a) for a in axes]
    blocks = blocks.reshape(*shape, *blocks.shape[1:])
    for k in order:
        blocks = lax.all_to_all(blocks, axes[k], split_axis=k, concat_axis=k, tiled=True)
    return blocks.reshape(-1, *blocks.shape[len(axes) :])


def two_step_exchange(array, groups, order, split_dim, concat_dim):
    size = lax.axis_size(groups[0]) * lax.axis_size(groups[1])
    blocks = cut_along(array, split_dim, size)
    return in_order(turned_blocks(blocks, groups, order), concat_dim)


def norm_rows(x, gain):
    values = x.astype(jnp.float32)
    square = jnp.mean(values * values, axis=-1, keepdims=True)
    return (values * lax.rsqrt(square + 1e-06) * gain).astype(jnp.bfloat16)


def attend(x, keyed, value_weighted, w_query, w_out, gain, heads):
    count, ntok, width = x.shape
    ctok = keyed.shape[1]
    hsize = w_query.shape[1] // heads
    rescaled_states = norm_rows(x, gain)
    query = jnp.dot(
        rescaled_states.reshape(count * ntok, width), w_query, preferred_element_type=jnp.float32
    ).astype(jnp.bfloat16)
    query = query.reshape(count, ntok, heads, hsize)
    khead = keyed.reshape(count, ctok, heads, hsize)
    vhead = value_weighted.reshape(count, ctok, heads, hsize)
    logits = jnp.einsum(
        "snhd,schd->shnc", query, khead, preferred_element_type=jnp.float32
    ) / math.sqrt(hsize)
    probs = jax.nn.softmax(logits, axis=-1).astype(jnp.bfloat16)
    mixed = jnp.einsum("shnc,schd->snhd", probs, vhead, preferred_element_type=jnp.float32).astype(
        jnp.bfloat16
    )
    mixed = mixed.reshape(count * ntok, heads * hsize)
    result = x.reshape(count * ntok, width).astype(jnp.float32) + jnp.dot(
        mixed, w_out, preferred_element_type=jnp.float32
    )
    return result.astype(jnp.bfloat16).reshape(count, ntok, width)


def per_device(
    keys, slab, neighbour_ids, group_acts, table, norm_gain, w_query, w_key, w_value, w_out
):
    groups = keys.shape[0]
    rows_dev = slab.shape[0]
    ctok = group_acts.shape[1]
    width = table.shape[2]
    ntok = table.shape[1]
    w_query, w_key, w_value, w_out = (
        *sent_together((w_query, w_key, w_value), "pb", 0, 1),
        lax.all_gather(w_out, "pb", axis=0, tiled=True),
    )
    scale = 1.0 / math.sqrt(keys.shape[1])
    lookup_match_rating = (
        jnp.einsum(
            "qk,rk->qr",
            lax.all_gather(keys.astype(jnp.bfloat16), DB, axis=0, tiled=True).astype(jnp.float32),
            slab,
            precision=lax.Precision.HIGHEST,
            preferred_element_type=jnp.float32,
        )
        * scale
    )
    candidates = lax.top_k(lookup_match_rating, 2)[0]
    received = lax.all_to_all(candidates, DB, split_axis=0, concat_axis=1, tiled=True)
    best = lax.top_k(received, 2)[0]
    peers = lax.axis_size(DB)
    pairs = 2 * groups
    flat_ids = neighbour_ids.reshape(pairs)
    owner = flat_ids // rows_dev
    local_row = flat_ids % rows_dev
    positions = lax.iota(jnp.int32, pairs)
    earlier = (owner[:, None] == owner[None, :]) & (positions[:, None] > positions[None, :])
    rank = jnp.sum(earlier.astype(jnp.int32), axis=1)
    slot = owner * CAP + rank
    dispatch = (lax.iota(jnp.int32, peers * CAP)[:, None] == slot[None, :]).astype(jnp.bfloat16)
    marks = jnp.dot(
        dispatch, (local_row + 1).astype(jnp.bfloat16)[:, None], preferred_element_type=jnp.float32
    )
    marks = marks.astype(jnp.bfloat16).reshape(peers, CAP)
    row_labels = (lax.iota(jnp.int32, rows_dev) + 1).astype(jnp.bfloat16)
    flat_table = table.reshape(rows_dev, ntok * width)
    wanted = lax.all_to_all(marks, DB, split_axis=0, concat_axis=0, tiled=True)
    count = wanted.shape[0] * wanted.shape[1]
    select = (wanted.reshape(count)[:, None] == row_labels[None, :]).astype(jnp.bfloat16)
    found = jnp.dot(select, flat_table, preferred_element_type=jnp.float32).astype(jnp.bfloat16)
    found = found.reshape(wanted.shape[0], wanted.shape[1], ntok * width)
    arrived = two_step_exchange(found, (("db_0", "db_1"), "db_2"), (1, 0), 0, 0)
    states = jnp.einsum(
        "sp,sf->pf",
        dispatch,
        arrived.reshape(peers * CAP, ntok * width),
        preferred_element_type=jnp.float32,
    )
    states = states.astype(jnp.bfloat16).reshape(pairs, ntok, width)
    rows = group_acts.reshape(groups * ctok, width)
    keyed = jnp.dot(rows, w_key, preferred_element_type=jnp.float32).astype(jnp.bfloat16)
    value_weighted = jnp.dot(rows, w_value, preferred_element_type=jnp.float32).astype(jnp.bfloat16)
    keyed, value_weighted = (
        keyed.reshape(groups, ctok, -1),
        value_weighted.reshape(groups, ctok, -1),
    )
    keyed = jnp.repeat(keyed, 2, axis=0)
    value_weighted = jnp.repeat(value_weighted, 2, axis=0)
    encoded = attend(states, keyed, value_weighted, w_query, w_out, norm_gain, HEADS).reshape(
        groups, 2, ntok, width
    )
    return (best, encoded)


def solution(mesh):
    split = Mesh(mesh.devices.reshape(4, 16, 2, mesh.shape["pb"]), ("db_0", "db_1", "db_2", "pb"))
    return jax.shard_map(
        per_device,
        mesh=split,
        in_specs=(
            P(DB_PB, None),
            P(DB, None),
            P(DB_PB, None),
            P(DB_PB, None, None),
            P(DB, None, None),
            P(),
            P("pb", None),
            P("pb", None),
            P("pb", None),
            P("pb", None),
        ),
        out_specs=(P(DB_PB, None), P(DB_PB, None, None, None)),
        check_vma=False,
    )
```

profile of v0, /device:TPU:6, one launch (start us, length us, event | category | flops | bytes accessed | tf_op | source)
XLA Modules:
  0.0 358.1 jit_solution(18028475150385619712)
XLA Ops:
  8.0 0.0 copy-start
  8.0 0.0 all-gather.6.cloned.1.call-start
  8.1 1.4 convert_bitcast_fusion
  9.5 0.0 all-gather.6.cloned.1.call-update
  9.5 0.7 broadcast_remainder_fusion
  10.2 0.1 copy.50
  10.3 0.1 div.41
  10.4 0.7 sign_compare_fusion
  11.1 0.1 copy.48
  11.2 0.1 ne.55
  11.3 0.1 copy.49
  11.4 0.1 rem.32
  11.5 0.2 convert_reduce_fusion
  11.7 0.2 fusion.17
  11.9 0.8 all_to_all.34
  12.7 19.9 %all-to-all-start.1 = ((bf16[128,1,2]{2,1,0:T(2,128)(2,1)}), bf16[128,1,2]{2,1,0:T(2,128)(2,1)S(1)}, u32[]{:S(2)}, u32[]{:S(2)}) async-start(bf16[128,1,2]{2,1,0:T(2,128)(2,1)} %all_to_all.34), calls=%async_computation.1 | async-start | bytes 131072 | tf_op jit(solution)/shard_map/all_to_all | solution.py:123
  32.6 1.2 copy.60
  33.8 12.2 %all-to-all-done.1 = bf16[128,1,2]{2,1,0:T(2,128)(2,1)S(1)} async-done(((bf16[128,1,2]{2,1,0:T(2,128)(2,1)}), bf16[128,1,2]{2,1,0:T(2,128)(2,1)S(1)}, u32[]{:S(2)}, u32[]{:S(2)}) %all-to-all-start.1) | async-done | bytes 544 | tf_op jit(solution)/shard_map/all_to_all | solution.py:123
  46.0 0.2 reduce
  46.2 0.1 eq.49
  46.3 0.7 convolution_convert_fusion
  47.0 1.7 reshape_reshape_reshape.6
  48.7 4.0 %copy.52 = bf16[64,2,1,2,3584]{4,3,0,2,1:T(2,128)(2,1)} copy(bf16[64,2,1,2,3584]{4,3,1,0,2:T(2,128)(2,1)} %reshape_reshape_reshape.6) | data formatting | bytes 3670016 | tf_op jit(solution)/shard_map/reshape;reshape;reshape | solution.py:38
  52.7 4.7 %all-to-all-start.2 = ((bf16[64,2,1,2,3584]{4,3,0,2,1:T(2,128)(2,1)}), bf16[64,2,1,2,3584]{4,3,0,2,1:T(2,128)(2,1)}, u32[]{:S(2)}, u32[]{:S(2)}) async-start(bf16[64,2,1,2,3584]{4,3,0,2,1:T(2,128)(2,1)} %copy.52), calls=%async_computation.2 | async-start | bytes 3670016 | tf_op jit(solution)/shard_map/all_to_all | solution.py:40
  57.4 99.0 %all-gather.6.cloned.1.call-done = bf16[128,26,384]{2,1,0:T(8,128)(2,1)} async-done(((bf16[1,26,384]{2,1,0:T(8,128)(2,1)}), bf16[128,26,384]{2,1,0:T(8,128)(2,1)}) %all-gather.6.cloned.1.call-update) | async-done | bytes 2555920 | tf_op jit(solution)/shard_map/all_gather | solution.py:97
  156.4 3.8 %reshape.131 = bf16[3328,384]{1,0:T(8,128)(2,1)S(1)} reshape(bf16[128,26,384]{2,1,0:T(8,128)(2,1)} %all-gather.6.cloned.1.call-done) | data formatting | bytes 5111808
  160.2 3.3 convolution_multiply_fusion
  163.5 51.7 %top_k.14 = (f32[3328,2]{0,1:T(2,128)S(1)}, s32[3328,2]{0,1:T(2,128)}) custom-call(f32[3328,96]{0,1:T(8,128)} %convolution_multiply_fusion), custom_call_target="TopK", called_computations={%compare_greater_than.1.1.clone.clone} | custom-call | tf_op jit(solution)/shard_map/top_k | solution.py:104
  215.2 0.2 all_to_all.26
  215.4 0.8 copy.47
  216.1 13.0 %all-to-all-start = ((f32[128,26,2]{1,2,0:T(2,128)}), f32[128,26,2]{1,2,0:T(2,128)S(1)}, u32[]{:S(2)}, u32[]{:S(2)}) async-start(f32[128,26,2]{1,2,0:T(2,128)} %copy.47), calls=%async_computation | async-start | bytes 262144 | tf_op jit(solution)/shard_map/all_to_all | solution.py:105
  229.1 4.0 %copy.53 = bf16[64,2,1,2,3584]{4,3,1,2,0:T(2,128)(2,1)} copy(bf16[64,2,1,2,3584]{4,3,0,2,1:T(2,128)(2,1)} %all-to-all-done.2) | data formatting | bytes 3670016 | tf_op jit(solution)/shard_map/all_to_all | solution.py:40
  233.1 12.0 %all-to-all-done = f32[128,26,2]{1,2,0:T(2,128)S(1)} async-done(((f32[128,26,2]{1,2,0:T(2,128)}), f32[128,26,2]{1,2,0:T(2,128)S(1)}, u32[]{:S(2)}, u32[]{:S(2)}) %all-to-all-start) | async-done | bytes 26656 | tf_op jit(solution)/shard_map/all_to_all | solution.py:105
  245.1 7.2 %all-to-all-start.3 = ((bf16[64,2,1,2,3584]{4,3,1,2,0:T(2,128)(2,1)}), bf16[64,2,1,2,3584]{4,3,1,2,0:T(2,128)(2,1)S(1)}, u32[]{:S(2)}, u32[]{:S(2)}) async-start(bf16[64,2,1,2,3584]{4,3,1,2,0:T(2,128)(2,1)} %copy.53), calls=%async_computation.3 | async-start | bytes 3670016 | tf_op jit(solution)/shard_map/all_to_all | solution.py:40
  252.3 0.0 copy-start.7
  252.4 0.0 copy-start.6
  252.4 0.0 all-gather.4.cloned.1.call-start
  252.5 1.1 concatenate.3
  253.5 0.0 all-gather.4.cloned.1.call-update
  253.6 14.2 %all_gather.11 = bf16[448,896]{1,0:T(8,128)(2,1)S(1)} all-gather(bf16[112,896]{1,0:T(8,128)(2,1)S(1)} %copy-done.6), channel_id=1, replica_groups=mesh['db_0'=4,'db_1'=16,'db_2'=2,'pb'=4] {'pb'}, dimensions={0}, use_global_device_ids=true | all-gather | bytes 1003520 | tf_op jit(solution)/shard_map/all_gather | solution.py:91
  267.8 29.6 %all-gather.4.cloned.1.call-done = bf16[896,1344]{1,0:T(8,128)(2,1)} async-done(((bf16[224,1344]{1,0:T(8,128)(2,1)}), bf16[896,1344]{1,0:T(8,128)(2,1)}) %all-gather.4.cloned.1.call-update) | async-done | bytes 2408464 | tf_op jit(solution)/shard_map/all_gather | solution.py:17
  297.4 1.7 fusion.7
  299.2 0.1 broadcast_in_dim.5
  299.3 1.0 reshape_reshape.11
  300.3 1.5 fusion.6
  301.8 0.1 broadcast_in_dim.4
  301.9 1.0 reshape_reshape.10
  302.9 1.8 top_k.15
  304.7 34.0 %all-to-all-done.3 = bf16[64,2,1,2,3584]{4,3,1,2,0:T(2,128)(2,1)S(1)} async-done(((bf16[64,2,1,2,3584]{4,3,1,2,0:T(2,128)(2,1)}), bf16[64,2,1,2,3584]{4,3,1,2,0:T(2,128)(2,1)S(1)}, u32[]{:S(2)}, u32[]{:S(2)}) %all-to-all-start.3) | async-done | bytes 1835040 | tf_op jit(solution)/shard_map/all_to_all | solution.py:40
  338.8 1.7 reshape_reshape_reshape.7
  340.4 2.0 fusion.44
  342.4 0.0 copy-start.8
  342.4 0.2 reshape.129
  342.6 0.3 mul.45
  342.9 0.2 reduce_sum.28
  343.1 0.1 rsqrt.12
  343.2 1.6 convolution_convert_fusion.3
  344.8 0.3 reshape.126
  345.2 2.1 fusion.45
  347.3 1.7 fusion.5
  349.0 0.1 copy.58
  349.1 0.3 reshape.128
  349.4 0.4 fusion.4
  349.8 0.8 reshape_reshape.12
  (23 shorter events, 0.2 us)
Async XLA Ops:
  8.0 152.2 %copy-start = (f32[96,384]{1,0:T(8,128)S(1)}, f32[96,384]{1,0:T(8,128)}, u32[]{:S(2)}) copy-start(f32[96,384]{1,0:T(8,128)} %param.11) | copy-start | bytes 442372
  8.0 148.4 %all-gather.6.cloned.1.call-start = ((), (), s32[]{:S(2)}) async-start(), calls=%async_computation.5 | async-start | bytes 3170304 | tf_op jit(solution)/shard_map/all_gather | solution.py:97
  12.7 33.3 %all-to-all-start.1 = ((bf16[128,1,2]{2,1,0:T(2,128)(2,1)}), bf16[128,1,2]{2,1,0:T(2,128)(2,1)S(1)}, u32[]{:S(2)}, u32[]{:S(2)}) async-start(bf16[128,1,2]{2,1,0:T(2,128)(2,1)} %all_to_all.34), calls=%async_computation.1 | async-start | bytes 131072 | tf_op jit(solution)/shard_map/all_to_all | solution.py:123
  52.7 163.4 %all-to-all-start.2 = ((bf16[64,2,1,2,3584]{4,3,0,2,1:T(2,128)(2,1)}), bf16[64,2,1,2,3584]{4,3,0,2,1:T(2,128)(2,1)}, u32[]{:S(2)}, u32[]{:S(2)}) async-start(bf16[64,2,1,2,3584]{4,3,0,2,1:T(2,128)(2,1)} %copy.52), calls=%async_computation.2 | async-start | bytes 3670016 | tf_op jit(solution)/shard_map/all_to_all | solution.py:40
  216.1 29.0 %all-to-all-start = ((f32[128,26,2]{1,2,0:T(2,128)}), f32[128,26,2]{1,2,0:T(2,128)S(1)}, u32[]{:S(2)}, u32[]{:S(2)}) async-start(f32[128,26,2]{1,2,0:T(2,128)} %copy.47), calls=%async_computation | async-start | bytes 262144 | tf_op jit(solution)/shard_map/all_to_all | solution.py:105
  233.1 19.3 %copy-start.3 = (bf16[224,448]{1,0:T(8,128)(2,1)S(1)}, bf16[224,448]{1,0:T(8,128)(2,1)}, u32[]{:S(2)}) copy-start(bf16[224,448]{1,0:T(8,128)(2,1)} %param.16) | copy-start | bytes 602116
  233.1 19.3 %copy-start.4 = (bf16[224,448]{1,0:T(8,128)(2,1)S(1)}, bf16[224,448]{1,0:T(8,128)(2,1)}, u32[]{:S(2)}) copy-start(bf16[224,448]{1,0:T(8,128)(2,1)} %param.17) | copy-start | bytes 602116
  233.1 19.3 %copy-start.5 = (bf16[224,448]{1,0:T(8,128)(2,1)S(1)}, bf16[224,448]{1,0:T(8,128)(2,1)}, u32[]{:S(2)}) copy-start(bf16[224,448]{1,0:T(8,128)(2,1)} %param.18) | copy-start | bytes 602116
  245.1 93.6 %all-to-all-start.3 = ((bf16[64,2,1,2,3584]{4,3,1,2,0:T(2,128)(2,1)}), bf16[64,2,1,2,3584]{4,3,1,2,0:T(2,128)(2,1)S(1)}, u32[]{:S(2)}, u32[]{:S(2)}) async-start(bf16[64,2,1,2,3584]{4,3,1,2,0:T(2,128)(2,1)} %copy.53), calls=%async_computation.3 | async-start | bytes 3670016 | tf_op jit(solution)/shard_map/all_to_all | solution.py:40
  252.3 1.2 copy-start.7
  252.4 1.3 copy-start.6
  252.4 45.1 %all-gather.4.cloned.1.call-start = ((), (), s32[]{:S(2)}) async-start(), calls=%async_computation.4 | async-start | bytes 3153920 | tf_op jit(solution)/shard_map/all_gather | solution.py:17
  342.4 0.8 copy-start.8
  342.9 2.2 copy-start.1
  345.1 2.1 copy-start.2
Sparse Core Ops, SparseCore 0:
  12.0 144.3 all-gather.5
Sparse Core Ops, SparseCore 1:
  254.9 42.4 all-gather.3
where the time goes:
time: 360 us; the launch traced here: 358 us
  waiting for transfers between devices  187 us (52%)
  other arithmetic  56.9 us (16%)
  starting transfers between devices  44.9 us (12%)
  local copies, waits for them, and re-layouts  24.2 us (7%)
  between operations  15.8 us (4%)
  matrix products  15.2 us (4%)
  blocking collectives  14.2 us (4%)
    all_gather x1, waiting for transfers between devices, per_device(): lax.all_gather(keys.astype(jnp.bfloat16), DB, axis=0, tiled=True)  99 us
    top_k x1, other arithmetic, per_device(): candidates = lax.top_k(lookup_match_rating, 2)[0]  51.7 us
    all_to_all x2, waiting for transfers between devices, turned_blocks(): lax.all_to_all(blocks, axes[k], split_axis=k, concat_axis=k, tiled=True)  34 us
    all_gather x1, waiting for transfers between devices, sent_together(): whole, at, done = (lax.all_gather(both, axis, axis=dim, tiled=True), 0, [])  29.6 us
    all_to_all x1, starting transfers between devices, per_device(): wanted = lax.all_to_all(marks, DB, split_axis=0, concat_axis=0, tiled=True)  19.9 us
    all_gather x1, blocking collectives, per_device(): lax.all_gather(w_out, 'pb', axis=0, tiled=True)  14.2 us
    all_to_all x1, starting transfers between devices, per_device(): lax.all_to_all(candidates, DB, split_axis=0, concat_axis=1, tiled=True)  13 us
    all_to_all x1, waiting for transfers between devices, per_device(): wanted = lax.all_to_all(marks, DB, split_axis=0, concat_axis=0, tiled=True)  12.2 us
  transfers between devices with their start and end apart: 6, of which 5 were waited for; matrix products, arithmetic and copies ran while one was open for 23% of the time, Pallas kernels for 0%

commit v1 on v0

v1 whole, which is shorter than its diff:
```python
import jax
import jax.numpy as jnp
from jax import lax
from jax.experimental import pallas as pl
from jax.experimental.pallas import tpu as pltpu
from jax.sharding import Mesh
from jax.sharding import PartitionSpec as P

KEY = 384
E = 896
HEADS = 7
HSIZE = 64
HD = HEADS * HSIZE
NT = 4
CT = 4
ROWS = 96
GROUPS = 26
PAIRS = 2 * GROUPS
RING = 8
PIECE = 112
SLAB_ROWS = 12
SERVERS = 64
SLOTS = 16
KEYPAD = 32
WIDE = E + 128
CUT = 64
LOW = -3.0e38
SPLIT = ("x", "zh", "zl", "core", "pb")
DB = ("x", "zh", "zl", "core")
NEAR = ("pb", "x", "zl", "core")
BF = jnp.bfloat16
F32 = jnp.float32


def best_two(hi, lo):
    count = hi.shape[0]
    while count > 1:
        half = count // 2
        h1, h2, l1, l2 = hi[:half], hi[half:count], lo[:half], lo[half:count]
        hi, lo = jnp.maximum(h1, h2), jnp.maximum(jnp.minimum(h1, h2), jnp.maximum(l1, l2))
        count = half
    return hi, lo


def serve_kernel(code, keys, *refs):
    pieces, out, held, slab = refs[: RING + 1], refs[RING + 1], refs[RING + 2], refs[RING + 3]
    at = 0
    for piece in pieces:
        rows = piece.shape[0]
        held[at : at + rows, :] = piece[...]
        at += rows
    for k in range(RING):
        for part in range(2):
            slab[(2 * k + part) * 16 : (2 * k + part + 1) * 16, :] = held[
                k * PIECE + ROWS : (k + 1) * PIECE, part * KEY : (part + 1) * KEY
            ]
    step = 256
    for i in range(SERVERS * SLOTS // step):
        label = lax.broadcasted_iota(jnp.int32, (step, RING * PIECE), 1)
        pick = (code[i * step : (i + 1) * step, :] == label).astype(F32).astype(BF)
        found = jnp.dot(pick, held[...], preferred_element_type=F32).astype(BF)
        n = step // SLOTS
        out[i * n : (i + 1) * n, :, :E] = found.reshape(n, SLOTS, E)
    queries = SERVERS * KEYPAD
    wide = 512
    n = wide // KEYPAD
    for i in range(queries // wide):
        block = keys[i * n : (i + 1) * n].reshape(wide, KEY)
        rating = lax.dot_general(
            slab[...], block, (((1,), (1,)), ((), ())), preferred_element_type=F32
        ) * (KEY**-0.5)
        row = lax.broadcasted_iota(jnp.int32, rating.shape, 0)
        rating = jnp.where(lax.rem(row, 16) < SLAB_ROWS, rating, LOW)
        h1, h2 = rating[:128], rating[128:]
        hi, lo = best_two(jnp.maximum(h1, h2), jnp.minimum(h1, h2))
        hi_a = hi.astype(BF).astype(F32)
        lo_a = lo.astype(BF).astype(F32)
        line = lax.broadcasted_iota(jnp.int32, (16, wide), 0)
        parts = jnp.where(
            line == 0,
            hi_a,
            jnp.where(line == 1, hi - hi_a, jnp.where(line == 2, lo_a, jnp.where(line == 3, lo - lo_a, 0.0))),
        ).astype(BF)
        for half in range(2):
            unit = (
                lax.broadcasted_iota(jnp.int32, (16, 128), 0) + 4 * half
                == lax.broadcasted_iota(jnp.int32, (16, 128), 1)
            ).astype(F32).astype(BF)
            turned = lax.dot_general(
                parts, unit, (((0,), (0,)), ((), ())), preferred_element_type=F32
            ).reshape(n, 2, 16, 128)
            if half == 0:
                total = turned[:, 0]
            else:
                total = total + turned[:, 1]
        out[i * n : (i + 1) * n, :, E:] = total.astype(BF)


def layer_kernel(place, got, keyed, valued, w_query, w_out, gain, best, encoded):
    label = lax.broadcasted_iota(jnp.int32, (PAIRS * NT, SERVERS * SLOTS), 1)
    pick = (place[...] == label).astype(F32).astype(BF)
    rows = got[:, :, :E].reshape(SERVERS * SLOTS, E)
    x = jnp.dot(pick, rows, preferred_element_type=F32)
    square = jnp.mean(x * x, axis=-1, keepdims=True)
    normed = (x * lax.rsqrt(square + 1e-06) * gain[...]).astype(BF)
    query = jnp.dot(normed, w_query[:, :HD], preferred_element_type=F32).astype(BF)
    query = query.astype(F32)
    k_all = keyed[...]
    v_all = valued[...].astype(F32)
    head = lax.broadcasted_iota(jnp.int32, (1, HD), 1) // HSIZE
    mine = (
        lax.broadcasted_iota(jnp.int32, (PAIRS * NT, GROUPS * CT), 0) // (2 * NT)
        == lax.broadcasted_iota(jnp.int32, (PAIRS * NT, GROUPS * CT), 1) // CT
    )
    mixed = jnp.zeros((PAIRS * NT, HD), F32)
    for h in range(HEADS):
        q_h = jnp.where(head == h, query, 0.0).astype(BF)
        v_h = jnp.where(head == h, v_all, 0.0).astype(BF)
        logits = lax.dot_general(
            q_h, k_all, (((1,), (1,)), ((), ())), preferred_element_type=F32
        ) * (HSIZE**-0.5)
        logits = jnp.where(mine, logits, LOW)
        top = jnp.max(logits, axis=-1, keepdims=True)
        e = jnp.exp(logits - top)
        probs = (e / jnp.sum(e, axis=-1, keepdims=True)).astype(BF)
        mixed = mixed + jnp.dot(probs, v_h, preferred_element_type=F32)
    result = x + jnp.dot(mixed.astype(BF), w_out[...], preferred_element_type=F32)
    encoded[...] = result.astype(BF)
    c = got[:, :, E:].astype(F32)
    c = c + pltpu.roll(c, 127, 2)
    hi, lo = best_two(c, pltpu.roll(c, 126, 2))
    hi, lo = hi[0], lo[0]
    for half in range(2):
        n = min(16, GROUPS - 16 * half)
        best[16 * half : 16 * half + n, 0:1] = hi[:n, 4 * half : 4 * half + 1]
        best[16 * half : 16 * half + n, 1:2] = lo[:n, 4 * half : 4 * half + 1]


def vmem(count):
    return [pl.BlockSpec(memory_space=pltpu.VMEM)] * count


def ring_moved(piece, step):
    return lax.ppermute(piece, "zh", [(i, (i + step) % RING) for i in range(RING)])


def per_device(keys, slab, neighbour_ids, group_acts, table, norm_gain, w_query, w_key, w_value, w_out):
    y = lax.axis_index("pb")
    zh = lax.axis_index("zh")
    token = lax.dynamic_index_in_dim(table, y, axis=1, keepdims=False)
    quarter = lax.dynamic_slice_in_dim(slab, y * 2 * SLAB_ROWS, 2 * SLAB_ROWS, 0).astype(BF)
    quarter = jnp.concatenate([quarter[:SLAB_ROWS], quarter[SLAB_ROWS:]], axis=1)
    quarter = jnp.pad(quarter, ((0, PIECE - ROWS - SLAB_ROWS), (0, E - 2 * KEY)))
    piece = jnp.concatenate([token, quarter], axis=0)
    right = [piece]
    left = [piece]
    for _ in range(3):
        right.append(ring_moved(right[-1], 1))
        left.append(ring_moved(left[-1], -1))
    far_a = ring_moved(right[3][:CUT], 1)
    far_b = ring_moved(left[3][CUT:], -1)
    pieces = [*right, far_a, far_b, left[3], left[2], left[1]]
    packed = jnp.concatenate(
        [
            jnp.concatenate([w_query, w_key], axis=1),
            jnp.concatenate([w_value[: ROWS + 16], w_value[ROWS + 16 :]], axis=1),
            w_out,
        ],
        axis=0,
    )
    whole = lax.all_gather(packed, "pb", axis=0, tiled=False)
    part = w_query.shape[0]
    w_qk = whole[:, :part].reshape(E, 2 * HD)
    w_v = whole[:, part : part + part // 2]
    w_v = jnp.concatenate([w_v[:, :, :HD], w_v[:, :, HD:]], axis=1).reshape(E, HD)
    w_o = whole[:, part + part // 2 :].reshape(HD, E)
    flat = neighbour_ids.T.reshape(PAIRS)
    owner = lax.div(flat, ROWS)
    local = flat - owner * ROWS
    at = lax.iota(jnp.int32, PAIRS)
    rank = jnp.max(
        jnp.where((owner[:, None] == owner[None, :]) & (at[:, None] > at[None, :]), 1, 0), axis=1
    )
    server = ((owner >> 5) << 2) | (owner & 3)
    code = server * SLOTS + ((owner >> 2) & 7) * 2 + rank
    marks = jnp.sum(
        jnp.where(code[None, :] == lax.iota(jnp.int32, 16 * SLOTS)[:, None], local[None, :] + 1, 0), axis=1
    )
    marks = marks.astype(BF).reshape(16, SLOTS)
    place = code.reshape(2, GROUPS).T.reshape(GROUPS, 2, 1) + lax.iota(jnp.int32, NT) * (16 * SLOTS)
    place = place.reshape(PAIRS * NT, 1)
    sent = jnp.pad(keys.astype(BF), ((0, KEYPAD - GROUPS), (0, 0)))
    marks = jnp.pad(marks[:, None, :], ((0, 0), (GROUPS, KEYPAD - GROUPS - 1), (0, KEY - SLOTS)))
    sent = sent[None] + marks
    sent = jnp.broadcast_to(sent[None], (4, 16, KEYPAD, KEY)).reshape(SERVERS, KEYPAD, KEY)
    asked = lax.all_to_all(sent, NEAR, split_axis=0, concat_axis=0, tiled=True)
    wanted = asked[:, GROUPS, :SLOTS].astype(jnp.int32)
    away = jnp.bitwise_and(zh - lax.iota(jnp.int32, SLOTS) // 2 + RING, RING - 1)
    wanted = jnp.where(wanted > 0, away[None, :] * PIECE + wanted - 1, -1).reshape(SERVERS * SLOTS, 1)
    served = pl.pallas_call(
        serve_kernel,
        out_shape=jax.ShapeDtypeStruct((SERVERS, SLOTS, WIDE), BF),
        in_specs=vmem(2 + RING + 1),
        out_specs=pl.BlockSpec(memory_space=pltpu.VMEM),
        scratch_shapes=[pltpu.VMEM((RING * PIECE, E), BF), pltpu.VMEM((RING * 32, KEY), BF)],
        compiler_params=pltpu.CompilerParams(vmem_limit_bytes=32 * 2**20),
    )(wanted, asked, *pieces)
    got = lax.all_to_all(served, NEAR, split_axis=0, concat_axis=0, tiled=True)
    acts = group_acts.reshape(GROUPS * CT, E)
    keyed = jnp.dot(acts, w_qk[:, HD:], preferred_element_type=F32).astype(BF)
    valued = jnp.dot(acts, w_v, preferred_element_type=F32).astype(BF)
    best, encoded = pl.pallas_call(
        layer_kernel,
        out_shape=(
            jax.ShapeDtypeStruct((GROUPS, 2), F32),
            jax.ShapeDtypeStruct((PAIRS * NT, E), BF),
        ),
        in_specs=vmem(7),
        out_specs=tuple(vmem(2)),
        compiler_params=pltpu.CompilerParams(vmem_limit_bytes=32 * 2**20),
    )(place, got, keyed, valued, w_qk, w_o, norm_gain.reshape(1, E))
    return best, encoded.reshape(GROUPS, 2, NT, E)


def solution(mesh):
    split = Mesh(mesh.devices.reshape(4, RING, 2, 2, 4), SPLIT)
    return jax.shard_map(
        per_device,
        mesh=split,
        in_specs=(
            P(SPLIT, None),
            P(DB, None),
            P(SPLIT, None),
            P(SPLIT, None, None),
            P(DB, None, None),
            P(),
            P("pb", None),
            P("pb", None),
            P("pb", None),
            P("pb", None),
        ),
        out_specs=(P(SPLIT, None), P(SPLIT, None, None, None)),
        check_vma=False,
    )
```

time: 360 us -> 187 us (0.52)
  waiting for transfers between devices: 187 us -> 81.8 us
  other arithmetic: 56.9 us -> 5.51 us
  matrix products: 15.2 us -> 0.77 us
  blocking collectives: 14.2 us -> 0 us
  starting transfers between devices: 44.9 us -> 56.4 us
  Pallas kernels: 0 us -> 8.27 us
  local copies, waits for them, and re-layouts: 24.2 us -> 17.2 us
    all_gather x2 -> x1, waiting for transfers between devices: 129 us -> 50.1 us  [per_device(): whole = lax.all_gather(packed, 'pb', axis=0, tiled=False)]
    all_to_all x4 -> x2, waiting for transfers between devices: 58.2 us -> 0.01 us  [the longest x1 0.01 us: per_device(): asked = lax.all_to_all(sent, NEAR, split_axis=0, concat_axis=0, tiled=True)]
    top_k x2 -> x0, other arithmetic: 53.5 us -> none  [the longest x1 51.7 us: per_device(): candidates = lax.top_k(lookup_match_rating, 2)[0]]
    ppermute x0 -> x8, starting transfers between devices: none -> 38.2 us  [ring_moved(): lax.ppermute(piece, 'zh', [(i, (i + step) % RING) for i in range(RING)])]
    ppermute x0 -> x8, waiting for transfers between devices: none -> 31.7 us  [ring_moved(): lax.ppermute(piece, 'zh', [(i, (i + step) % RING) for i in range(RING)])]
    all_to_all x4 -> x2, starting transfers between devices: 44.8 us -> 18.1 us  [the longest x1 10 us: per_device(): asked = lax.all_to_all(sent, NEAR, split_axis=0, concat_axis=0, tiled=True)]
    all_gather x1 -> x0, blocking collectives: 14.2 us -> none  [per_device(): lax.all_gather(w_out, 'pb', axis=0, tiled=True)]
    dot_general x9 -> x2, matrix products: 13.1 us -> 0.77 us  [the longest x1 0.48 us: per_device(): keyed = jnp.dot(acts, w_qk[:, HD:], preferred_element_type=F32).astype(BF)]
  transfers between devices with their start and end apart: 6 -> 11, of which waited for: 5 -> 5; matrix products, arithmetic and copies ran while one was open for 23% -> 8% of each run, Pallas kernels for 0% -> 0%
where the time goes in v1:
time: 187 us; the launch traced here: 184 us
  waiting for transfers between devices  81.8 us (44%)
  starting transfers between devices  56.4 us (30%)
  local copies, waits for them, and re-layouts  17.2 us (9%)
  between operations  14.4 us (8%)
  Pallas kernels  8.27 us (4%)
  other arithmetic  5.51 us (3%)
    all_gather x1, waiting for transfers between devices, per_device(): whole = lax.all_gather(packed, 'pb', axis=0, tiled=False)  50.1 us
    ppermute x8, starting transfers between devices, ring_moved(): lax.ppermute(piece, 'zh', [(i, (i + step) % RING) for i in range(RING)])  38.2 us
    ppermute x8, waiting for transfers between devices, ring_moved(): lax.ppermute(piece, 'zh', [(i, (i + step) % RING) for i in range(RING)])  31.7 us
    all_to_all x1, starting transfers between devices, per_device(): asked = lax.all_to_all(sent, NEAR, split_axis=0, concat_axis=0, tiled=True)  10 us
    all_to_all x1, starting transfers between devices, per_device(): got = lax.all_to_all(served, NEAR, split_axis=0, concat_axis=0, tiled=True)  8.07 us
    unnamed x26, local copies, waits for them, and re-layouts  5.32 us
    pallas_call x1, Pallas kernels, per_device(): pl.pallas_call(serve_kernel, out_shape=jax.ShapeDtypeStruct((SERVERS, SLO...  5.14 us
  transfers between devices with their start and end apart: 11, of which 5 were waited for; matrix products, arithmetic and copies ran while one was open for 8% of the time, Pallas kernels for 0%

profile of v1, /device:TPU:6, one launch (start us, length us, event | category | flops | bytes accessed | tf_op | source)
XLA Modules:
  0.0 184.3 jit_solution(690815039154825994)
XLA Ops:
  7.2 0.0 copy-start
  7.2 0.8 reshape.159
  8.0 0.2 select_reduce_fusion.1
  8.2 0.1 select_reduce_fusion
  8.3 0.1 convert_element_type.50
  8.4 0.8 convert_element_type.48
  9.3 0.1 copy.25
  9.4 1.3 broadcast_in_dim.42
  10.7 10.0 %all-to-all-start = ((bf16[64,32,384]{2,1,0:T(8,128)(2,1)}), bf16[64,32,384]{2,1,0:T(8,128)(2,1)S(1)}, u32[]{:S(2)}, u32[]{:S(2)}) async-start(bf16[64,32,384]{2,1,0:T(8,128)(2,1)} %bitcast.22), calls=%async_computation | async-start | bytes 3145728 | tf_op jit(solution)/shard_map/all_to_all | solution.py:196
  20.8 0.4 constant_dynamic-slice_fusion
  21.2 0.8 dynamic-slice_convert_fusion
  22.0 4.5 %collective-permute-start = (bf16[112,896]{1,0:T(8,128)(2,1)S(1)}, bf16[112,896]{1,0:T(8,128)(2,1)S(1)}, u32[]{:S(2)}, u32[]{:S(2)}) collective-permute-start(bf16[112,896]{1,0:T(8,128)(2,1)S(1)} %pad_maximum_fusion.2.refs_0_), channel_id=1, source_target_pairs={{0,16},{16,32},{32,48},{48,64},{64,80},{80,96},{96,112},{112,0},{1... | collective-permute-start | bytes 602120 | tf_op jit(solution)/shard_map/ppermute | solution.py:144
  26.5 7.7 %collective-permute-start.4 = (bf16[112,896]{1,0:T(8,128)(2,1)S(1)}, bf16[112,896]{1,0:T(8,128)(2,1)S(1)}, u32[]{:S(2)}, u32[]{:S(2)}) collective-permute-start(bf16[112,896]{1,0:T(8,128)(2,1)S(1)} %pad_maximum_fusion.2.refs_0_), channel_id=1, source_target_pairs={{0,112},{16,0},{32,16},{48,32},{64,48},{80,64},{96,80},{112,96},{1... | collective-permute-start | bytes 602120 | tf_op jit(solution)/shard_map/ppermute | solution.py:144
  34.2 25.5 %collective-permute-done.refs_1_ = bf16[112,896]{1,0:T(8,128)(2,1)S(1)} collective-permute-done((bf16[112,896]{1,0:T(8,128)(2,1)S(1)}, bf16[112,896]{1,0:T(8,128)(2,1)S(1)}, u32[]{:S(2)}, u32[]{:S(2)}) %collective-permute-start) | collective-permute-done | bytes 200736 | tf_op jit(solution)/shard_map/ppermute | solution.py:144
  59.7 1.9 %collective-permute-start.1 = (bf16[112,896]{1,0:T(8,128)(2,1)S(1)}, bf16[112,896]{1,0:T(8,128)(2,1)S(1)}, u32[]{:S(2)}, u32[]{:S(2)}) collective-permute-start(bf16[112,896]{1,0:T(8,128)(2,1)S(1)} %collective-permute-done.refs_1_), channel_id=1, source_target_pairs={{0,16},{16,32},{32,48},{48,64},{64,80},{80,96},{96,112},{112,0},{1... | collective-permute-start | bytes 602120 | tf_op jit(solution)/shard_map/ppermute | solution.py:144
  61.6 0.0 collective-permute-done.4.refs_8_
  61.6 6.0 %collective-permute-start.5 = (bf16[112,896]{1,0:T(8,128)(2,1)S(1)}, bf16[112,896]{1,0:T(8,128)(2,1)}, u32[]{:S(2)}, u32[]{:S(2)}) collective-permute-start(bf16[112,896]{1,0:T(8,128)(2,1)S(1)} %collective-permute-done.4.refs_8_), channel_id=1, source_target_pairs={{0,112},{16,0},{32,16},{48,32},{64,48},{80,64},{96,80},{112,96},{1... | collective-permute-start | bytes 602120 | tf_op jit(solution)/shard_map/ppermute | solution.py:144
  67.6 5.6 %collective-permute-done.1.refs_2_ = bf16[112,896]{1,0:T(8,128)(2,1)S(1)} collective-permute-done((bf16[112,896]{1,0:T(8,128)(2,1)S(1)}, bf16[112,896]{1,0:T(8,128)(2,1)S(1)}, u32[]{:S(2)}, u32[]{:S(2)}) %collective-permute-start.1) | collective-permute-done | bytes 200736 | tf_op jit(solution)/shard_map/ppermute | solution.py:144
  73.3 2.2 %collective-permute-start.2 = (bf16[112,896]{1,0:T(8,128)(2,1)S(1)}, bf16[112,896]{1,0:T(8,128)(2,1)S(1)}, u32[]{:S(2)}, u32[]{:S(2)}) collective-permute-start(bf16[112,896]{1,0:T(8,128)(2,1)S(1)} %collective-permute-done.1.refs_2_), channel_id=1, source_target_pairs={{0,16},{16,32},{32,48},{48,64},{64,80},{80,96},{96,112},{112,0},{1... | collective-permute-start | bytes 602120 | tf_op jit(solution)/shard_map/ppermute | solution.py:144
  75.5 0.2 collective-permute-done.5.refs_7_
  75.7 6.6 %collective-permute-start.6 = (bf16[112,896]{1,0:T(8,128)(2,1)}, bf16[112,896]{1,0:T(8,128)(2,1)S(1)}, u32[]{:S(2)}, u32[]{:S(2)}) collective-permute-start(bf16[112,896]{1,0:T(8,128)(2,1)} %collective-permute-done.5.refs_7_), channel_id=1, source_target_pairs={{0,112},{16,0},{32,16},{48,32},{64,48},{80,64},{96,80},{112,96},{1... | collective-permute-start | bytes 602120 | tf_op jit(solution)/shard_map/ppermute | solution.py:144
  82.3 1.1 add.131
  83.4 0.4 collective-permute-done.2.refs_3_
  83.8 0.7 slice.54
  84.5 3.1 %collective-permute-start.3 = (bf16[64,896]{1,0:T(8,128)(2,1)}, bf16[64,896]{1,0:T(8,128)(2,1)}, u32[]{:S(2)}, u32[]{:S(2)}) collective-permute-start(bf16[64,896]{1,0:T(8,128)(2,1)} %slice.54), channel_id=1, source_target_pairs={{0,16},{16,32},{32,48},{48,64},{64,80},{80,96},{96,112},{112,0},{1... | collective-permute-start | bytes 344072 | tf_op jit(solution)/shard_map/ppermute | solution.py:144
  87.5 0.0 collective-permute-done.6.refs_6_
  87.5 0.6 slice.55
  88.2 6.3 %collective-permute-start.7 = (bf16[48,896]{1,0:T(8,128)(2,1)}, bf16[48,896]{1,0:T(8,128)(2,1)S(1)}, u32[]{:S(2)}, u32[]{:S(2)}) collective-permute-start(bf16[48,896]{1,0:T(8,128)(2,1)} %slice.55), channel_id=1, source_target_pairs={{0,112},{16,0},{32,16},{48,32},{64,48},{80,64},{96,80},{112,96},{1... | collective-permute-start | bytes 258056 | tf_op jit(solution)/shard_map/ppermute | solution.py:144
  94.5 0.0 all-to-all-done.keys
  94.5 0.7 fusion.8
  95.2 1.9 %reshape.169 = s32[1024,1]{1,0:T(8,128)} reshape(s32[64,16]{1,0:T(8,128)} %fusion.8) | data formatting | bytes 8192 | tf_op jit(solution)/shard_map/convert_element_type | solution.py:197
  97.1 1.3 add_select_fusion.code
  98.3 0.0 collective-permute-done.7.refs_5_
  98.3 0.0 collective-permute-done.3.refs_4_
  98.3 5.1 %shard_map.113 = bf16[64,16,1024]{2,1,0:T(8,128)(2,1)S(1)} custom-call(s32[1024,1]{1,0:T(8,128)S(1)} %add_select_fusion.code, bf16[64,32,384]{2,1,0:T(8,128)(2,1)S(1)} %all-to-all-done.keys, bf16[112,896]{1,0:T(8,128)(2,1)S(1)} %pad_maximum_fusion.2.refs_0_, bf16[112,896]{1,0:T(8,128)(2,1)S(1)} %collective-permute-done.refs_1_, ...), custom_call_target="tpu_custom_call" | custom-call | tf_op jit(solution)/shard_map/pallas_call | solution.py:200
  103.5 1.4 copy-done.1
  104.9 8.1 %all-to-all-start.1 = ((bf16[64,16,1024]{2,1,0:T(8,128)(2,1)}), bf16[64,16,1024]{2,1,0:T(8,128)(2,1)S(1)}, u32[]{:S(2)}, u32[]{:S(2)}) async-start(bf16[64,16,1024]{2,1,0:T(8,128)(2,1)} %copy-done.1), calls=%async_computation.1 | async-start | bytes 4194304 | tf_op jit(solution)/shard_map/all_to_all | solution.py:208
  113.0 0.0 copy-start.11
  113.0 0.0 all-gather.3.cloned.1.call-start
  113.1 0.0 copy-start.9
  113.1 0.0 copy-start.10
  113.1 2.1 %pad_maximum_fusion.1 = bf16[448,896]{1,0:T(8,128)(2,1)} fusion(bf16[112,896]{1,0:T(8,128)(2,1)} %param.19, bf16[112,448]{1,0:T(8,128)(2,1)S(1)} %get-tuple-element.17, bf16[112,448]{1,0:T(8,128)(2,1)S(1)} %get-tuple-element.16, bf16[224,448]{1,0:T(8,128)(2,1)S(1)} %copy-done.6, bf16[224,448]{1,0:T(8,128)(2,1)S(1)} %copy-done.7), kind=kLoop, calls=%fused_computation.6 | loop fusion | flops 4014080 | bytes 1605632 | tf_op jit(solution)/shard_map/concatenate | solution.py:163
  115.2 0.0 all-gather.3.cloned.1.call-update
  115.2 0.1 reduce_max.12
  115.3 0.0 copy-done.11
  115.4 0.1 copy.24
  115.5 0.1 broadcast_add_fusion
  115.6 0.1 add.130.place
  115.7 0.0 copy-done.10
  115.7 50.1 %all-gather.3.cloned.1.call-done = bf16[1792,896]{1,0:T(8,128)(2,1)} async-done(((bf16[448,896]{1,0:T(8,128)(2,1)}), bf16[1792,896]{1,0:T(8,128)(2,1)}) %all-gather.3.cloned.1.call-update) | async-done | bytes 3211280 | tf_op jit(solution)/shard_map/all_gather | solution.py:171
  165.8 1.7 slice.56
  167.5 0.7 copy-done.5
  168.2 1.0 slice.60
  169.2 0.2 fusion.15
  169.4 0.1 pad_maximum_fusion
  169.5 0.3 fusion.1.valued
  169.8 0.0 copy-done.2
  169.8 0.5 fusion.keyed
  170.3 0.0 all-to-all-done.1.got
  170.3 1.4 copy-done.3
  171.8 1.1 copy-done.4
  172.9 3.1 %shard_map.114 = (f32[26,2]{1,0:T(8,128)S(1)}, bf16[208,896]{1,0:T(8,128)(2,1)S(1)}) custom-call(s32[208,1]{1,0:T(8,128)S(1)} %add.130.place, bf16[64,16,1024]{2,1,0:T(8,128)(2,1)S(1)} %all-to-all-done.1.got, bf16[104,448]{1,0:T(8,128)(2,1)S(1)} %fusion.keyed, bf16[104,448]{1,0:T(8,128)(2,1)S(1)} %fusion.1.valued, bf16[896,896]{1,0:T(8,128)(2,1)S(1)} %bitcast.20, ...), custom_call_target="tpu_custom_call" | custom-call | tf_op jit(solution)/shard_map/pallas_call | solution.py:212
  176.0 0.8 reshape.166
  176.9 0.6 copy.31
  (29 shorter events, 0.3 us)
Async XLA Ops:
  7.2 13.6 %copy-start = (bf16[96,4,896]{2,1,0:T(4,128)(2,1)S(1)}, bf16[96,4,896]{2,1,0:T(4,128)(2,1)}, u32[]{:S(2)}) copy-start(bf16[96,4,896]{2,1,0:T(4,128)(2,1)} %param.14) | copy-start | bytes 2064388
  10.7 83.8 %all-to-all-start = ((bf16[64,32,384]{2,1,0:T(8,128)(2,1)}), bf16[64,32,384]{2,1,0:T(8,128)(2,1)S(1)}, u32[]{:S(2)}, u32[]{:S(2)}) async-start(bf16[64,32,384]{2,1,0:T(8,128)(2,1)} %bitcast.22), calls=%async_computation | async-start | bytes 3145728 | tf_op jit(solution)/shard_map/all_to_all | solution.py:196
  22.0 37.7 %collective-permute-start = (bf16[112,896]{1,0:T(8,128)(2,1)S(1)}, bf16[112,896]{1,0:T(8,128)(2,1)S(1)}, u32[]{:S(2)}, u32[]{:S(2)}) collective-permute-start(bf16[112,896]{1,0:T(8,128)(2,1)S(1)} %pad_maximum_fusion.2.refs_0_), channel_id=1, source_target_pairs={{0,16},{16,32},{32,48},{48,64},{64,80},{80,96},{96,112},{112,0},{1... | collective-permute-start | bytes 602120 | tf_op jit(solution)/shard_map/ppermute | solution.py:144
  26.5 35.1 %collective-permute-start.4 = (bf16[112,896]{1,0:T(8,128)(2,1)S(1)}, bf16[112,896]{1,0:T(8,128)(2,1)S(1)}, u32[]{:S(2)}, u32[]{:S(2)}) collective-permute-start(bf16[112,896]{1,0:T(8,128)(2,1)S(1)} %pad_maximum_fusion.2.refs_0_), channel_id=1, source_target_pairs={{0,112},{16,0},{32,16},{48,32},{64,48},{80,64},{96,80},{112,96},{1... | collective-permute-start | bytes 602120 | tf_op jit(solution)/shard_map/ppermute | solution.py:144
  59.7 13.6 %collective-permute-start.1 = (bf16[112,896]{1,0:T(8,128)(2,1)S(1)}, bf16[112,896]{1,0:T(8,128)(2,1)S(1)}, u32[]{:S(2)}, u32[]{:S(2)}) collective-permute-start(bf16[112,896]{1,0:T(8,128)(2,1)S(1)} %collective-permute-done.refs_1_), channel_id=1, source_target_pairs={{0,16},{16,32},{32,48},{48,64},{64,80},{80,96},{96,112},{112,0},{1... | collective-permute-start | bytes 602120 | tf_op jit(solution)/shard_map/ppermute | solution.py:144
  61.6 14.1 %collective-permute-start.5 = (bf16[112,896]{1,0:T(8,128)(2,1)S(1)}, bf16[112,896]{1,0:T(8,128)(2,1)}, u32[]{:S(2)}, u32[]{:S(2)}) collective-permute-start(bf16[112,896]{1,0:T(8,128)(2,1)S(1)} %collective-permute-done.4.refs_8_), channel_id=1, source_target_pairs={{0,112},{16,0},{32,16},{48,32},{64,48},{80,64},{96,80},{112,96},{1... | collective-permute-start | bytes 602120 | tf_op jit(solution)/shard_map/ppermute | solution.py:144
  73.3 10.5 %collective-permute-start.2 = (bf16[112,896]{1,0:T(8,128)(2,1)S(1)}, bf16[112,896]{1,0:T(8,128)(2,1)S(1)}, u32[]{:S(2)}, u32[]{:S(2)}) collective-permute-start(bf16[112,896]{1,0:T(8,128)(2,1)S(1)} %collective-permute-done.1.refs_2_), channel_id=1, source_target_pairs={{0,16},{16,32},{32,48},{48,64},{64,80},{80,96},{96,112},{112,0},{1... | collective-permute-start | bytes 602120 | tf_op jit(solution)/shard_map/ppermute | solution.py:144
  75.7 11.8 %collective-permute-start.6 = (bf16[112,896]{1,0:T(8,128)(2,1)}, bf16[112,896]{1,0:T(8,128)(2,1)S(1)}, u32[]{:S(2)}, u32[]{:S(2)}) collective-permute-start(bf16[112,896]{1,0:T(8,128)(2,1)} %collective-permute-done.5.refs_7_), channel_id=1, source_target_pairs={{0,112},{16,0},{32,16},{48,32},{64,48},{80,64},{96,80},{112,96},{1... | collective-permute-start | bytes 602120 | tf_op jit(solution)/shard_map/ppermute | solution.py:144
  84.5 13.9 %collective-permute-start.3 = (bf16[64,896]{1,0:T(8,128)(2,1)}, bf16[64,896]{1,0:T(8,128)(2,1)}, u32[]{:S(2)}, u32[]{:S(2)}) collective-permute-start(bf16[64,896]{1,0:T(8,128)(2,1)} %slice.54), channel_id=1, source_target_pairs={{0,16},{16,32},{32,48},{48,64},{64,80},{80,96},{96,112},{112,0},{1... | collective-permute-start | bytes 344072 | tf_op jit(solution)/shard_map/ppermute | solution.py:144
  88.2 10.1 %collective-permute-start.7 = (bf16[48,896]{1,0:T(8,128)(2,1)}, bf16[48,896]{1,0:T(8,128)(2,1)S(1)}, u32[]{:S(2)}, u32[]{:S(2)}) collective-permute-start(bf16[48,896]{1,0:T(8,128)(2,1)} %slice.55), channel_id=1, source_target_pairs={{0,112},{16,0},{32,16},{48,32},{64,48},{80,64},{96,80},{112,96},{1... | collective-permute-start | bytes 258056 | tf_op jit(solution)/shard_map/ppermute | solution.py:144
  103.5 1.4 copy-start.1
  104.9 8.2 %copy-start.8 = (bf16[224,448]{1,0:T(8,128)(2,1)S(1)}, bf16[224,448]{1,0:T(8,128)(2,1)}, u32[]{:S(2)}) copy-start(bf16[224,448]{1,0:T(8,128)(2,1)} %param.18) | copy-start | bytes 602116
  104.9 8.2 %copy-start.6 = (bf16[224,448]{1,0:T(8,128)(2,1)S(1)}, bf16[224,448]{1,0:T(8,128)(2,1)}, u32[]{:S(2)}) copy-start(bf16[224,448]{1,0:T(8,128)(2,1)} %param.17) | copy-start | bytes 602116
  104.9 8.2 %copy-start.7 = (bf16[224,448]{1,0:T(8,128)(2,1)S(1)}, bf16[224,448]{1,0:T(8,128)(2,1)}, u32[]{:S(2)}) copy-start(bf16[224,448]{1,0:T(8,128)(2,1)} %param.16) | copy-start | bytes 602116
  104.9 65.4 %all-to-all-start.1 = ((bf16[64,16,1024]{2,1,0:T(8,128)(2,1)}), bf16[64,16,1024]{2,1,0:T(8,128)(2,1)S(1)}, u32[]{:S(2)}, u32[]{:S(2)}) async-start(bf16[64,16,1024]{2,1,0:T(8,128)(2,1)} %copy-done.1), calls=%async_computation.1 | async-start | bytes 4194304 | tf_op jit(solution)/shard_map/all_to_all | solution.py:208
  113.0 2.4 %copy-start.11 = (s32[26,2]{0,1:T(2,128)S(1)}, s32[26,2]{0,1:T(2,128)}, u32[]{:S(2)}) copy-start(s32[26,2]{0,1:T(2,128)} %param.12) | copy-start | bytes 628
  113.0 52.8 %all-gather.3.cloned.1.call-start = ((), (), s32[]{:S(2)}) async-start(), calls=%async_computation.2 | async-start | bytes 4014080 | tf_op jit(solution)/shard_map/all_gather | solution.py:171
  113.1 2.2 %copy-start.9 = (bf16[26,4,896]{2,1,0:T(4,128)(2,1)S(1)}, bf16[26,4,896]{2,1,0:T(4,128)(2,1)}, u32[]{:S(2)}) copy-start(bf16[26,4,896]{2,1,0:T(4,128)(2,1)} %param.13) | copy-start | bytes 559108
  113.1 2.6 %copy-start.10 = (f32[896]{0:T(1024)S(1)}, f32[896]{0:T(1024)}, u32[]{:S(2)}) copy-start(f32[896]{0:T(1024)} %param.15) | copy-start | bytes 10756
  165.8 2.4 %copy-start.5 = (bf16[1792,896]{1,0:T(8,128)(2,1)S(1)}, bf16[1792,896]{1,0:T(8,128)(2,1)}, u32[]{:S(2)}) copy-start(bf16[1792,896]{1,0:T(8,128)(2,1)} %all-gather.3.cloned.1.call-done) | copy-start | bytes 9633796
  168.2 1.7 copy-start.2
  170.3 1.4 copy-start.3
  171.8 1.1 copy-start.4
Sparse Core Ops, SparseCore 0:
  115.9 49.8 all-gather.2

commit v2 on v1

--- a/solution.py
+++ b/solution.py
@@ -17,17 +17,19 @@
 GROUPS = 26
 PAIRS = 2 * GROUPS
 RING = 8
-PIECE = 112
-SLAB_ROWS = 12
-SERVERS = 64
+SLAB_ROWS = 24
+PIECE = ROWS + SLAB_ROWS
+PLANE = 32
+SERVERS = 2 * PLANE
 SLOTS = 16
 KEYPAD = 32
 WIDE = E + 128
 CUT = 64
-LOW = -3.0e38
+LOW = -1.0e38
 SPLIT = ("x", "zh", "zl", "core", "pb")
 DB = ("x", "zh", "zl", "core")
-NEAR = ("pb", "x", "zl", "core")
+FLAT = ("pb", "x", "core")
+NEAR = ("zl", *FLAT)
 BF = jnp.bfloat16
 F32 = jnp.float32
 
@@ -42,37 +44,40 @@
     return hi, lo
 
 
-def serve_kernel(code, keys, *refs):
-    pieces, out, held, slab = refs[: RING + 1], refs[RING + 1], refs[RING + 2], refs[RING + 3]
-    at = 0
-    for piece in pieces:
-        rows = piece.shape[0]
-        held[at : at + rows, :] = piece[...]
-        at += rows
+def serve_kernel(parity, code, keys, *refs):
+    *pieces, far_a, far_b, out, held, slab = refs
     for k in range(RING):
+        if k == RING // 2:
+            held[k * ROWS : k * ROWS + CUT, :] = far_a[...]
+            held[k * ROWS + CUT : (k + 1) * ROWS, :] = far_b[: ROWS - CUT, :]
+            extra = far_b[ROWS - CUT :, :]
+        else:
+            piece = pieces[k if k < RING // 2 else k - 1]
+            held[k * ROWS : (k + 1) * ROWS, :] = piece[:ROWS, :]
+            extra = piece[ROWS:, :]
         for part in range(2):
-            slab[(2 * k + part) * 16 : (2 * k + part + 1) * 16, :] = held[
-                k * PIECE + ROWS : (k + 1) * PIECE, part * KEY : (part + 1) * KEY
-            ]
+            at = (2 * k + part) * SLAB_ROWS
+            slab[at : at + SLAB_ROWS, :] = extra[:, part * KEY : (part + 1) * KEY].astype(F32)
     step = 256
     for i in range(SERVERS * SLOTS // step):
-        label = lax.broadcasted_iota(jnp.int32, (step, RING * PIECE), 1)
+        label = lax.broadcasted_iota(jnp.int32, (step, RING * ROWS), 1)
         pick = (code[i * step : (i + 1) * step, :] == label).astype(F32).astype(BF)
         found = jnp.dot(pick, held[...], preferred_element_type=F32).astype(BF)
         n = step // SLOTS
         out[i * n : (i + 1) * n, :, :E] = found.reshape(n, SLOTS, E)
-    queries = SERVERS * KEYPAD
     wide = 512
     n = wide // KEYPAD
-    for i in range(queries // wide):
+    rows = slab[...].astype(BF)
+    mine = parity[...]
+    for i in range(PLANE * KEYPAD // wide):
         block = keys[i * n : (i + 1) * n].reshape(wide, KEY)
         rating = lax.dot_general(
-            slab[...], block, (((1,), (1,)), ((), ())), preferred_element_type=F32
+            rows, block, (((1,), (1,)), ((), ())), preferred_element_type=F32
         ) * (KEY**-0.5)
-        row = lax.broadcasted_iota(jnp.int32, rating.shape, 0)
-        rating = jnp.where(lax.rem(row, 16) < SLAB_ROWS, rating, LOW)
-        h1, h2 = rating[:128], rating[128:]
-        hi, lo = best_two(jnp.maximum(h1, h2), jnp.minimum(h1, h2))
+        h1, h2, h3 = rating[:128], rating[128:256], rating[256:]
+        hi, lo = jnp.maximum(h1, h2), jnp.minimum(h1, h2)
+        hi, lo = jnp.maximum(hi, h3), jnp.maximum(lo, jnp.minimum(hi, h3))
+        hi, lo = best_two(hi, lo)
         hi_a = hi.astype(BF).astype(F32)
         lo_a = lo.astype(BF).astype(F32)
         line = lax.broadcasted_iota(jnp.int32, (16, wide), 0)
@@ -93,7 +98,11 @@
                 total = turned[:, 0]
             else:
                 total = total + turned[:, 1]
-        out[i * n : (i + 1) * n, :, E:] = total.astype(BF)
+        lane = lax.broadcasted_iota(jnp.int32, (1, 1, 128), 2)
+        none = jnp.where(lax.rem(lane, 2) == 0, LOW, 0.0)
+        for z in range(2):
+            at = z * PLANE + i * n
+            out[at : at + n, :, E:] = jnp.where(mine == z, total, none).astype(BF)
 
 
 def layer_kernel(place, got, keyed, valued, w_query, w_out, gain, best, encoded):
@@ -147,11 +156,49 @@
 def per_device(keys, slab, neighbour_ids, group_acts, table, norm_gain, w_query, w_key, w_value, w_out):
     y = lax.axis_index("pb")
     zh = lax.axis_index("zh")
+    zl = lax.axis_index("zl")
+    packed = jnp.concatenate(
+        [
+            jnp.concatenate([w_query, w_key], axis=1),
+            jnp.concatenate([w_value[: ROWS + 16], w_value[ROWS + 16 :]], axis=1),
+            w_out,
+        ],
+        axis=0,
+    )
+    whole = lax.all_gather(packed, "pb", axis=0, tiled=False)
+    part = w_query.shape[0]
+    w_qk = whole[:, :part].reshape(E, 2 * HD)
+    w_v = whole[:, part : part + part // 2]
+    w_v = jnp.concatenate([w_v[:, :, :HD], w_v[:, :, HD:]], axis=1).reshape(E, HD)
+    w_o = whole[:, part + part // 2 :].reshape(HD, E)
+    acts = group_acts.reshape(GROUPS * CT, E)
+    keyed = jnp.dot(acts, w_qk[:, HD:], preferred_element_type=F32).astype(BF)
+    valued = jnp.dot(acts, w_v, preferred_element_type=F32).astype(BF)
+    flat = neighbour_ids.T.reshape(PAIRS)
+    owner = lax.div(flat, ROWS)
+    local = flat - owner * ROWS
+    at = lax.iota(jnp.int32, PAIRS)
+    rank = jnp.max(
+        jnp.where((owner[:, None] == owner[None, :]) & (at[:, None] > at[None, :]), 1, 0), axis=1
+    )
+    column = ((owner >> 5) << 1) | (owner & 1)
+    code = ((owner >> 1) & 1) * 128 + column * SLOTS + ((owner >> 2) & 7) * 2 + rank
+    place = (code >> 7) * (PLANE * SLOTS) + (code & 127)
+    place = place.reshape(2, GROUPS).T.reshape(GROUPS, 2, 1) + lax.iota(jnp.int32, NT) * 128
+    place = place.reshape(PAIRS * NT, 1)
+    flip = code ^ (zl * 128)
+    marks = jnp.sum(
+        jnp.where(flip[None, :] == lax.iota(jnp.int32, 256)[:, None], local[None, :] + 1, 0), axis=1
+    )
+    marks = marks.astype(BF)
+    quarter = lax.dynamic_slice_in_dim(slab, y * SLAB_ROWS, SLAB_ROWS, 0).astype(BF)
+    other = jnp.pad(marks[None, 128:], ((0, KEYPAD - SLAB_ROWS - 1), (0, KEY - 128)))
+    pair = jnp.concatenate([quarter, other], axis=0)
+    pair = lax.ppermute(pair, "zl", [(0, 1), (1, 0)])
     token = lax.dynamic_index_in_dim(table, y, axis=1, keepdims=False)
-    quarter = lax.dynamic_slice_in_dim(slab, y * 2 * SLAB_ROWS, 2 * SLAB_ROWS, 0).astype(BF)
-    quarter = jnp.concatenate([quarter[:SLAB_ROWS], quarter[SLAB_ROWS:]], axis=1)
-    quarter = jnp.pad(quarter, ((0, PIECE - ROWS - SLAB_ROWS), (0, E - 2 * KEY)))
-    piece = jnp.concatenate([token, quarter], axis=0)
+    both = jnp.concatenate([quarter, pair[:SLAB_ROWS]], axis=1)
+    both = jnp.pad(both, ((0, 0), (0, E - 2 * KEY)))
+    piece = jnp.concatenate([token, both], axis=0)
     right = [piece]
     left = [piece]
     for _ in range(3):
@@ -159,56 +206,28 @@
         left.append(ring_moved(left[-1], -1))
     far_a = ring_moved(right[3][:CUT], 1)
     far_b = ring_moved(left[3][CUT:], -1)
-    pieces = [*right, far_a, far_b, left[3], left[2], left[1]]
-    packed = jnp.concatenate(
-        [
-            jnp.concatenate([w_query, w_key], axis=1),
-            jnp.concatenate([w_value[: ROWS + 16], w_value[ROWS + 16 :]], axis=1),
-            w_out,
-        ],
-        axis=0,
-    )
-    whole = lax.all_gather(packed, "pb", axis=0, tiled=False)
-    part = w_query.shape[0]
-    w_qk = whole[:, :part].reshape(E, 2 * HD)
-    w_v = whole[:, part : part + part // 2]
-    w_v = jnp.concatenate([w_v[:, :, :HD], w_v[:, :, HD:]], axis=1).reshape(E, HD)
-    w_o = whole[:, part + part // 2 :].reshape(HD, E)
-    flat = neighbour_ids.T.reshape(PAIRS)
-    owner = lax.div(flat, ROWS)
-    local = flat - owner * ROWS
-    at = lax.iota(jnp.int32, PAIRS)
-    rank = jnp.max(
-        jnp.where((owner[:, None] == owner[None, :]) & (at[:, None] > at[None, :]), 1, 0), axis=1
-    )
-    server = ((owner >> 5) << 2) | (owner & 3)
-    code = server * SLOTS + ((owner >> 2) & 7) * 2 + rank
-    marks = jnp.sum(
-        jnp.where(code[None, :] == lax.iota(jnp.int32, 16 * SLOTS)[:, None], local[None, :] + 1, 0), axis=1
-    )
-    marks = marks.astype(BF).reshape(16, SLOTS)
-    place = code.reshape(2, GROUPS).T.reshape(GROUPS, 2, 1) + lax.iota(jnp.int32, NT) * (16 * SLOTS)
-    place = place.reshape(PAIRS * NT, 1)
+    pieces = [*right, left[3], left[2], left[1], far_a, far_b]
     sent = jnp.pad(keys.astype(BF), ((0, KEYPAD - GROUPS), (0, 0)))
-    marks = jnp.pad(marks[:, None, :], ((0, 0), (GROUPS, KEYPAD - GROUPS - 1), (0, KEY - SLOTS)))
-    sent = sent[None] + marks
-    sent = jnp.broadcast_to(sent[None], (4, 16, KEYPAD, KEY)).reshape(SERVERS, KEYPAD, KEY)
-    asked = lax.all_to_all(sent, NEAR, split_axis=0, concat_axis=0, tiled=True)
-    wanted = asked[:, GROUPS, :SLOTS].astype(jnp.int32)
+    asks = jnp.stack([marks[:128].reshape(8, SLOTS), pair[SLAB_ROWS, :128].reshape(8, SLOTS)], axis=1)
+    asks = jnp.pad(asks, ((0, 0), (GROUPS, KEYPAD - GROUPS - 2), (0, KEY - SLOTS)))
+    sent = sent[None] + asks
+    sent = jnp.broadcast_to(sent[None], (4, 8, KEYPAD, KEY)).reshape(PLANE, KEYPAD, KEY)
+    asked = lax.all_to_all(sent, FLAT, split_axis=0, concat_axis=0, tiled=True)
+    wanted = asked[:, GROUPS : GROUPS + 2, :SLOTS].astype(jnp.int32)
+    wanted = jnp.where(zl == 0, jnp.stack([wanted[:, 0], wanted[:, 1]]), jnp.stack([wanted[:, 1], wanted[:, 0]]))
     away = jnp.bitwise_and(zh - lax.iota(jnp.int32, SLOTS) // 2 + RING, RING - 1)
-    wanted = jnp.where(wanted > 0, away[None, :] * PIECE + wanted - 1, -1).reshape(SERVERS * SLOTS, 1)
+    wanted = jnp.where(wanted > 0, away * ROWS + wanted - 1, -1).reshape(SERVERS * SLOTS, 1)
+    wanted, keyed, valued = lax.optimization_barrier((wanted, keyed, valued))
+    parity = jnp.full((1, 1, 128), zl, jnp.int32)
     served = pl.pallas_call(
         serve_kernel,
         out_shape=jax.ShapeDtypeStruct((SERVERS, SLOTS, WIDE), BF),
-        in_specs=vmem(2 + RING + 1),
+        in_specs=vmem(3 + RING + 1),
         out_specs=pl.BlockSpec(memory_space=pltpu.VMEM),
-        scratch_shapes=[pltpu.VMEM((RING * PIECE, E), BF), pltpu.VMEM((RING * 32, KEY), BF)],
+        scratch_shapes=[pltpu.VMEM((RING * ROWS, E), BF), pltpu.VMEM((RING * 2 * SLAB_ROWS, KEY), F32)],
         compiler_params=pltpu.CompilerParams(vmem_limit_bytes=32 * 2**20),
-    )(wanted, asked, *pieces)
+    )(parity, wanted, asked, *pieces)
     got = lax.all_to_all(served, NEAR, split_axis=0, concat_axis=0, tiled=True)
-    acts = group_acts.reshape(GROUPS * CT, E)
-    keyed = jnp.dot(acts, w_qk[:, HD:], preferred_element_type=F32).astype(BF)
-    valued = jnp.dot(acts, w_v, preferred_element_type=F32).astype(BF)
     best, encoded = pl.pallas_call(
         layer_kernel,
         out_shape=(

time: 187 us -> 151 us (0.81)
  waiting for transfers between devices: 81.8 us -> 45.1 us
  starting transfers between devices: 56.4 us -> 59.9 us
  other arithmetic: 5.51 us -> 2.94 us
    all_gather x1, waiting for transfers between devices: 50.1 us -> 0.01 us  [per_device(): whole = lax.all_gather(packed, 'pb', axis=0, tiled=False)]
    all_to_all x1, waiting for transfers between devices: 0.01 us -> 25.5 us  [per_device(): got = lax.all_to_all(served, NEAR, split_axis=0, concat_axis=0, tiled=True)]
    ppermute x8, waiting for transfers between devices: 31.7 us -> 18.2 us  [ring_moved(): lax.ppermute(piece, 'zh', [(i, (i + step) % RING) for i in range(RING)])]
    all_to_all x1, starting transfers between devices: 8.07 us -> 12 us  [per_device(): got = lax.all_to_all(served, NEAR, split_axis=0, concat_axis=0, tiled=True)]
    ppermute x0 -> x1, starting transfers between devices: none -> 3.83 us  [per_device(): pair = lax.ppermute(pair, 'zl', [(0, 1), (1, 0)])]
    ppermute x8, starting transfers between devices: 38.2 us -> 34.5 us  [ring_moved(): lax.ppermute(piece, 'zh', [(i, (i + step) % RING) for i in range(RING)])]
    convert_element_type x3 -> x1, local copies, waits for them, and re-layouts: 2.72 us -> 0.78 us  [per_device(): lax.dynamic_slice_in_dim(slab, y * SLAB_ROWS, SLAB_ROWS, 0).astype(BF)]
    unnamed x26 -> x28, local copies, waits for them, and re-layouts: 5.32 us -> 6.55 us
  transfers between devices with their start and end apart: 11 -> 12, of which waited for: 5 -> 7; matrix products, arithmetic and copies ran while one was open for 8% -> 8% of each run, Pallas kernels for 0% -> 0%
where the time goes in v2:
time: 151 us; the launch traced here: 149 us
  starting transfers between devices  59.9 us (40%)
  waiting for transfers between devices  45.1 us (30%)
  local copies, waits for them, and re-layouts  18.6 us (12%)
  between operations  14.5 us (10%)
  Pallas kernels  6.96 us (5%)
  other arithmetic  2.94 us (2%)
    ppermute x8, starting transfers between devices, ring_moved(): lax.ppermute(piece, 'zh', [(i, (i + step) % RING) for i in range(RING)])  34.5 us
    all_to_all x1, waiting for transfers between devices, per_device(): got = lax.all_to_all(served, NEAR, split_axis=0, concat_axis=0, tiled=True)  25.5 us
    ppermute x8, waiting for transfers between devices, ring_moved(): lax.ppermute(piece, 'zh', [(i, (i + step) % RING) for i in range(RING)])  18.2 us
    all_to_all x1, starting transfers between devices, per_device(): got = lax.all_to_all(served, NEAR, split_axis=0, concat_axis=0, tiled=True)  12 us
    all_to_all x1, starting transfers between devices, per_device(): asked = lax.all_to_all(sent, FLAT, split_axis=0, concat_axis=0, tiled=True)  9.45 us
    unnamed x28, local copies, waits for them, and re-layouts  6.55 us
    pallas_call x1, Pallas kernels, per_device(): pl.pallas_call(serve_kernel, out_shape=jax.ShapeDtypeStruct((SERVERS, SLO...  3.84 us
    ppermute x1, starting transfers between devices, per_device(): pair = lax.ppermute(pair, 'zl', [(0, 1), (1, 0)])  3.83 us
  transfers between devices with their start and end apart: 12, of which 7 were waited for; matrix products, arithmetic and copies ran while one was open for 8% of the time, Pallas kernels for 0%

profile of v2, /device:TPU:6, one launch (start us, length us, event | category | flops | bytes accessed | tf_op | source)
XLA Modules:
  0.0 149.3 jit_solution(6821406759810319185)
XLA Ops:
  7.2 0.0 copy-start
  7.2 0.0 copy-start.12
  7.2 0.0 all-gather.3.cloned.1.call-start
  7.2 1.0 fusion.22
  8.3 0.0 copy-start.10
  8.3 2.3 %pad_maximum_fusion.1 = bf16[448,896]{1,0:T(8,128)(2,1)} fusion(bf16[112,896]{1,0:T(8,128)(2,1)} %param.19, bf16[112,448]{1,0:T(8,128)(2,1)S(1)} %get-tuple-element.23, bf16[112,448]{1,0:T(8,128)(2,1)S(1)} %get-tuple-element.22, bf16[224,448]{1,0:T(8,128)(2,1)} %param.17, bf16[224,448]{1,0:T(8,128)(2,1)} %param.16), kind=kLoop, calls=%fused_computation.6 | loop fusion | flops 4014080 | bytes 1605632 | tf_op jit(solution)/shard_map/concatenate | solution.py:160
  10.6 0.0 all-gather.3.cloned.1.call-update
  10.6 0.0 copy-done.12
  10.6 0.1 reshape.179
  10.7 0.2 select_reduce_fusion.1
  10.9 0.1 select_reduce_fusion
  11.0 0.8 dynamic-slice_convert_fusion
  11.8 3.8 %collective-permute-start = (bf16[32,384]{1,0:T(8,128)(2,1)S(1)}, bf16[32,384]{1,0:T(8,128)(2,1)S(1)}, u32[]{:S(2)}, u32[]{:S(2)}) collective-permute-start(bf16[32,384]{1,0:T(8,128)(2,1)S(1)} %fusion.16), channel_id=1, source_target_pairs={{0,8},{8,0},{1,9},{9,1},{2,10},{10,2},{3,11},{11,3},{4,12},{12,4},... | collective-permute-start | bytes 73736 | tf_op jit(solution)/shard_map/ppermute | solution.py:197
  15.6 0.4 constant_dynamic-slice_fusion
  16.0 0.1 slice.58
  16.2 1.4 collective-permute-done
  17.5 0.1 stack_reshape_squeeze.3
  17.7 0.0 copy-start.9
  17.7 1.0 broadcast_in_dim.50
  18.7 9.4 %all-to-all-start = ((bf16[32,32,384]{2,1,0:T(8,128)(2,1)}), bf16[32,32,384]{2,1,0:T(8,128)(2,1)S(1)}, u32[]{:S(2)}, u32[]{:S(2)}) async-start(bf16[32,32,384]{2,1,0:T(8,128)(2,1)} %bitcast.3), calls=%async_computation | async-start | bytes 1572864 | tf_op jit(solution)/shard_map/all_to_all | solution.py:215
  28.2 10.0 %collective-permute-start.4 = (bf16[120,896]{1,0:T(8,128)(2,1)S(1)}, bf16[120,896]{1,0:T(8,128)(2,1)S(1)}, u32[]{:S(2)}, u32[]{:S(2)}) collective-permute-start(bf16[120,896]{1,0:T(8,128)(2,1)S(1)} %pad_maximum_fusion.2.refs_0_), channel_id=1, source_target_pairs={{0,112},{16,0},{32,16},{48,32},{64,48},{80,64},{96,80},{112,96},{1... | collective-permute-start | bytes 645128 | tf_op jit(solution)/shard_map/ppermute | solution.py:153
  38.2 1.9 %collective-permute-start.1 = (bf16[120,896]{1,0:T(8,128)(2,1)S(1)}, bf16[120,896]{1,0:T(8,128)(2,1)S(1)}, u32[]{:S(2)}, u32[]{:S(2)}) collective-permute-start(bf16[120,896]{1,0:T(8,128)(2,1)S(1)} %pad_maximum_fusion.2.refs_0_), channel_id=1, source_target_pairs={{0,16},{16,32},{32,48},{48,64},{64,80},{80,96},{96,112},{112,0},{1... | collective-permute-start | bytes 645128 | tf_op jit(solution)/shard_map/ppermute | solution.py:153
  40.1 7.5 %collective-permute-done.4.refs_6_ = bf16[120,896]{1,0:T(8,128)(2,1)S(1)} collective-permute-done((bf16[120,896]{1,0:T(8,128)(2,1)S(1)}, bf16[120,896]{1,0:T(8,128)(2,1)S(1)}, u32[]{:S(2)}, u32[]{:S(2)}) %collective-permute-start.4) | collective-permute-done | bytes 215072 | tf_op jit(solution)/shard_map/ppermute | solution.py:153
  47.6 6.5 %collective-permute-start.5 = (bf16[120,896]{1,0:T(8,128)(2,1)S(1)}, bf16[120,896]{1,0:T(8,128)(2,1)S(1)}, u32[]{:S(2)}, u32[]{:S(2)}) collective-permute-start(bf16[120,896]{1,0:T(8,128)(2,1)S(1)} %collective-permute-done.4.refs_6_), channel_id=1, source_target_pairs={{0,112},{16,0},{32,16},{48,32},{64,48},{80,64},{96,80},{112,96},{1... | collective-permute-start | bytes 645128 | tf_op jit(solution)/shard_map/ppermute | solution.py:153
  54.1 0.0 collective-permute-done.1.refs_1_
  54.1 1.9 %collective-permute-start.2 = (bf16[120,896]{1,0:T(8,128)(2,1)S(1)}, bf16[120,896]{1,0:T(8,128)(2,1)S(1)}, u32[]{:S(2)}, u32[]{:S(2)}) collective-permute-start(bf16[120,896]{1,0:T(8,128)(2,1)S(1)} %collective-permute-done.1.refs_1_), channel_id=1, source_target_pairs={{0,16},{16,32},{32,48},{48,64},{64,80},{80,96},{96,112},{112,0},{1... | collective-permute-start | bytes 645128 | tf_op jit(solution)/shard_map/ppermute | solution.py:153
  56.1 4.3 %collective-permute-done.5.refs_5_ = bf16[120,896]{1,0:T(8,128)(2,1)S(1)} collective-permute-done((bf16[120,896]{1,0:T(8,128)(2,1)S(1)}, bf16[120,896]{1,0:T(8,128)(2,1)S(1)}, u32[]{:S(2)}, u32[]{:S(2)}) %collective-permute-start.5) | collective-permute-done | bytes 215072 | tf_op jit(solution)/shard_map/ppermute | solution.py:153
  60.4 5.6 %collective-permute-start.6 = (bf16[120,896]{1,0:T(8,128)(2,1)S(1)}, bf16[120,896]{1,0:T(8,128)(2,1)S(1)}, u32[]{:S(2)}, u32[]{:S(2)}) collective-permute-start(bf16[120,896]{1,0:T(8,128)(2,1)S(1)} %collective-permute-done.5.refs_5_), channel_id=1, source_target_pairs={{0,112},{16,0},{32,16},{48,32},{64,48},{80,64},{96,80},{112,96},{1... | collective-permute-start | bytes 645128 | tf_op jit(solution)/shard_map/ppermute | solution.py:153
  66.0 1.5 %collective-permute-done.2.refs_2_ = bf16[120,896]{1,0:T(8,128)(2,1)S(1)} collective-permute-done((bf16[120,896]{1,0:T(8,128)(2,1)S(1)}, bf16[120,896]{1,0:T(8,128)(2,1)S(1)}, u32[]{:S(2)}, u32[]{:S(2)}) %collective-permute-start.2) | collective-permute-done | bytes 215072 | tf_op jit(solution)/shard_map/ppermute | solution.py:153
  67.5 1.9 %collective-permute-start.3 = (bf16[120,896]{1,0:T(8,128)(2,1)S(1)}, bf16[120,896]{1,0:T(8,128)(2,1)S(1)}, u32[]{:S(2)}, u32[]{:S(2)}) collective-permute-start(bf16[120,896]{1,0:T(8,128)(2,1)S(1)} %collective-permute-done.2.refs_2_), channel_id=1, source_target_pairs={{0,16},{16,32},{32,48},{48,64},{64,80},{80,96},{96,112},{112,0},{1... | collective-permute-start | bytes 645128 | tf_op jit(solution)/shard_map/ppermute | solution.py:153
  69.5 0.7 reshape.182
  70.2 3.1 %collective-permute-done.6.refs_4_ = bf16[120,896]{1,0:T(8,128)(2,1)S(1)} collective-permute-done((bf16[120,896]{1,0:T(8,128)(2,1)S(1)}, bf16[120,896]{1,0:T(8,128)(2,1)S(1)}, u32[]{:S(2)}, u32[]{:S(2)}) %collective-permute-start.6) | collective-permute-done | bytes 215072 | tf_op jit(solution)/shard_map/ppermute | solution.py:153
  73.3 0.6 slice.84
  73.9 4.8 %collective-permute-start.8 = (bf16[56,896]{1,0:T(8,128)(2,1)}, bf16[56,896]{1,0:T(8,128)(2,1)}, u32[]{:S(2)}, u32[]{:S(2)}) collective-permute-start(bf16[56,896]{1,0:T(8,128)(2,1)} %slice.84), channel_id=1, source_target_pairs={{0,112},{16,0},{32,16},{48,32},{64,48},{80,64},{96,80},{112,96},{1... | collective-permute-start | bytes 301064 | tf_op jit(solution)/shard_map/ppermute | solution.py:153
  78.8 0.0 collective-permute-done.3.refs_3_
  78.8 0.7 slice.83
  79.5 1.9 %collective-permute-start.7 = (bf16[64,896]{1,0:T(8,128)(2,1)}, bf16[64,896]{1,0:T(8,128)(2,1)}, u32[]{:S(2)}, u32[]{:S(2)}) collective-permute-start(bf16[64,896]{1,0:T(8,128)(2,1)} %slice.83), channel_id=1, source_target_pairs={{0,16},{16,32},{32,48},{48,64},{64,80},{80,96},{96,112},{112,0},{1... | collective-permute-start | bytes 344072 | tf_op jit(solution)/shard_map/ppermute | solution.py:153
  81.4 0.0 all-to-all-done.keys
  81.5 0.1 select_n.61
  81.6 0.0 all-gather.3.cloned.1.call-done
  81.6 1.4 fusion.21
  83.0 1.6 %slice.78 = bf16[4,224,896]{2,1,0:T(8,128)(2,1)S(1)} slice(bf16[4,448,896]{2,1,0:T(8,128)(2,1)} %bitcast.30), slice={[0:4], [0:224], [0:896]} | slice | bytes 3211264 | tf_op jit(solution)/shard_map/slice | solution.py:170
  84.6 0.1 pad_maximum_fusion
  84.7 1.0 copy-done.8
  85.7 0.3 fusion.1.valued
  86.0 1.1 fusion.keyed
  87.2 0.2 copy.28.code
  87.4 0.0 collective-permute-done.8.refs_8_
  87.4 1.7 %collective-permute-done.7.refs_7_ = bf16[64,896]{1,0:T(8,128)(2,1)} collective-permute-done((bf16[64,896]{1,0:T(8,128)(2,1)}, bf16[64,896]{1,0:T(8,128)(2,1)}, u32[]{:S(2)}, u32[]{:S(2)}) %collective-permute-start.7) | collective-permute-done | bytes 114720 | tf_op jit(solution)/shard_map/ppermute | solution.py:153
  89.1 0.9 copy-done.6
  90.0 3.8 %shard_map.113 = bf16[64,16,1024]{2,1,0:T(8,128)(2,1)S(1)} custom-call(s32[1,1,128]{2,1,0:T(1,128)S(1)} %broadcast_in_dim.46.parity, s32[1024,1]{1,0:T(8,128)S(1)} %copy.28.code, bf16[32,32,384]{2,1,0:T(8,128)(2,1)S(1)} %all-to-all-done.keys, bf16[120,896]{1,0:T(8,128)(2,1)S(1)} %pad_maximum_fusion.2.refs_0_, ...), custom_call_target="tpu_custom_call" | custom-call | tf_op jit(solution)/shard_map/pallas_call | solution.py:222
  93.9 1.3 copy-done.1
  95.2 12.0 %all-to-all-start.1 = ((bf16[64,16,1024]{2,1,0:T(8,128)(2,1)}), bf16[64,16,1024]{2,1,0:T(8,128)(2,1)S(1)}, u32[]{:S(2)}, u32[]{:S(2)}) async-start(bf16[64,16,1024]{2,1,0:T(8,128)(2,1)} %copy-done.1), calls=%async_computation.1 | async-start | bytes 4194304 | tf_op jit(solution)/shard_map/all_to_all | solution.py:230
  107.3 0.1 reduce_max.12
  107.4 0.1 copy.24
  107.5 0.1 broadcast_add_fusion
  107.6 0.1 add.145.place
  107.7 2.1 %slice.85 = bf16[4,112,896]{2,1,0:T(8,128)(2,1)} slice(bf16[4,448,896]{2,1,0:T(8,128)(2,1)} %bitcast.31), slice={[0:4], [336:448], [0:896]} | slice | bytes 1605632 | tf_op jit(solution)/shard_map/slice | solution.py:173
  109.8 25.5 %all-to-all-done.1.got = bf16[64,16,1024]{2,1,0:T(8,128)(2,1)S(1)} async-done(((bf16[64,16,1024]{2,1,0:T(8,128)(2,1)}), bf16[64,16,1024]{2,1,0:T(8,128)(2,1)S(1)}, u32[]{:S(2)}, u32[]{:S(2)}) %all-to-all-start.1) | async-done | bytes 2097184 | tf_op jit(solution)/shard_map/all_to_all | solution.py:230
  135.3 1.4 copy-done.3
  136.7 1.1 copy-done.4
  137.9 3.1 %shard_map.114 = (f32[26,2]{1,0:T(8,128)S(1)}, bf16[208,896]{1,0:T(8,128)(2,1)S(1)}) custom-call(s32[208,1]{1,0:T(8,128)S(1)} %add.145.place, bf16[64,16,1024]{2,1,0:T(8,128)(2,1)S(1)} %all-to-all-done.1.got, bf16[104,448]{1,0:T(8,128)(2,1)S(1)} %copy-done.7, bf16[104,448]{1,0:T(8,128)(2,1)S(1)} %fusion.1.valued, bf16[896,896]{1,0:T(8,128)(2,1)S(1)} %bitcast.26, ...), custom_call_target="tpu_custom_call" | custom-call | tf_op jit(solution)/shard_map/pallas_call | solution.py:231
  141.0 0.6 copy.30
  141.7 0.8 reshape.186
  (38 shorter events, 0.3 us)
Async XLA Ops:
  7.2 8.5 %copy-start = (bf16[96,4,896]{2,1,0:T(4,128)(2,1)S(1)}, bf16[96,4,896]{2,1,0:T(4,128)(2,1)}, u32[]{:S(2)}) copy-start(bf16[96,4,896]{2,1,0:T(4,128)(2,1)} %param.14) | copy-start | bytes 2064388
  7.2 3.4 %copy-start.12 = (s32[26,2]{0,1:T(2,128)S(1)}, s32[26,2]{0,1:T(2,128)}, u32[]{:S(2)}) copy-start(s32[26,2]{0,1:T(2,128)} %param.12) | copy-start | bytes 628
  7.2 74.4 %all-gather.3.cloned.1.call-start = ((), (), s32[]{:S(2)}) async-start(), calls=%async_computation.2 | async-start | bytes 4014080 | tf_op jit(solution)/shard_map/all_gather | solution.py:168
  8.3 7.8 %copy-start.10 = (f32[26,384]{1,0:T(8,128)S(1)}, f32[26,384]{1,0:T(8,128)}, u32[]{:S(2)}) copy-start(f32[26,384]{1,0:T(8,128)} %param.10) | copy-start | bytes 119812
  11.8 5.7 %collective-permute-start = (bf16[32,384]{1,0:T(8,128)(2,1)S(1)}, bf16[32,384]{1,0:T(8,128)(2,1)S(1)}, u32[]{:S(2)}, u32[]{:S(2)}) collective-permute-start(bf16[32,384]{1,0:T(8,128)(2,1)S(1)} %fusion.16), channel_id=1, source_target_pairs={{0,8},{8,0},{1,9},{9,1},{2,10},{10,2},{3,11},{11,3},{4,12},{12,4},... | collective-permute-start | bytes 73736 | tf_op jit(solution)/shard_map/ppermute | solution.py:197
  17.7 51.8 %copy-start.9 = (bf16[26,4,896]{2,1,0:T(4,128)(2,1)S(1)}, bf16[26,4,896]{2,1,0:T(4,128)(2,1)}, u32[]{:S(2)}) copy-start(bf16[26,4,896]{2,1,0:T(4,128)(2,1)} %param.13) | copy-start | bytes 559108
  18.7 62.7 %all-to-all-start = ((bf16[32,32,384]{2,1,0:T(8,128)(2,1)}), bf16[32,32,384]{2,1,0:T(8,128)(2,1)S(1)}, u32[]{:S(2)}, u32[]{:S(2)}) async-start(bf16[32,32,384]{2,1,0:T(8,128)(2,1)} %bitcast.3), calls=%async_computation | async-start | bytes 1572864 | tf_op jit(solution)/shard_map/all_to_all | solution.py:215
  28.2 19.4 %collective-permute-start.4 = (bf16[120,896]{1,0:T(8,128)(2,1)S(1)}, bf16[120,896]{1,0:T(8,128)(2,1)S(1)}, u32[]{:S(2)}, u32[]{:S(2)}) collective-permute-start(bf16[120,896]{1,0:T(8,128)(2,1)S(1)} %pad_maximum_fusion.2.refs_0_), channel_id=1, source_target_pairs={{0,112},{16,0},{32,16},{48,32},{64,48},{80,64},{96,80},{112,96},{1... | collective-permute-start | bytes 645128 | tf_op jit(solution)/shard_map/ppermute | solution.py:153
  38.2 16.0 %collective-permute-start.1 = (bf16[120,896]{1,0:T(8,128)(2,1)S(1)}, bf16[120,896]{1,0:T(8,128)(2,1)S(1)}, u32[]{:S(2)}, u32[]{:S(2)}) collective-permute-start(bf16[120,896]{1,0:T(8,128)(2,1)S(1)} %pad_maximum_fusion.2.refs_0_), channel_id=1, source_target_pairs={{0,16},{16,32},{32,48},{48,64},{64,80},{80,96},{96,112},{112,0},{1... | collective-permute-start | bytes 645128 | tf_op jit(solution)/shard_map/ppermute | solution.py:153
  47.6 12.8 %collective-permute-start.5 = (bf16[120,896]{1,0:T(8,128)(2,1)S(1)}, bf16[120,896]{1,0:T(8,128)(2,1)S(1)}, u32[]{:S(2)}, u32[]{:S(2)}) collective-permute-start(bf16[120,896]{1,0:T(8,128)(2,1)S(1)} %collective-permute-done.4.refs_6_), channel_id=1, source_target_pairs={{0,112},{16,0},{32,16},{48,32},{64,48},{80,64},{96,80},{112,96},{1... | collective-permute-start | bytes 645128 | tf_op jit(solution)/shard_map/ppermute | solution.py:153
  54.1 13.4 %collective-permute-start.2 = (bf16[120,896]{1,0:T(8,128)(2,1)S(1)}, bf16[120,896]{1,0:T(8,128)(2,1)S(1)}, u32[]{:S(2)}, u32[]{:S(2)}) collective-permute-start(bf16[120,896]{1,0:T(8,128)(2,1)S(1)} %collective-permute-done.1.refs_1_), channel_id=1, source_target_pairs={{0,16},{16,32},{32,48},{48,64},{64,80},{80,96},{96,112},{112,0},{1... | collective-permute-start | bytes 645128 | tf_op jit(solution)/shard_map/ppermute | solution.py:153
  60.4 12.9 %collective-permute-start.6 = (bf16[120,896]{1,0:T(8,128)(2,1)S(1)}, bf16[120,896]{1,0:T(8,128)(2,1)S(1)}, u32[]{:S(2)}, u32[]{:S(2)}) collective-permute-start(bf16[120,896]{1,0:T(8,128)(2,1)S(1)} %collective-permute-done.5.refs_5_), channel_id=1, source_target_pairs={{0,112},{16,0},{32,16},{48,32},{64,48},{80,64},{96,80},{112,96},{1... | collective-permute-start | bytes 645128 | tf_op jit(solution)/shard_map/ppermute | solution.py:153
  67.5 17.0 %copy-start.5 = (bf16[120,896]{1,0:T(8,128)(2,1)}, bf16[120,896]{1,0:T(8,128)(2,1)S(1)}, u32[]{:S(2)}) copy-start(bf16[120,896]{1,0:T(8,128)(2,1)S(1)} %collective-permute-done.2.refs_2_) | copy-start | bytes 645124
  67.5 11.3 %collective-permute-start.3 = (bf16[120,896]{1,0:T(8,128)(2,1)S(1)}, bf16[120,896]{1,0:T(8,128)(2,1)S(1)}, u32[]{:S(2)}, u32[]{:S(2)}) collective-permute-start(bf16[120,896]{1,0:T(8,128)(2,1)S(1)} %collective-permute-done.2.refs_2_), channel_id=1, source_target_pairs={{0,16},{16,32},{32,48},{48,64},{64,80},{80,96},{96,112},{112,0},{1... | collective-permute-start | bytes 645128 | tf_op jit(solution)/shard_map/ppermute | solution.py:153
  73.9 13.5 %collective-permute-start.8 = (bf16[56,896]{1,0:T(8,128)(2,1)}, bf16[56,896]{1,0:T(8,128)(2,1)}, u32[]{:S(2)}, u32[]{:S(2)}) collective-permute-start(bf16[56,896]{1,0:T(8,128)(2,1)} %slice.84), channel_id=1, source_target_pairs={{0,112},{16,0},{32,16},{48,32},{64,48},{80,64},{96,80},{112,96},{1... | collective-permute-start | bytes 301064 | tf_op jit(solution)/shard_map/ppermute | solution.py:153
  79.5 9.6 %collective-permute-start.7 = (bf16[64,896]{1,0:T(8,128)(2,1)}, bf16[64,896]{1,0:T(8,128)(2,1)}, u32[]{:S(2)}, u32[]{:S(2)}) collective-permute-start(bf16[64,896]{1,0:T(8,128)(2,1)} %slice.83), channel_id=1, source_target_pairs={{0,16},{16,32},{32,48},{48,64},{64,80},{80,96},{96,112},{112,0},{1... | collective-permute-start | bytes 344072 | tf_op jit(solution)/shard_map/ppermute | solution.py:153
  84.6 1.4 copy-start.2
  84.6 1.1 copy-start.8
  89.1 0.9 copy-start.6
  93.8 1.4 copy-start.1
  95.2 12.2 %copy-start.11 = (f32[896]{0:T(1024)S(1)}, f32[896]{0:T(1024)}, u32[]{:S(2)}) copy-start(f32[896]{0:T(1024)} %param.15) | copy-start | bytes 10756
  95.2 40.1 %all-to-all-start.1 = ((bf16[64,16,1024]{2,1,0:T(8,128)(2,1)}), bf16[64,16,1024]{2,1,0:T(8,128)(2,1)S(1)}, u32[]{:S(2)}, u32[]{:S(2)}) async-start(bf16[64,16,1024]{2,1,0:T(8,128)(2,1)} %copy-done.1), calls=%async_computation.1 | async-start | bytes 4194304 | tf_op jit(solution)/shard_map/all_to_all | solution.py:230
  107.3 28.1 %copy-start.7 = (bf16[104,448]{1,0:T(8,128)(2,1)S(1)}, bf16[104,448]{1,0:T(8,128)(2,1)}, u32[]{:S(2)}) copy-start(bf16[104,448]{1,0:T(8,128)(2,1)} %fusion.keyed) | copy-start | bytes 279556
  135.3 1.4 copy-start.3
  136.7 1.1 copy-start.4
Sparse Core Ops, SparseCore 0:
  10.7 55.9 all-gather.2

commit v3 on v2

--- a/solution.py
+++ b/solution.py
@@ -25,6 +25,8 @@
 KEYPAD = 32
 WIDE = E + 128
 CUT = 64
+LIMIT = 52 * 2**20
+SERVE_LIMIT = 52 * 2**20
 LOW = -1.0e38
 SPLIT = ("x", "zh", "zl", "core", "pb")
 DB = ("x", "zh", "zl", "core")
@@ -44,8 +46,8 @@
     return hi, lo
 
 
-def serve_kernel(parity, code, keys, *refs):
-    *pieces, far_a, far_b, out, held, slab = refs
+def serve_kernel(parity, tick, code, keys, *refs):
+    *pieces, far_a, far_b, sent, held, slab, out, sems = refs
     for k in range(RING):
         if k == RING // 2:
             held[k * ROWS : k * ROWS + CUT, :] = far_a[...]
@@ -58,13 +60,6 @@
         for part in range(2):
             at = (2 * k + part) * SLAB_ROWS
             slab[at : at + SLAB_ROWS, :] = extra[:, part * KEY : (part + 1) * KEY].astype(F32)
-    step = 256
-    for i in range(SERVERS * SLOTS // step):
-        label = lax.broadcasted_iota(jnp.int32, (step, RING * ROWS), 1)
-        pick = (code[i * step : (i + 1) * step, :] == label).astype(F32).astype(BF)
-        found = jnp.dot(pick, held[...], preferred_element_type=F32).astype(BF)
-        n = step // SLOTS
-        out[i * n : (i + 1) * n, :, :E] = found.reshape(n, SLOTS, E)
     wide = 512
     n = wide // KEYPAD
     rows = slab[...].astype(BF)
@@ -103,15 +98,48 @@
         for z in range(2):
             at = z * PLANE + i * n
             out[at : at + n, :, E:] = jnp.where(mine == z, total, none).astype(BF)
-
-
-def layer_kernel(place, got, keyed, valued, w_query, w_out, gain, best, encoded):
+    step = 256
+    n = step // SLOTS
+    copies = []
+    for i in range(SERVERS * SLOTS // step):
+        label = lax.broadcasted_iota(jnp.int32, (step, RING * ROWS), 1)
+        pick = (code[i * step : (i + 1) * step, :] == label).astype(F32).astype(BF)
+        found = jnp.dot(pick, held[...], preferred_element_type=F32).astype(BF)
+        out[i * n : (i + 1) * n, :, :E] = found.reshape(n, SLOTS, E)
+        block = pl.ds(i * n, n)
+        copies.append(pltpu.make_async_copy(out.at[block], sent.at[block], sems.at[i]))
+        copies[-1].start()
+    for copy in copies:
+        copy.wait()
+
+
+def layer_kernel(place, got, keyed, valued, whole, gain, best, encoded, w_query, w_out, sems):
+    copies = []
+    part = E // 4
+    for b in range(4):
+        copies.append(
+            pltpu.make_async_copy(
+                whole.at[b, pl.ds(0, part)], w_query.at[pl.ds(b * part, part)], sems.at[b]
+            )
+        )
+    for b in range(4):
+        copies.append(
+            pltpu.make_async_copy(
+                whole.at[b, pl.ds(part + part // 2, part // 2)],
+                w_out.at[pl.ds(b * part // 2, part // 2)],
+                sems.at[4 + b],
+            )
+        )
+    for copy in copies:
+        copy.start()
     label = lax.broadcasted_iota(jnp.int32, (PAIRS * NT, SERVERS * SLOTS), 1)
     pick = (place[...] == label).astype(F32).astype(BF)
     rows = got[:, :, :E].reshape(SERVERS * SLOTS, E)
     x = jnp.dot(pick, rows, preferred_element_type=F32)
     square = jnp.mean(x * x, axis=-1, keepdims=True)
     normed = (x * lax.rsqrt(square + 1e-06) * gain[...]).astype(BF)
+    for copy in copies:
+        copy.wait()
     query = jnp.dot(normed, w_query[:, :HD], preferred_element_type=F32).astype(BF)
     query = query.astype(F32)
     k_all = keyed[...]
@@ -134,15 +162,15 @@
         probs = (e / jnp.sum(e, axis=-1, keepdims=True)).astype(BF)
         mixed = mixed + jnp.dot(probs, v_h, preferred_element_type=F32)
     result = x + jnp.dot(mixed.astype(BF), w_out[...], preferred_element_type=F32)
-    encoded[...] = result.astype(BF)
+    encoded[...] = result.astype(BF).reshape(GROUPS, 2, NT, E)
     c = got[:, :, E:].astype(F32)
     c = c + pltpu.roll(c, 127, 2)
     hi, lo = best_two(c, pltpu.roll(c, 126, 2))
-    hi, lo = hi[0], lo[0]
-    for half in range(2):
-        n = min(16, GROUPS - 16 * half)
-        best[16 * half : 16 * half + n, 0:1] = hi[:n, 4 * half : 4 * half + 1]
-        best[16 * half : 16 * half + n, 1:2] = lo[:n, 4 * half : 4 * half + 1]
+    line = lax.broadcasted_iota(jnp.int32, (16, 128), 0)
+    lane = lax.broadcasted_iota(jnp.int32, (16, 128), 1)
+    for k, value in enumerate((hi[0], lo[0])):
+        turned = jnp.where(line == lane, value[:, 0:1], 0.0) + jnp.where(line + 16 == lane, value[:, 4:5], 0.0)
+        best[k : k + 1, :] = jnp.sum(turned, axis=0, keepdims=True)[:, :GROUPS]
 
 
 def vmem(count):
@@ -153,47 +181,38 @@
     return lax.ppermute(piece, "zh", [(i, (i + step) % RING) for i in range(RING)])
 
 
-def per_device(keys, slab, neighbour_ids, group_acts, table, norm_gain, w_query, w_key, w_value, w_out):
-    y = lax.axis_index("pb")
-    zh = lax.axis_index("zh")
-    zl = lax.axis_index("zl")
-    packed = jnp.concatenate(
-        [
-            jnp.concatenate([w_query, w_key], axis=1),
-            jnp.concatenate([w_value[: ROWS + 16], w_value[ROWS + 16 :]], axis=1),
-            w_out,
-        ],
-        axis=0,
-    )
-    whole = lax.all_gather(packed, "pb", axis=0, tiled=False)
+def pack_kernel(w_query, w_key, w_value, w_out, packed):
     part = w_query.shape[0]
-    w_qk = whole[:, :part].reshape(E, 2 * HD)
-    w_v = whole[:, part : part + part // 2]
-    w_v = jnp.concatenate([w_v[:, :, :HD], w_v[:, :, HD:]], axis=1).reshape(E, HD)
-    w_o = whole[:, part + part // 2 :].reshape(HD, E)
-    acts = group_acts.reshape(GROUPS * CT, E)
-    keyed = jnp.dot(acts, w_qk[:, HD:], preferred_element_type=F32).astype(BF)
-    valued = jnp.dot(acts, w_v, preferred_element_type=F32).astype(BF)
-    flat = neighbour_ids.T.reshape(PAIRS)
-    owner = lax.div(flat, ROWS)
-    local = flat - owner * ROWS
+    half = part // 2
+    packed[:part, :HD] = w_query[...]
+    packed[:part, HD:] = w_key[...]
+    packed[part : part + half, :HD] = w_value[:half, :]
+    packed[part : part + half, HD:] = w_value[half:, :]
+    packed[part + half :, :] = w_out[...]
+
+
+def marks_of(owner, local, parity):
     at = lax.iota(jnp.int32, PAIRS)
     rank = jnp.max(
         jnp.where((owner[:, None] == owner[None, :]) & (at[:, None] > at[None, :]), 1, 0), axis=1
     )
     column = ((owner >> 5) << 1) | (owner & 1)
     code = ((owner >> 1) & 1) * 128 + column * SLOTS + ((owner >> 2) & 7) * 2 + rank
-    place = (code >> 7) * (PLANE * SLOTS) + (code & 127)
-    place = place.reshape(2, GROUPS).T.reshape(GROUPS, 2, 1) + lax.iota(jnp.int32, NT) * 128
-    place = place.reshape(PAIRS * NT, 1)
-    flip = code ^ (zl * 128)
-    marks = jnp.sum(
-        jnp.where(flip[None, :] == lax.iota(jnp.int32, 256)[:, None], local[None, :] + 1, 0), axis=1
-    )
-    marks = marks.astype(BF)
+    label = lax.iota(jnp.int32, 128) + parity * 128
+    marks = jnp.sum(jnp.where(code[None, :] == label[:, None], local[None, :] + 1, 0), axis=1)
+    return code, marks.astype(BF)
+
+
+def per_device(keys, slab, neighbour_ids, group_acts, table, norm_gain, w_query, w_key, w_value, w_out):
+    y = lax.axis_index("pb")
+    zh = lax.axis_index("zh")
+    zl = lax.axis_index("zl")
+    flat = neighbour_ids.T.reshape(PAIRS)
+    owner = lax.div(flat, ROWS)
+    local = flat - owner * ROWS
     quarter = lax.dynamic_slice_in_dim(slab, y * SLAB_ROWS, SLAB_ROWS, 0).astype(BF)
-    other = jnp.pad(marks[None, 128:], ((0, KEYPAD - SLAB_ROWS - 1), (0, KEY - 128)))
-    pair = jnp.concatenate([quarter, other], axis=0)
+    numbers = jnp.pad(jnp.stack([owner, local]).astype(BF), ((0, KEYPAD - SLAB_ROWS - 2), (0, KEY - PAIRS)))
+    pair = jnp.concatenate([quarter, numbers], axis=0)
     pair = lax.ppermute(pair, "zl", [(0, 1), (1, 0)])
     token = lax.dynamic_index_in_dim(table, y, axis=1, keepdims=False)
     both = jnp.concatenate([quarter, pair[:SLAB_ROWS]], axis=1)
@@ -207,8 +226,30 @@
     far_a = ring_moved(right[3][:CUT], 1)
     far_b = ring_moved(left[3][CUT:], -1)
     pieces = [*right, left[3], left[2], left[1], far_a, far_b]
+    packed = pl.pallas_call(
+        pack_kernel,
+        out_shape=jax.ShapeDtypeStruct((2 * w_query.shape[0], E), BF),
+        in_specs=vmem(4),
+        out_specs=pl.BlockSpec(memory_space=pltpu.VMEM),
+    )(w_query, w_key, w_value, w_out)
+    whole = lax.all_gather(packed, "pb", axis=0, tiled=False)
+    part = w_query.shape[0]
+    w_k = whole[:, :part, HD:].reshape(E, HD)
+    w_v = whole[:, part : part + part // 2]
+    w_v = jnp.concatenate([w_v[:, :, :HD], w_v[:, :, HD:]], axis=1).reshape(E, HD)
+    acts = group_acts.reshape(GROUPS * CT, E)
+    keyed = jnp.dot(acts, w_k, preferred_element_type=F32).astype(BF)
+    valued = jnp.dot(acts, w_v, preferred_element_type=F32).astype(BF)
+    tick = right[1][:8, :128]
+    owner, local, pair, keys, tick = lax.optimization_barrier((owner, local, pair, keys, tick))
+    code, own = marks_of(owner, local, zl)
+    partner = pair[SLAB_ROWS : SLAB_ROWS + 2, :PAIRS].astype(jnp.int32)
+    _, other = marks_of(partner[0], partner[1], zl)
+    place = (code >> 7) * (PLANE * SLOTS) + (code & 127)
+    place = place.reshape(2, GROUPS).T.reshape(GROUPS, 2, 1) + lax.iota(jnp.int32, NT) * 128
+    place = place.reshape(PAIRS * NT, 1)
     sent = jnp.pad(keys.astype(BF), ((0, KEYPAD - GROUPS), (0, 0)))
-    asks = jnp.stack([marks[:128].reshape(8, SLOTS), pair[SLAB_ROWS, :128].reshape(8, SLOTS)], axis=1)
+    asks = jnp.stack([own.reshape(8, SLOTS), other.reshape(8, SLOTS)], axis=1)
     asks = jnp.pad(asks, ((0, 0), (GROUPS, KEYPAD - GROUPS - 2), (0, KEY - SLOTS)))
     sent = sent[None] + asks
     sent = jnp.broadcast_to(sent[None], (4, 8, KEYPAD, KEY)).reshape(PLANE, KEYPAD, KEY)
@@ -222,23 +263,33 @@
     served = pl.pallas_call(
         serve_kernel,
         out_shape=jax.ShapeDtypeStruct((SERVERS, SLOTS, WIDE), BF),
-        in_specs=vmem(3 + RING + 1),
-        out_specs=pl.BlockSpec(memory_space=pltpu.VMEM),
-        scratch_shapes=[pltpu.VMEM((RING * ROWS, E), BF), pltpu.VMEM((RING * 2 * SLAB_ROWS, KEY), F32)],
-        compiler_params=pltpu.CompilerParams(vmem_limit_bytes=32 * 2**20),
-    )(parity, wanted, asked, *pieces)
+        in_specs=vmem(4 + RING + 1),
+        out_specs=pl.BlockSpec(memory_space=pltpu.HBM),
+        scratch_shapes=[
+            pltpu.VMEM((RING * ROWS, E), BF),
+            pltpu.VMEM((RING * 2 * SLAB_ROWS, KEY), F32),
+            pltpu.VMEM((SERVERS, SLOTS, WIDE), BF),
+            pltpu.SemaphoreType.DMA((4,)),
+        ],
+        compiler_params=pltpu.CompilerParams(vmem_limit_bytes=SERVE_LIMIT),
+    )(parity, tick, wanted, asked, *pieces)
     got = lax.all_to_all(served, NEAR, split_axis=0, concat_axis=0, tiled=True)
     best, encoded = pl.pallas_call(
         layer_kernel,
         out_shape=(
-            jax.ShapeDtypeStruct((GROUPS, 2), F32),
-            jax.ShapeDtypeStruct((PAIRS * NT, E), BF),
+            jax.ShapeDtypeStruct((2, GROUPS), F32),
+            jax.ShapeDtypeStruct((GROUPS, 2, NT, E), BF),
         ),
-        in_specs=vmem(7),
+        in_specs=[*vmem(4), pl.BlockSpec(memory_space=pltpu.HBM), *vmem(1)],
         out_specs=tuple(vmem(2)),
-        compiler_params=pltpu.CompilerParams(vmem_limit_bytes=32 * 2**20),
-    )(place, got, keyed, valued, w_qk, w_o, norm_gain.reshape(1, E))
-    return best, encoded.reshape(GROUPS, 2, NT, E)
+        scratch_shapes=[
+            pltpu.VMEM((E, 2 * HD), BF),
+            pltpu.VMEM((HD, E), BF),
+            pltpu.SemaphoreType.DMA((8,)),
+        ],
+        compiler_params=pltpu.CompilerParams(vmem_limit_bytes=LIMIT),
+    )(place, got, keyed, valued, whole, norm_gain.reshape(1, E))
+    return best.T, encoded
 
 
 def solution(mesh):

time: 151 us -> 156 us (1.033)
  waiting for transfers between devices: 45.1 us -> 60.5 us
  local copies, waits for them, and re-layouts: 18.6 us -> 8.49 us
  Pallas kernels: 6.96 us -> 13.9 us
  starting transfers between devices: 59.9 us -> 55.5 us
  other arithmetic: 2.94 us -> 0.91 us
    ppermute x8, waiting for transfers between devices: 18.2 us -> 31.5 us  [ring_moved(): lax.ppermute(piece, 'zh', [(i, (i + step) % RING) for i in range(RING)])]
    unnamed x28 -> x15, local copies, waits for them, and re-layouts: 6.55 us -> 0.06 us
    pallas_call x1 -> x2, Pallas kernels: 3.12 us -> 8.82 us  [the longest x1 6.47 us: per_device(): pl.pallas_call(layer_kernel, out_shape=(jax.ShapeDtypeStruct((2, GROUPS),...]
    all_to_all x1, starting transfers between devices: 12 us -> 8 us  [per_device(): got = lax.all_to_all(served, NEAR, split_axis=0, concat_axis=0, tiled=True)]
    slice x6 -> x2, local copies, waits for them, and re-layouts: 4.79 us -> 1.63 us  [the longest x1 1.63 us: per_device(): w_k = whole[:, :part, HD:].reshape(E, HD)]
    concatenate x2 -> x1, other arithmetic: 2.29 us -> 0.01 us  [per_device(): pair = jnp.concatenate([quarter, numbers], axis=0)]
    all_to_all x1, waiting for transfers between devices: 25.5 us -> 27.6 us  [per_device(): got = lax.all_to_all(served, NEAR, split_axis=0, concat_axis=0, tiled=True)]
    all_to_all x1, starting transfers between devices: 9.45 us -> 7.56 us  [per_device(): asked = lax.all_to_all(sent, FLAT, split_axis=0, concat_axis=0, tiled=True)]
  transfers between devices with their start and end apart: 12 -> 12, of which waited for: 7 -> 7; matrix products, arithmetic and copies ran while one was open for 8% -> 6% of each run, Pallas kernels for 0% -> 0%
where the time goes in v3:
time: 156 us; the launch traced here: 154 us
  waiting for transfers between devices  60.5 us (39%)
  starting transfers between devices  55.5 us (36%)
  between operations  14.5 us (9%)
  Pallas kernels  13.9 us (9%)
  local copies, waits for them, and re-layouts  8.49 us (5%)
    ppermute x8, starting transfers between devices, ring_moved(): lax.ppermute(piece, 'zh', [(i, (i + step) % RING) for i in range(RING)])  36.1 us
    ppermute x8, waiting for transfers between devices, ring_moved(): lax.ppermute(piece, 'zh', [(i, (i + step) % RING) for i in range(RING)])  31.5 us
    all_to_all x1, waiting for transfers between devices, per_device(): got = lax.all_to_all(served, NEAR, split_axis=0, concat_axis=0, tiled=True)  27.6 us
    all_to_all x1, starting transfers between devices, per_device(): got = lax.all_to_all(served, NEAR, split_axis=0, concat_axis=0, tiled=True)  8 us
    all_to_all x1, starting transfers between devices, per_device(): asked = lax.all_to_all(sent, FLAT, split_axis=0, concat_axis=0, tiled=True)  7.56 us
    pallas_call x1, Pallas kernels, per_device(): pl.pallas_call(layer_kernel, out_shape=(jax.ShapeDtypeStruct((2, GROUPS),...  6.47 us
    pallas_call x1, Pallas kernels, per_device(): pl.pallas_call(serve_kernel, out_shape=jax.ShapeDtypeStruct((SERVERS, SLO...  5.04 us
    ppermute x1, starting transfers between devices, per_device(): pair = lax.ppermute(pair, 'zl', [(0, 1), (1, 0)])  3.81 us
  transfers between devices with their start and end apart: 12, of which 7 were waited for; matrix products, arithmetic and copies ran while one was open for 6% of the time, Pallas kernels for 0%

profile of v3, /device:TPU:6, one launch (start us, length us, event | category | flops | bytes accessed | tf_op | source)
XLA Modules:
  0.0 154.3 jit_solution(4611325840716359373)
XLA Ops:
  7.2 0.0 copy-start
  7.2 0.0 copy-start.6
  7.2 0.0 copy-start.4
  7.2 0.0 all-gather.3.cloned.1.call-start
  7.2 2.4 %shard_map.113 = bf16[448,896]{1,0:T(8,128)(2,1)} custom-call(bf16[224,448]{1,0:T(8,128)(2,1)} %w_query.1, bf16[224,448]{1,0:T(8,128)(2,1)} %w_key.1, bf16[224,448]{1,0:T(8,128)(2,1)} %w_value.1, bf16[112,896]{1,0:T(8,128)(2,1)} %w_out.1), custom_call_target="tpu_custom_call" | custom-call | tf_op jit(solution)/shard_map/pallas_call | solution.py:229
  9.6 0.0 all-gather.3.cloned.1.call-update
  9.6 0.0 copy-done.6
  9.6 0.1 reshape.183
  9.8 0.8 dynamic-slice_convert_fusion
  10.5 3.8 %collective-permute-start = (bf16[32,384]{1,0:T(8,128)(2,1)S(1)}, bf16[32,384]{1,0:T(8,128)(2,1)S(1)}, u32[]{:S(2)}, u32[]{:S(2)}) collective-permute-start(bf16[32,384]{1,0:T(8,128)(2,1)S(1)} %pad_maximum_fusion.2), channel_id=1, source_target_pairs={{0,8},{8,0},{1,9},{9,1},{2,10},{10,2},{3,11},{11,3},{4,12},{12,4},... | collective-permute-start | bytes 73736 | tf_op jit(solution)/shard_map/ppermute | solution.py:216
  14.4 0.0 copy-done
  14.4 0.4 constant_dynamic-slice_fusion
  14.8 0.1 reshape.182
  14.9 1.4 collective-permute-done
  16.3 5.2 %collective-permute-start.1 = (bf16[120,896]{1,0:T(8,128)(2,1)S(1)}, bf16[120,896]{1,0:T(8,128)(2,1)S(1)}, u32[]{:S(2)}, u32[]{:S(2)}) collective-permute-start(bf16[120,896]{1,0:T(8,128)(2,1)S(1)} %pad_maximum_fusion.1.refs_0_), channel_id=1, source_target_pairs={{0,16},{16,32},{32,48},{48,64},{64,80},{80,96},{96,112},{112,0},{1... | collective-permute-start | bytes 645128 | tf_op jit(solution)/shard_map/ppermute | solution.py:181
  21.5 12.3 %collective-permute-done.1.refs_1_ = bf16[120,896]{1,0:T(8,128)(2,1)S(1)} collective-permute-done((bf16[120,896]{1,0:T(8,128)(2,1)S(1)}, bf16[120,896]{1,0:T(8,128)(2,1)S(1)}, u32[]{:S(2)}, u32[]{:S(2)}) %collective-permute-start.1) | collective-permute-done | bytes 215072 | tf_op jit(solution)/shard_map/ppermute | solution.py:181
  33.8 0.2 select_reduce_fusion.1
  34.0 0.2 select_reduce_fusion.3
  34.2 0.1 select_reduce_fusion.2
  34.3 0.1 convert_element_type.62
  34.4 0.1 convert_element_type.65
  34.5 0.0 copy-done.4
  34.6 1.0 broadcast_in_dim.62
  35.6 7.6 %all-to-all-start = ((bf16[32,32,384]{2,1,0:T(8,128)(2,1)}), bf16[32,32,384]{2,1,0:T(8,128)(2,1)S(1)}, u32[]{:S(2)}, u32[]{:S(2)}) async-start(bf16[32,32,384]{2,1,0:T(8,128)(2,1)} %bitcast.7), calls=%async_computation | async-start | bytes 1572864 | tf_op jit(solution)/shard_map/all_to_all | solution.py:256
  43.2 4.7 %collective-permute-start.4 = (bf16[120,896]{1,0:T(8,128)(2,1)S(1)}, bf16[120,896]{1,0:T(8,128)(2,1)S(1)}, u32[]{:S(2)}, u32[]{:S(2)}) collective-permute-start(bf16[120,896]{1,0:T(8,128)(2,1)S(1)} %pad_maximum_fusion.1.refs_0_), channel_id=1, source_target_pairs={{0,112},{16,0},{32,16},{48,32},{64,48},{80,64},{96,80},{112,96},{1... | collective-permute-start | bytes 645128 | tf_op jit(solution)/shard_map/ppermute | solution.py:181
  47.9 2.0 %collective-permute-start.2 = (bf16[120,896]{1,0:T(8,128)(2,1)S(1)}, bf16[120,896]{1,0:T(8,128)(2,1)S(1)}, u32[]{:S(2)}, u32[]{:S(2)}) collective-permute-start(bf16[120,896]{1,0:T(8,128)(2,1)S(1)} %collective-permute-done.1.refs_1_), channel_id=1, source_target_pairs={{0,16},{16,32},{32,48},{48,64},{64,80},{80,96},{96,112},{112,0},{1... | collective-permute-start | bytes 645128 | tf_op jit(solution)/shard_map/ppermute | solution.py:181
  49.9 7.5 %collective-permute-done.4.refs_6_ = bf16[120,896]{1,0:T(8,128)(2,1)S(1)} collective-permute-done((bf16[120,896]{1,0:T(8,128)(2,1)S(1)}, bf16[120,896]{1,0:T(8,128)(2,1)S(1)}, u32[]{:S(2)}, u32[]{:S(2)}) %collective-permute-start.4) | collective-permute-done | bytes 215072 | tf_op jit(solution)/shard_map/ppermute | solution.py:181
  57.4 7.4 %collective-permute-start.5 = (bf16[120,896]{1,0:T(8,128)(2,1)S(1)}, bf16[120,896]{1,0:T(8,128)(2,1)S(1)}, u32[]{:S(2)}, u32[]{:S(2)}) collective-permute-start(bf16[120,896]{1,0:T(8,128)(2,1)S(1)} %collective-permute-done.4.refs_6_), channel_id=1, source_target_pairs={{0,112},{16,0},{32,16},{48,32},{64,48},{80,64},{96,80},{112,96},{1... | collective-permute-start | bytes 645128 | tf_op jit(solution)/shard_map/ppermute | solution.py:181
  64.8 0.6 collective-permute-done.2.refs_2_
  65.4 1.9 %collective-permute-start.3 = (bf16[120,896]{1,0:T(8,128)(2,1)S(1)}, bf16[120,896]{1,0:T(8,128)(2,1)S(1)}, u32[]{:S(2)}, u32[]{:S(2)}) collective-permute-start(bf16[120,896]{1,0:T(8,128)(2,1)S(1)} %collective-permute-done.2.refs_2_), channel_id=1, source_target_pairs={{0,16},{16,32},{32,48},{48,64},{64,80},{80,96},{96,112},{112,0},{1... | collective-permute-start | bytes 645128 | tf_op jit(solution)/shard_map/ppermute | solution.py:181
  67.3 6.0 %collective-permute-done.5.refs_5_ = bf16[120,896]{1,0:T(8,128)(2,1)S(1)} collective-permute-done((bf16[120,896]{1,0:T(8,128)(2,1)S(1)}, bf16[120,896]{1,0:T(8,128)(2,1)S(1)}, u32[]{:S(2)}, u32[]{:S(2)}) %collective-permute-start.5) | collective-permute-done | bytes 215072 | tf_op jit(solution)/shard_map/ppermute | solution.py:181
  73.3 6.5 %collective-permute-start.6 = (bf16[120,896]{1,0:T(8,128)(2,1)S(1)}, bf16[120,896]{1,0:T(8,128)(2,1)S(1)}, u32[]{:S(2)}, u32[]{:S(2)}) collective-permute-start(bf16[120,896]{1,0:T(8,128)(2,1)S(1)} %collective-permute-done.5.refs_5_), channel_id=1, source_target_pairs={{0,112},{16,0},{32,16},{48,32},{64,48},{80,64},{96,80},{112,96},{1... | collective-permute-start | bytes 645128 | tf_op jit(solution)/shard_map/ppermute | solution.py:181
  79.8 0.0 copy-done.3
  79.8 0.7 reshape.187
  80.6 0.0 collective-permute-done.3.refs_3_
  80.6 1.9 %collective-permute-start.7 = (bf16[64,896]{1,0:T(8,128)(2,1)S(1)}, bf16[64,896]{1,0:T(8,128)(2,1)S(1)}, u32[]{:S(2)}, u32[]{:S(2)}) collective-permute-start(bf16[64,896]{1,0:T(8,128)(2,1)S(1)} %slice.65), channel_id=1, source_target_pairs={{0,16},{16,32},{32,48},{48,64},{64,80},{80,96},{96,112},{112,0},{1... | collective-permute-start | bytes 344072 | tf_op jit(solution)/shard_map/ppermute | solution.py:181
  82.5 5.1 %collective-permute-done.6.refs_4_ = bf16[120,896]{1,0:T(8,128)(2,1)S(1)} collective-permute-done((bf16[120,896]{1,0:T(8,128)(2,1)S(1)}, bf16[120,896]{1,0:T(8,128)(2,1)S(1)}, u32[]{:S(2)}, u32[]{:S(2)}) %collective-permute-start.6) | collective-permute-done | bytes 215072 | tf_op jit(solution)/shard_map/ppermute | solution.py:181
  87.7 0.6 slice.66
  88.3 6.5 %collective-permute-start.8 = (bf16[56,896]{1,0:T(8,128)(2,1)}, bf16[56,896]{1,0:T(8,128)(2,1)S(1)}, u32[]{:S(2)}, u32[]{:S(2)}) collective-permute-start(bf16[56,896]{1,0:T(8,128)(2,1)} %slice.66), channel_id=1, source_target_pairs={{0,112},{16,0},{32,16},{48,32},{64,48},{80,64},{96,80},{112,96},{1... | collective-permute-start | bytes 301064 | tf_op jit(solution)/shard_map/ppermute | solution.py:181
  94.8 0.0 all-to-all-done.keys
  94.8 0.0 copy-start.1
  94.9 0.1 select_n.70
  95.0 0.0 all-gather.3.cloned.1.call-done
  95.0 1.5 fusion.27
  96.5 0.0 copy-start.2
  96.5 1.6 %slice.62 = bf16[4,224,448]{2,1,0:T(8,128)(2,1)S(1)} slice(bf16[4,448,896]{2,1,0:T(8,128)(2,1)} %bitcast.33), slice={[0:4], [0:224], [448:896]} | slice | bytes 1605632 | tf_op jit(solution)/shard_map/slice | solution.py:237
  98.1 0.1 pad_maximum_fusion
  98.3 0.0 copy-done.1
  98.3 0.0 copy-done.2
  98.3 0.3 fusion.1.valued
  98.6 0.3 fusion.keyed
  98.9 1.0 copy.26.code
  99.9 0.0 collective-permute-done.8.refs_8_
  99.9 0.0 collective-permute-done.7.refs_7_
  99.9 5.0 %shard_map.114 = bf16[64,16,1024]{2,1,0:T(8,128)(2,1)} custom-call(s32[1,1,128]{2,1,0:T(1,128)S(1)} %broadcast_in_dim.57.parity, bf16[8,128]{1,0:T(8,128)(2,1)S(1)} %slice.58.tick, s32[1024,1]{1,0:T(8,128)} %copy.26.code, bf16[32,32,384]{2,1,0:T(8,128)(2,1)} %copy-done.1, bf16[120,896]{1,0:T(8,128)(2,1)S(1)} %pad_maximum_fusion.1.refs_0_, ...), custom_call_target="tpu_custom_call" | custom-call | tf_op jit(solution)/shard_map/pallas_call | solution.py:263
  105.0 0.0 copy-start.5
  105.0 8.0 %all-to-all-start.1 = ((bf16[64,16,1024]{2,1,0:T(8,128)(2,1)}), bf16[64,16,1024]{2,1,0:T(8,128)(2,1)}, u32[]{:S(2)}, u32[]{:S(2)}) async-start(bf16[64,16,1024]{2,1,0:T(8,128)(2,1)} %shard_map.114), calls=%async_computation.1 | async-start | bytes 4194304 | tf_op jit(solution)/shard_map/all_to_all | solution.py:276
  113.0 0.0 copy-done.5
  113.0 0.1 reshape.184
  113.1 0.1 copy.23
  113.2 0.1 broadcast_add_fusion
  113.3 0.1 add.148.place
  113.4 27.6 %all-to-all-done.1.got = bf16[64,16,1024]{2,1,0:T(8,128)(2,1)} async-done(((bf16[64,16,1024]{2,1,0:T(8,128)(2,1)}), bf16[64,16,1024]{2,1,0:T(8,128)(2,1)}, u32[]{:S(2)}, u32[]{:S(2)}) %all-to-all-start.1) | async-done | bytes 2097184 | tf_op jit(solution)/shard_map/all_to_all | solution.py:276
  141.0 6.5 %shard_map.115 = (f32[2,26]{1,0:T(2,128)}, bf16[26,2,4,896]{3,2,1,0:T(4,128)(2,1)}) custom-call(s32[208,1]{1,0:T(8,128)S(1)} %add.148.place, bf16[64,16,1024]{2,1,0:T(8,128)(2,1)} %all-to-all-done.1.got, bf16[104,448]{1,0:T(8,128)(2,1)S(1)} %fusion.keyed, bf16[104,448]{1,0:T(8,128)(2,1)S(1)} %fusion.1.valued, bf16[4,448,896]{2,1,0:T(8,128)(2,1)} %bitcast.34, ...), custom_call_target="tpu_custom_call" | custom-call | tf_op jit(solution)/shard_map/pallas_call | solution.py:277
  (30 shorter events, 0.3 us)
Async XLA Ops:
  7.2 7.2 %copy-start = (bf16[96,4,896]{2,1,0:T(4,128)(2,1)S(1)}, bf16[96,4,896]{2,1,0:T(4,128)(2,1)}, u32[]{:S(2)}) copy-start(bf16[96,4,896]{2,1,0:T(4,128)(2,1)} %param.14) | copy-start | bytes 2064388
  7.2 2.5 %copy-start.6 = (s32[26,2]{0,1:T(2,128)S(1)}, s32[26,2]{0,1:T(2,128)}, u32[]{:S(2)}) copy-start(s32[26,2]{0,1:T(2,128)} %param.12) | copy-start | bytes 628
  7.2 27.3 %copy-start.4 = (f32[26,384]{1,0:T(8,128)S(1)}, f32[26,384]{1,0:T(8,128)}, u32[]{:S(2)}) copy-start(f32[26,384]{1,0:T(8,128)} %param.10) | copy-start | bytes 119812
  7.2 87.8 %all-gather.3.cloned.1.call-start = ((), (), s32[]{:S(2)}) async-start(), calls=%async_computation.2 | async-start | bytes 4014080 | tf_op jit(solution)/shard_map/all_gather | solution.py:235
  10.5 5.7 %collective-permute-start = (bf16[32,384]{1,0:T(8,128)(2,1)S(1)}, bf16[32,384]{1,0:T(8,128)(2,1)S(1)}, u32[]{:S(2)}, u32[]{:S(2)}) collective-permute-start(bf16[32,384]{1,0:T(8,128)(2,1)S(1)} %pad_maximum_fusion.2), channel_id=1, source_target_pairs={{0,8},{8,0},{1,9},{9,1},{2,10},{10,2},{3,11},{11,3},{4,12},{12,4},... | collective-permute-start | bytes 73736 | tf_op jit(solution)/shard_map/ppermute | solution.py:216
  14.8 65.0 %copy-start.3 = (bf16[26,4,896]{2,1,0:T(4,128)(2,1)S(1)}, bf16[26,4,896]{2,1,0:T(4,128)(2,1)}, u32[]{:S(2)}) copy-start(bf16[26,4,896]{2,1,0:T(4,128)(2,1)} %param.13) | copy-start | bytes 559108
  16.3 17.5 %collective-permute-start.1 = (bf16[120,896]{1,0:T(8,128)(2,1)S(1)}, bf16[120,896]{1,0:T(8,128)(2,1)S(1)}, u32[]{:S(2)}, u32[]{:S(2)}) collective-permute-start(bf16[120,896]{1,0:T(8,128)(2,1)S(1)} %pad_maximum_fusion.1.refs_0_), channel_id=1, source_target_pairs={{0,16},{16,32},{32,48},{48,64},{64,80},{80,96},{96,112},{112,0},{1... | collective-permute-start | bytes 645128 | tf_op jit(solution)/shard_map/ppermute | solution.py:181
  35.6 59.2 %all-to-all-start = ((bf16[32,32,384]{2,1,0:T(8,128)(2,1)}), bf16[32,32,384]{2,1,0:T(8,128)(2,1)S(1)}, u32[]{:S(2)}, u32[]{:S(2)}) async-start(bf16[32,32,384]{2,1,0:T(8,128)(2,1)} %bitcast.7), calls=%async_computation | async-start | bytes 1572864 | tf_op jit(solution)/shard_map/all_to_all | solution.py:256
  43.2 14.2 %collective-permute-start.4 = (bf16[120,896]{1,0:T(8,128)(2,1)S(1)}, bf16[120,896]{1,0:T(8,128)(2,1)S(1)}, u32[]{:S(2)}, u32[]{:S(2)}) collective-permute-start(bf16[120,896]{1,0:T(8,128)(2,1)S(1)} %pad_maximum_fusion.1.refs_0_), channel_id=1, source_target_pairs={{0,112},{16,0},{32,16},{48,32},{64,48},{80,64},{96,80},{112,96},{1... | collective-permute-start | bytes 645128 | tf_op jit(solution)/shard_map/ppermute | solution.py:181
  47.9 17.5 %collective-permute-start.2 = (bf16[120,896]{1,0:T(8,128)(2,1)S(1)}, bf16[120,896]{1,0:T(8,128)(2,1)S(1)}, u32[]{:S(2)}, u32[]{:S(2)}) collective-permute-start(bf16[120,896]{1,0:T(8,128)(2,1)S(1)} %collective-permute-done.1.refs_1_), channel_id=1, source_target_pairs={{0,16},{16,32},{32,48},{48,64},{64,80},{80,96},{96,112},{112,0},{1... | collective-permute-start | bytes 645128 | tf_op jit(solution)/shard_map/ppermute | solution.py:181
  57.4 15.9 %collective-permute-start.5 = (bf16[120,896]{1,0:T(8,128)(2,1)S(1)}, bf16[120,896]{1,0:T(8,128)(2,1)S(1)}, u32[]{:S(2)}, u32[]{:S(2)}) collective-permute-start(bf16[120,896]{1,0:T(8,128)(2,1)S(1)} %collective-permute-done.4.refs_6_), channel_id=1, source_target_pairs={{0,112},{16,0},{32,16},{48,32},{64,48},{80,64},{96,80},{112,96},{1... | collective-permute-start | bytes 645128 | tf_op jit(solution)/shard_map/ppermute | solution.py:181
  65.4 15.2 %collective-permute-start.3 = (bf16[120,896]{1,0:T(8,128)(2,1)S(1)}, bf16[120,896]{1,0:T(8,128)(2,1)S(1)}, u32[]{:S(2)}, u32[]{:S(2)}) collective-permute-start(bf16[120,896]{1,0:T(8,128)(2,1)S(1)} %collective-permute-done.2.refs_2_), channel_id=1, source_target_pairs={{0,16},{16,32},{32,48},{48,64},{64,80},{80,96},{96,112},{112,0},{1... | collective-permute-start | bytes 645128 | tf_op jit(solution)/shard_map/ppermute | solution.py:181
  73.3 14.3 %collective-permute-start.6 = (bf16[120,896]{1,0:T(8,128)(2,1)S(1)}, bf16[120,896]{1,0:T(8,128)(2,1)S(1)}, u32[]{:S(2)}, u32[]{:S(2)}) collective-permute-start(bf16[120,896]{1,0:T(8,128)(2,1)S(1)} %collective-permute-done.5.refs_5_), channel_id=1, source_target_pairs={{0,112},{16,0},{32,16},{48,32},{64,48},{80,64},{96,80},{112,96},{1... | collective-permute-start | bytes 645128 | tf_op jit(solution)/shard_map/ppermute | solution.py:181
  80.6 19.3 %collective-permute-start.7 = (bf16[64,896]{1,0:T(8,128)(2,1)S(1)}, bf16[64,896]{1,0:T(8,128)(2,1)S(1)}, u32[]{:S(2)}, u32[]{:S(2)}) collective-permute-start(bf16[64,896]{1,0:T(8,128)(2,1)S(1)} %slice.65), channel_id=1, source_target_pairs={{0,16},{16,32},{32,48},{48,64},{64,80},{80,96},{96,112},{112,0},{1... | collective-permute-start | bytes 344072 | tf_op jit(solution)/shard_map/ppermute | solution.py:181
  88.3 11.6 %collective-permute-start.8 = (bf16[56,896]{1,0:T(8,128)(2,1)}, bf16[56,896]{1,0:T(8,128)(2,1)S(1)}, u32[]{:S(2)}, u32[]{:S(2)}) collective-permute-start(bf16[56,896]{1,0:T(8,128)(2,1)} %slice.66), channel_id=1, source_target_pairs={{0,112},{16,0},{32,16},{48,32},{64,48},{80,64},{96,80},{112,96},{1... | collective-permute-start | bytes 301064 | tf_op jit(solution)/shard_map/ppermute | solution.py:181
  94.8 3.5 %copy-start.1 = (bf16[32,32,384]{2,1,0:T(8,128)(2,1)}, bf16[32,32,384]{2,1,0:T(8,128)(2,1)S(1)}, u32[]{:S(2)}) copy-start(bf16[32,32,384]{2,1,0:T(8,128)(2,1)S(1)} %all-to-all-done.keys) | copy-start | bytes 2359300
  96.5 1.8 %copy-start.2 = (bf16[104,896]{1,0:T(8,128)(2,1)S(1)}, bf16[104,896]{1,0:T(8,128)(2,1)}, u32[]{:S(2)}) copy-start(bf16[104,896]{1,0:T(8,128)(2,1)} %reshape.187) | copy-start | bytes 559108
  105.0 8.0 %copy-start.5 = (f32[896]{0:T(1024)S(1)}, f32[896]{0:T(1024)}, u32[]{:S(2)}) copy-start(f32[896]{0:T(1024)} %param.15) | copy-start | bytes 10756
  105.0 36.0 %all-to-all-start.1 = ((bf16[64,16,1024]{2,1,0:T(8,128)(2,1)}), bf16[64,16,1024]{2,1,0:T(8,128)(2,1)}, u32[]{:S(2)}, u32[]{:S(2)}) async-start(bf16[64,16,1024]{2,1,0:T(8,128)(2,1)} %shard_map.114), calls=%async_computation.1 | async-start | bytes 4194304 | tf_op jit(solution)/shard_map/all_to_all | solution.py:276
Sparse Core Ops, SparseCore 0:
  10.1 60.6 all-gather.2

commit v4 on v3

--- a/solution.py
+++ b/solution.py
@@ -24,8 +24,7 @@
 SLOTS = 16
 KEYPAD = 32
 WIDE = E + 128
-CUT = 64
-LIMIT = 52 * 2**20
+LIMIT = 24 * 2**20
 SERVE_LIMIT = 52 * 2**20
 LOW = -1.0e38
 SPLIT = ("x", "zh", "zl", "core", "pb")
@@ -46,17 +45,11 @@
     return hi, lo
 
 
-def serve_kernel(parity, tick, code, keys, *refs):
-    *pieces, far_a, far_b, sent, held, slab, out, sems = refs
-    for k in range(RING):
-        if k == RING // 2:
-            held[k * ROWS : k * ROWS + CUT, :] = far_a[...]
-            held[k * ROWS + CUT : (k + 1) * ROWS, :] = far_b[: ROWS - CUT, :]
-            extra = far_b[ROWS - CUT :, :]
-        else:
-            piece = pieces[k if k < RING // 2 else k - 1]
-            held[k * ROWS : (k + 1) * ROWS, :] = piece[:ROWS, :]
-            extra = piece[ROWS:, :]
+def serve_kernel(parity, code, keys, *refs):
+    *pieces, sent, held, slab, out, sems = refs
+    for k, piece in enumerate(pieces):
+        held[k * ROWS : (k + 1) * ROWS, :] = piece[:ROWS, :]
+        extra = piece[ROWS:, :]
         for part in range(2):
             at = (2 * k + part) * SLAB_ROWS
             slab[at : at + SLAB_ROWS, :] = extra[:, part * KEY : (part + 1) * KEY].astype(F32)
@@ -113,34 +106,14 @@
         copy.wait()
 
 
-def layer_kernel(place, got, keyed, valued, whole, gain, best, encoded, w_query, w_out, sems):
-    copies = []
-    part = E // 4
-    for b in range(4):
-        copies.append(
-            pltpu.make_async_copy(
-                whole.at[b, pl.ds(0, part)], w_query.at[pl.ds(b * part, part)], sems.at[b]
-            )
-        )
-    for b in range(4):
-        copies.append(
-            pltpu.make_async_copy(
-                whole.at[b, pl.ds(part + part // 2, part // 2)],
-                w_out.at[pl.ds(b * part // 2, part // 2)],
-                sems.at[4 + b],
-            )
-        )
-    for copy in copies:
-        copy.start()
+def layer_kernel(place, got, keyed, valued, w_query, w_out, gain, best, encoded):
     label = lax.broadcasted_iota(jnp.int32, (PAIRS * NT, SERVERS * SLOTS), 1)
     pick = (place[...] == label).astype(F32).astype(BF)
     rows = got[:, :, :E].reshape(SERVERS * SLOTS, E)
     x = jnp.dot(pick, rows, preferred_element_type=F32)
     square = jnp.mean(x * x, axis=-1, keepdims=True)
     normed = (x * lax.rsqrt(square + 1e-06) * gain[...]).astype(BF)
-    for copy in copies:
-        copy.wait()
-    query = jnp.dot(normed, w_query[:, :HD], preferred_element_type=F32).astype(BF)
+    query = jnp.dot(normed, w_query[...], preferred_element_type=F32).astype(BF)
     query = query.astype(F32)
     k_all = keyed[...]
     v_all = valued[...].astype(F32)
@@ -177,8 +150,12 @@
     return [pl.BlockSpec(memory_space=pltpu.VMEM)] * count
 
 
-def ring_moved(piece, step):
-    return lax.ppermute(piece, "zh", [(i, (i + step) % RING) for i in range(RING)])
+def ring_moved(piece):
+    pairs = []
+    for at in range(RING):
+        pairs.append((2 * at, 2 * ((at + 1) % RING)))
+        pairs.append((2 * at + 1, 2 * ((at - 1) % RING) + 1))
+    return lax.ppermute(piece, ("zh", "core"), pairs)
 
 
 def pack_kernel(w_query, w_key, w_value, w_out, packed):
@@ -191,13 +168,33 @@
     packed[part + half :, :] = w_out[...]
 
 
-def marks_of(owner, local, parity):
+def project_kernel(acts, whole, keyed, valued, w_query, w_out, w_key, w_value):
+    part = E // 4
+    half = part // 2
+    for b in range(4):
+        at = b * part
+        w_query[at : at + part, :] = whole[b, :part, :HD]
+        w_key[at : at + part, :] = whole[b, :part, HD:]
+        w_value[at : at + half, :] = whole[b, part : part + half, :HD]
+        w_value[at + half : at + part, :] = whole[b, part : part + half, HD:]
+        w_out[b * half : (b + 1) * half, :] = whole[b, part + half :, :]
+    x = acts[...]
+    keyed[...] = jnp.dot(x, w_key[...], preferred_element_type=F32).astype(BF)
+    valued[...] = jnp.dot(x, w_value[...], preferred_element_type=F32).astype(BF)
+
+
+def marks_of(owner, local, zh, parity):
     at = lax.iota(jnp.int32, PAIRS)
     rank = jnp.max(
         jnp.where((owner[:, None] == owner[None, :]) & (at[:, None] > at[None, :]), 1, 0), axis=1
     )
-    column = ((owner >> 5) << 1) | (owner & 1)
-    code = ((owner >> 1) & 1) * 128 + column * SLOTS + ((owner >> 2) & 7) * 2 + rank
+    core = owner & 1
+    away = (zh - (owner >> 2)) & 7
+    direct = (away & 3) == 0
+    server = jnp.where(direct, core, away >> 2)
+    steps = jnp.where(away > 4, 8 - away, away)
+    slot = jnp.where(direct, 12 + (away >> 1), (steps - 1) * 4 + (core ^ server) * 2) + rank
+    code = ((owner >> 1) & 1) * 128 + (((owner >> 5) << 1) | server) * SLOTS + slot
     label = lax.iota(jnp.int32, 128) + parity * 128
     marks = jnp.sum(jnp.where(code[None, :] == label[:, None], local[None, :] + 1, 0), axis=1)
     return code, marks.astype(BF)
@@ -218,14 +215,13 @@
     both = jnp.concatenate([quarter, pair[:SLAB_ROWS]], axis=1)
     both = jnp.pad(both, ((0, 0), (0, E - 2 * KEY)))
     piece = jnp.concatenate([token, both], axis=0)
-    right = [piece]
-    left = [piece]
+    ours = [piece]
+    others = [lax.ppermute(piece, "core", [(0, 1), (1, 0)])]
     for _ in range(3):
-        right.append(ring_moved(right[-1], 1))
-        left.append(ring_moved(left[-1], -1))
-    far_a = ring_moved(right[3][:CUT], 1)
-    far_b = ring_moved(left[3][CUT:], -1)
-    pieces = [*right, left[3], left[2], left[1], far_a, far_b]
+        ours.append(ring_moved(ours[-1]))
+        others.append(ring_moved(others[-1]))
+    far = ring_moved(ours[3])
+    pieces = [ours[1], others[1], ours[2], others[2], ours[3], others[3], ours[0], far]
     packed = pl.pallas_call(
         pack_kernel,
         out_shape=jax.ShapeDtypeStruct((2 * w_query.shape[0], E), BF),
@@ -233,18 +229,9 @@
         out_specs=pl.BlockSpec(memory_space=pltpu.VMEM),
     )(w_query, w_key, w_value, w_out)
     whole = lax.all_gather(packed, "pb", axis=0, tiled=False)
-    part = w_query.shape[0]
-    w_k = whole[:, :part, HD:].reshape(E, HD)
-    w_v = whole[:, part : part + part // 2]
-    w_v = jnp.concatenate([w_v[:, :, :HD], w_v[:, :, HD:]], axis=1).reshape(E, HD)
-    acts = group_acts.reshape(GROUPS * CT, E)
-    keyed = jnp.dot(acts, w_k, preferred_element_type=F32).astype(BF)
-    valued = jnp.dot(acts, w_v, preferred_element_type=F32).astype(BF)
-    tick = right[1][:8, :128]
-    owner, local, pair, keys, tick = lax.optimization_barrier((owner, local, pair, keys, tick))
-    code, own = marks_of(owner, local, zl)
+    code, own = marks_of(owner, local, zh, zl)
     partner = pair[SLAB_ROWS : SLAB_ROWS + 2, :PAIRS].astype(jnp.int32)
-    _, other = marks_of(partner[0], partner[1], zl)
+    _, other = marks_of(partner[0], partner[1], zh, zl)
     place = (code >> 7) * (PLANE * SLOTS) + (code & 127)
     place = place.reshape(2, GROUPS).T.reshape(GROUPS, 2, 1) + lax.iota(jnp.int32, NT) * 128
     place = place.reshape(PAIRS * NT, 1)
@@ -256,14 +243,13 @@
     asked = lax.all_to_all(sent, FLAT, split_axis=0, concat_axis=0, tiled=True)
     wanted = asked[:, GROUPS : GROUPS + 2, :SLOTS].astype(jnp.int32)
     wanted = jnp.where(zl == 0, jnp.stack([wanted[:, 0], wanted[:, 1]]), jnp.stack([wanted[:, 1], wanted[:, 0]]))
-    away = jnp.bitwise_and(zh - lax.iota(jnp.int32, SLOTS) // 2 + RING, RING - 1)
-    wanted = jnp.where(wanted > 0, away * ROWS + wanted - 1, -1).reshape(SERVERS * SLOTS, 1)
-    wanted, keyed, valued = lax.optimization_barrier((wanted, keyed, valued))
+    block = lax.iota(jnp.int32, SLOTS) // 2
+    wanted = jnp.where(wanted > 0, block * ROWS + wanted - 1, -1).reshape(SERVERS * SLOTS, 1)
     parity = jnp.full((1, 1, 128), zl, jnp.int32)
     served = pl.pallas_call(
         serve_kernel,
         out_shape=jax.ShapeDtypeStruct((SERVERS, SLOTS, WIDE), BF),
-        in_specs=vmem(4 + RING + 1),
+        in_specs=vmem(3 + RING),
         out_specs=pl.BlockSpec(memory_space=pltpu.HBM),
         scratch_shapes=[
             pltpu.VMEM((RING * ROWS, E), BF),
@@ -272,23 +258,32 @@
             pltpu.SemaphoreType.DMA((4,)),
         ],
         compiler_params=pltpu.CompilerParams(vmem_limit_bytes=SERVE_LIMIT),
-    )(parity, tick, wanted, asked, *pieces)
+    )(parity, wanted, asked, *pieces)
+    served, whole = lax.optimization_barrier((served, whole))
     got = lax.all_to_all(served, NEAR, split_axis=0, concat_axis=0, tiled=True)
+    keyed, valued, w_q, w_o = pl.pallas_call(
+        project_kernel,
+        out_shape=(
+            jax.ShapeDtypeStruct((GROUPS * CT, HD), BF),
+            jax.ShapeDtypeStruct((GROUPS * CT, HD), BF),
+            jax.ShapeDtypeStruct((E, HD), BF),
+            jax.ShapeDtypeStruct((HD, E), BF),
+        ),
+        in_specs=vmem(2),
+        out_specs=tuple(vmem(4)),
+        scratch_shapes=[pltpu.VMEM((E, HD), BF), pltpu.VMEM((E, HD), BF)],
+        compiler_params=pltpu.CompilerParams(vmem_limit_bytes=LIMIT),
+    )(group_acts.reshape(GROUPS * CT, E), whole)
     best, encoded = pl.pallas_call(
         layer_kernel,
         out_shape=(
             jax.ShapeDtypeStruct((2, GROUPS), F32),
             jax.ShapeDtypeStruct((GROUPS, 2, NT, E), BF),
         ),
-        in_specs=[*vmem(4), pl.BlockSpec(memory_space=pltpu.HBM), *vmem(1)],
+        in_specs=vmem(7),
         out_specs=tuple(vmem(2)),
-        scratch_shapes=[
-            pltpu.VMEM((E, 2 * HD), BF),
-            pltpu.VMEM((HD, E), BF),
-            pltpu.SemaphoreType.DMA((8,)),
-        ],
         compiler_params=pltpu.CompilerParams(vmem_limit_bytes=LIMIT),
-    )(place, got, keyed, valued, whole, norm_gain.reshape(1, E))
+    )(place, got, keyed, valued, w_q, w_o, norm_gain.reshape(1, E))
     return best.T, encoded
 
 

time: 156 us -> 139 us (0.89)
  waiting for transfers between devices: 60.5 us -> 37.7 us
  starting transfers between devices: 55.5 us -> 62.9 us
  Pallas kernels: 13.9 us -> 12.1 us
  local copies, waits for them, and re-layouts: 8.49 us -> 10.1 us
    ppermute x8, waiting for transfers between devices: 31.5 us -> 13.5 us  [the longest x7 13.5 us: ring_moved(): return lax.ppermute(piece, ('zh', 'core'), pairs)]
    unnamed x15 -> x23, local copies, waits for them, and re-layouts: 0.06 us -> 6.15 us
    all_to_all x1, waiting for transfers between devices: 27.6 us -> 23 us  [per_device(): got = lax.all_to_all(served, NEAR, split_axis=0, concat_axis=0, tiled=True)]
    slice x5 -> x0, local copies, waits for them, and re-layouts: 3.77 us -> none  [the longest x1 1.63 us: per_device(): w_k = whole[:, :part, HD:].reshape(E, HD)]
    all_to_all x1, starting transfers between devices: 8 us -> 11 us  [per_device(): got = lax.all_to_all(served, NEAR, split_axis=0, concat_axis=0, tiled=True)]
    pallas_call x1, Pallas kernels: 6.47 us -> 3.88 us  [per_device(): pl.pallas_call(layer_kernel, out_shape=(jax.ShapeDtypeStruct((2, GROUPS),...]
    ppermute x8, starting transfers between devices: 36.1 us -> 38.5 us  [the longest x7 30.1 us: ring_moved(): return lax.ppermute(piece, ('zh', 'core'), pairs)]
    all_to_all x1, starting transfers between devices: 7.56 us -> 9.45 us  [per_device(): asked = lax.all_to_all(sent, FLAT, split_axis=0, concat_axis=0, tiled=True)]
  transfers between devices with their start and end apart: 12 -> 12, of which waited for: 7 -> 8; matrix products, arithmetic and copies ran while one was open for 6% -> 3% of each run, Pallas kernels for 0% -> 4%
where the time goes in v4:
time: 139 us; the launch traced here: 138 us
  starting transfers between devices  62.9 us (45%)
  waiting for transfers between devices  37.7 us (27%)
  between operations  14.4 us (10%)
  Pallas kernels  12.1 us (9%)
  local copies, waits for them, and re-layouts  10.1 us (7%)
    ppermute x7, starting transfers between devices, ring_moved(): return lax.ppermute(piece, ('zh', 'core'), pairs)  30.1 us
    all_to_all x1, waiting for transfers between devices, per_device(): got = lax.all_to_all(served, NEAR, split_axis=0, concat_axis=0, tiled=True)  23 us
    ppermute x7, waiting for transfers between devices, ring_moved(): return lax.ppermute(piece, ('zh', 'core'), pairs)  13.5 us
    all_to_all x1, starting transfers between devices, per_device(): got = lax.all_to_all(served, NEAR, split_axis=0, concat_axis=0, tiled=True)  11 us
    all_to_all x1, starting transfers between devices, per_device(): asked = lax.all_to_all(sent, FLAT, split_axis=0, concat_axis=0, tiled=True)  9.45 us
    ppermute x1, starting transfers between devices, per_device(): others = [lax.ppermute(piece, 'core', [(0, 1), (1, 0)])]  8.44 us
    unnamed x23, local copies, waits for them, and re-layouts  6.15 us
    pallas_call x1, Pallas kernels, per_device(): pl.pallas_call(serve_kernel, out_shape=jax.ShapeDtypeStruct((SERVERS, SLO...  5.06 us
  transfers between devices with their start and end apart: 12, of which 8 were waited for; matrix products, arithmetic and copies ran while one was open for 3% of the time, Pallas kernels for 4%

profile of v4, /device:TPU:6, one launch (start us, length us, event | category | flops | bytes accessed | tf_op | source)
XLA Modules:
  0.0 138.0 jit_solution(12195544410212073521)
XLA Ops:
  7.2 0.0 copy-start
  7.2 0.0 copy-start.10
  7.2 0.0 copy-start.8
  7.2 0.0 all-gather.3.cloned.1.call-start
  7.2 2.4 %shard_map.114 = bf16[448,896]{1,0:T(8,128)(2,1)} custom-call(bf16[224,448]{1,0:T(8,128)(2,1)} %w_query.1, bf16[224,448]{1,0:T(8,128)(2,1)} %w_key.1, bf16[224,448]{1,0:T(8,128)(2,1)} %w_value.1, bf16[112,896]{1,0:T(8,128)(2,1)} %w_out.1), custom_call_target="tpu_custom_call" | custom-call | tf_op jit(solution)/shard_map/pallas_call | solution.py:225
  9.6 0.0 all-gather.3.cloned.1.call-update
  9.6 0.0 copy-done.10
  9.7 0.1 reshape.215
  9.8 0.8 dynamic-slice_convert_fusion
  10.6 3.8 %collective-permute-start = (bf16[32,384]{1,0:T(8,128)(2,1)S(1)}, bf16[32,384]{1,0:T(8,128)(2,1)S(1)}, u32[]{:S(2)}, u32[]{:S(2)}) collective-permute-start(bf16[32,384]{1,0:T(8,128)(2,1)S(1)} %pad_maximum_fusion.1), channel_id=1, source_target_pairs={{0,8},{8,0},{1,9},{9,1},{2,10},{10,2},{3,11},{11,3},{4,12},{12,4},... | collective-permute-start | bytes 73736 | tf_op jit(solution)/shard_map/ppermute | solution.py:213
  14.4 0.1 reshape.214
  14.5 0.2 select_reduce_fusion.3
  14.7 0.0 copy-done
  14.7 0.4 constant_dynamic-slice_fusion
  15.1 0.0 copy-done.8
  15.1 1.1 collective-permute-done
  16.3 0.2 select_reduce_fusion.1
  16.5 0.1 select_reduce_fusion.2
  16.6 0.1 convert_element_type.49
  16.7 0.1 convert_element_type.53
  16.9 1.0 broadcast_in_dim.62
  17.8 9.4 %all-to-all-start = ((bf16[32,32,384]{2,1,0:T(8,128)(2,1)}), bf16[32,32,384]{2,1,0:T(8,128)(2,1)S(1)}, u32[]{:S(2)}, u32[]{:S(2)}) async-start(bf16[32,32,384]{2,1,0:T(8,128)(2,1)} %bitcast.6), calls=%async_computation | async-start | bytes 1572864 | tf_op jit(solution)/shard_map/all_to_all | solution.py:243
  27.3 3.3 %collective-permute-start.1 = (bf16[120,896]{1,0:T(8,128)(2,1)S(1)}, bf16[120,896]{1,0:T(8,128)(2,1)S(1)}, u32[]{:S(2)}, u32[]{:S(2)}) collective-permute-start(bf16[120,896]{1,0:T(8,128)(2,1)S(1)} %pad_maximum_fusion.refs_6_), channel_id=1, source_target_pairs={{0,16},{4,116},{16,32},{20,4},{32,48},{36,20},{48,64},{52,36},{64,... | collective-permute-start | bytes 645128 | tf_op jit(solution)/shard_map/ppermute | solution.py:158
  30.6 8.4 %collective-permute-start.2 = (bf16[120,896]{1,0:T(8,128)(2,1)S(1)}, bf16[120,896]{1,0:T(8,128)(2,1)S(1)}, u32[]{:S(2)}, u32[]{:S(2)}) collective-permute-start(bf16[120,896]{1,0:T(8,128)(2,1)S(1)} %pad_maximum_fusion.refs_6_), channel_id=1, source_target_pairs={{0,4},{4,0},{1,5},{5,1},{2,6},{6,2},{3,7},{7,3},{8,12},{12,8},{9,1... | collective-permute-start | bytes 645128 | tf_op jit(solution)/shard_map/ppermute | solution.py:219
  39.1 2.6 %collective-permute-done.1.refs_0_ = bf16[120,896]{1,0:T(8,128)(2,1)S(1)} collective-permute-done((bf16[120,896]{1,0:T(8,128)(2,1)S(1)}, bf16[120,896]{1,0:T(8,128)(2,1)S(1)}, u32[]{:S(2)}, u32[]{:S(2)}) %collective-permute-start.1) | collective-permute-done | bytes 215072 | tf_op jit(solution)/shard_map/ppermute | solution.py:158
  41.7 1.9 %collective-permute-start.4 = (bf16[120,896]{1,0:T(8,128)(2,1)S(1)}, bf16[120,896]{1,0:T(8,128)(2,1)S(1)}, u32[]{:S(2)}, u32[]{:S(2)}) collective-permute-start(bf16[120,896]{1,0:T(8,128)(2,1)S(1)} %collective-permute-done.1.refs_0_), channel_id=1, source_target_pairs={{0,16},{4,116},{16,32},{20,4},{32,48},{36,20},{48,64},{52,36},{64,... | collective-permute-start | bytes 645128 | tf_op jit(solution)/shard_map/ppermute | solution.py:158
  43.6 0.0 collective-permute-done.2
  43.7 5.6 %collective-permute-start.3 = (bf16[120,896]{1,0:T(8,128)(2,1)S(1)}, bf16[120,896]{1,0:T(8,128)(2,1)S(1)}, u32[]{:S(2)}, u32[]{:S(2)}) collective-permute-start(bf16[120,896]{1,0:T(8,128)(2,1)S(1)} %collective-permute-done.2), channel_id=1, source_target_pairs={{0,16},{4,116},{16,32},{20,4},{32,48},{36,20},{48,64},{52,36},{64,... | collective-permute-start | bytes 645128 | tf_op jit(solution)/shard_map/ppermute | solution.py:158
  49.2 2.5 %collective-permute-done.4.refs_2_ = bf16[120,896]{1,0:T(8,128)(2,1)S(1)} collective-permute-done((bf16[120,896]{1,0:T(8,128)(2,1)S(1)}, bf16[120,896]{1,0:T(8,128)(2,1)S(1)}, u32[]{:S(2)}, u32[]{:S(2)}) %collective-permute-start.4) | collective-permute-done | bytes 215072 | tf_op jit(solution)/shard_map/ppermute | solution.py:158
  51.7 3.2 %collective-permute-start.6 = (bf16[120,896]{1,0:T(8,128)(2,1)S(1)}, bf16[120,896]{1,0:T(8,128)(2,1)S(1)}, u32[]{:S(2)}, u32[]{:S(2)}) collective-permute-start(bf16[120,896]{1,0:T(8,128)(2,1)S(1)} %collective-permute-done.4.refs_2_), channel_id=1, source_target_pairs={{0,16},{4,116},{16,32},{20,4},{32,48},{36,20},{48,64},{52,36},{64,... | collective-permute-start | bytes 645128 | tf_op jit(solution)/shard_map/ppermute | solution.py:158
  54.9 0.0 collective-permute-done.3.refs_1_
  54.9 6.5 %collective-permute-start.5 = (bf16[120,896]{1,0:T(8,128)(2,1)S(1)}, bf16[120,896]{1,0:T(8,128)(2,1)S(1)}, u32[]{:S(2)}, u32[]{:S(2)}) collective-permute-start(bf16[120,896]{1,0:T(8,128)(2,1)S(1)} %collective-permute-done.3.refs_1_), channel_id=1, source_target_pairs={{0,16},{4,116},{16,32},{20,4},{32,48},{36,20},{48,64},{52,36},{64,... | collective-permute-start | bytes 645128 | tf_op jit(solution)/shard_map/ppermute | solution.py:158
  61.4 1.7 %collective-permute-done.6.refs_4_ = bf16[120,896]{1,0:T(8,128)(2,1)S(1)} collective-permute-done((bf16[120,896]{1,0:T(8,128)(2,1)S(1)}, bf16[120,896]{1,0:T(8,128)(2,1)S(1)}, u32[]{:S(2)}, u32[]{:S(2)}) %collective-permute-start.6) | collective-permute-done | bytes 215072 | tf_op jit(solution)/shard_map/ppermute | solution.py:158
  63.1 4.4 %collective-permute-start.8 = (bf16[120,896]{1,0:T(8,128)(2,1)S(1)}, bf16[120,896]{1,0:T(8,128)(2,1)S(1)}, u32[]{:S(2)}, u32[]{:S(2)}) collective-permute-start(bf16[120,896]{1,0:T(8,128)(2,1)S(1)} %collective-permute-done.6.refs_4_), channel_id=1, source_target_pairs={{0,16},{4,116},{16,32},{20,4},{32,48},{36,20},{48,64},{52,36},{64,... | collective-permute-start | bytes 645128 | tf_op jit(solution)/shard_map/ppermute | solution.py:158
  67.5 1.9 %collective-permute-done.5.refs_3_ = bf16[120,896]{1,0:T(8,128)(2,1)S(1)} collective-permute-done((bf16[120,896]{1,0:T(8,128)(2,1)S(1)}, bf16[120,896]{1,0:T(8,128)(2,1)S(1)}, u32[]{:S(2)}, u32[]{:S(2)}) %collective-permute-start.5) | collective-permute-done | bytes 215072 | tf_op jit(solution)/shard_map/ppermute | solution.py:158
  69.4 5.2 %collective-permute-start.7 = (bf16[120,896]{1,0:T(8,128)(2,1)S(1)}, bf16[120,896]{1,0:T(8,128)(2,1)S(1)}, u32[]{:S(2)}, u32[]{:S(2)}) collective-permute-start(bf16[120,896]{1,0:T(8,128)(2,1)S(1)} %collective-permute-done.5.refs_3_), channel_id=1, source_target_pairs={{0,16},{4,116},{16,32},{20,4},{32,48},{36,20},{48,64},{52,36},{64,... | collective-permute-start | bytes 645128 | tf_op jit(solution)/shard_map/ppermute | solution.py:158
  74.7 0.0 all-to-all-done.keys
  74.7 0.0 copy-start.6
  74.8 1.1 select_n.123.code
  75.9 0.2 collective-permute-done.8.refs_7_
  76.0 4.7 %collective-permute-done.7.refs_5_ = bf16[120,896]{1,0:T(8,128)(2,1)S(1)} collective-permute-done((bf16[120,896]{1,0:T(8,128)(2,1)S(1)}, bf16[120,896]{1,0:T(8,128)(2,1)S(1)}, u32[]{:S(2)}, u32[]{:S(2)}) %collective-permute-start.7) | collective-permute-done | bytes 215072 | tf_op jit(solution)/shard_map/ppermute | solution.py:158
  80.7 0.0 copy-done.6
  80.7 5.1 %shard_map.113 = bf16[64,16,1024]{2,1,0:T(8,128)(2,1)} custom-call(s32[1,1,128]{2,1,0:T(1,128)S(1)} %broadcast_in_dim.57.parity, s32[1024,1]{1,0:T(8,128)} %select_n.123.code, bf16[32,32,384]{2,1,0:T(8,128)(2,1)} %copy-done.6, bf16[120,896]{1,0:T(8,128)(2,1)S(1)} %collective-permute-done.1.refs_0_, bf16[120,896]{1,0:T(8,128)(2,1)S(1)} %collective-permute-done.3.refs_1_, ...), custom_call_target="tpu_custom_call" | custom-call | tf_op jit(solution)/shard_map/pallas_call | solution.py:249
  85.8 0.0 all-gather.3.cloned.1.call-done
  85.8 0.0 copy-start.7
  85.8 0.0 copy-start.9
  85.8 11.0 %all-to-all-start.1 = ((bf16[64,16,1024]{2,1,0:T(8,128)(2,1)}), bf16[64,16,1024]{2,1,0:T(8,128)(2,1)S(1)}, u32[]{:S(2)}, u32[]{:S(2)}) async-start(bf16[64,16,1024]{2,1,0:T(8,128)(2,1)} %shard_map.113), calls=%async_computation.1 | async-start | bytes 4194304 | tf_op jit(solution)/shard_map/all_to_all | solution.py:263
  96.9 0.1 reduce_max.23
  96.9 0.0 copy-done.7
  97.0 0.1 copy.22
  97.1 0.1 broadcast_add_fusion
  97.2 0.1 add.211.place
  97.3 0.0 copy-done.9
  97.3 0.0 copy-start.1
  97.4 1.9 %copy-done.1 = bf16[1792,896]{1,0:T(8,128)(2,1)S(1)} copy-done((bf16[1792,896]{1,0:T(8,128)(2,1)S(1)}, bf16[1792,896]{1,0:T(8,128)(2,1)}, u32[]{:S(2)}) %copy-start.1) | copy-done | bytes 3211288
  99.3 0.8 shard_map.115
  100.0 0.0 copy-start.2
  100.0 0.9 copy-done.2
  101.0 0.0 copy-start.4
  101.0 0.9 copy-done.4
  101.9 23.0 %all-to-all-done.1.got = bf16[64,16,1024]{2,1,0:T(8,128)(2,1)S(1)} async-done(((bf16[64,16,1024]{2,1,0:T(8,128)(2,1)}), bf16[64,16,1024]{2,1,0:T(8,128)(2,1)S(1)}, u32[]{:S(2)}, u32[]{:S(2)}) %all-to-all-start.1) | async-done | bytes 2097184 | tf_op jit(solution)/shard_map/all_to_all | solution.py:263
  124.9 1.2 copy-done.3
  126.1 1.1 copy-done.5
  127.2 3.9 %shard_map.116 = (f32[2,26]{1,0:T(2,128)}, bf16[26,2,4,896]{3,2,1,0:T(4,128)(2,1)}) custom-call(s32[208,1]{1,0:T(8,128)S(1)} %add.211.place, bf16[64,16,1024]{2,1,0:T(8,128)(2,1)S(1)} %all-to-all-done.1.got, bf16[104,448]{1,0:T(8,128)(2,1)S(1)} %get-tuple-element.12.keyed, bf16[104,448]{1,0:T(8,128)(2,1)S(1)} %get-tuple-element.13.valued, ...), custom_call_target="tpu_custom_call" | custom-call | tf_op jit(solution)/shard_map/pallas_call | solution.py:277
  (31 shorter events, 0.4 us)
Async XLA Ops:
  7.2 7.5 %copy-start = (bf16[96,4,896]{2,1,0:T(4,128)(2,1)S(1)}, bf16[96,4,896]{2,1,0:T(4,128)(2,1)}, u32[]{:S(2)}) copy-start(bf16[96,4,896]{2,1,0:T(4,128)(2,1)} %param.14) | copy-start | bytes 2064388
  7.2 2.5 %copy-start.10 = (s32[26,2]{0,1:T(2,128)S(1)}, s32[26,2]{0,1:T(2,128)}, u32[]{:S(2)}) copy-start(s32[26,2]{0,1:T(2,128)} %param.12) | copy-start | bytes 628
  7.2 7.9 %copy-start.8 = (f32[26,384]{1,0:T(8,128)S(1)}, f32[26,384]{1,0:T(8,128)}, u32[]{:S(2)}) copy-start(f32[26,384]{1,0:T(8,128)} %param.10) | copy-start | bytes 119812
  7.2 78.6 %all-gather.3.cloned.1.call-start = ((), (), s32[]{:S(2)}) async-start(), calls=%async_computation.2 | async-start | bytes 4014080 | tf_op jit(solution)/shard_map/all_gather | solution.py:231
  10.6 5.7 %collective-permute-start = (bf16[32,384]{1,0:T(8,128)(2,1)S(1)}, bf16[32,384]{1,0:T(8,128)(2,1)S(1)}, u32[]{:S(2)}, u32[]{:S(2)}) collective-permute-start(bf16[32,384]{1,0:T(8,128)(2,1)S(1)} %pad_maximum_fusion.1), channel_id=1, source_target_pairs={{0,8},{8,0},{1,9},{9,1},{2,10},{10,2},{3,11},{11,3},{4,12},{12,4},... | collective-permute-start | bytes 73736 | tf_op jit(solution)/shard_map/ppermute | solution.py:213
  17.8 56.8 %all-to-all-start = ((bf16[32,32,384]{2,1,0:T(8,128)(2,1)}), bf16[32,32,384]{2,1,0:T(8,128)(2,1)S(1)}, u32[]{:S(2)}, u32[]{:S(2)}) async-start(bf16[32,32,384]{2,1,0:T(8,128)(2,1)} %bitcast.6), calls=%async_computation | async-start | bytes 1572864 | tf_op jit(solution)/shard_map/all_to_all | solution.py:243
  27.3 14.4 %collective-permute-start.1 = (bf16[120,896]{1,0:T(8,128)(2,1)S(1)}, bf16[120,896]{1,0:T(8,128)(2,1)S(1)}, u32[]{:S(2)}, u32[]{:S(2)}) collective-permute-start(bf16[120,896]{1,0:T(8,128)(2,1)S(1)} %pad_maximum_fusion.refs_6_), channel_id=1, source_target_pairs={{0,16},{4,116},{16,32},{20,4},{32,48},{36,20},{48,64},{52,36},{64,... | collective-permute-start | bytes 645128 | tf_op jit(solution)/shard_map/ppermute | solution.py:158
  30.6 13.0 %collective-permute-start.2 = (bf16[120,896]{1,0:T(8,128)(2,1)S(1)}, bf16[120,896]{1,0:T(8,128)(2,1)S(1)}, u32[]{:S(2)}, u32[]{:S(2)}) collective-permute-start(bf16[120,896]{1,0:T(8,128)(2,1)S(1)} %pad_maximum_fusion.refs_6_), channel_id=1, source_target_pairs={{0,4},{4,0},{1,5},{5,1},{2,6},{6,2},{3,7},{7,3},{8,12},{12,8},{9,1... | collective-permute-start | bytes 645128 | tf_op jit(solution)/shard_map/ppermute | solution.py:219
  41.7 10.0 %collective-permute-start.4 = (bf16[120,896]{1,0:T(8,128)(2,1)S(1)}, bf16[120,896]{1,0:T(8,128)(2,1)S(1)}, u32[]{:S(2)}, u32[]{:S(2)}) collective-permute-start(bf16[120,896]{1,0:T(8,128)(2,1)S(1)} %collective-permute-done.1.refs_0_), channel_id=1, source_target_pairs={{0,16},{4,116},{16,32},{20,4},{32,48},{36,20},{48,64},{52,36},{64,... | collective-permute-start | bytes 645128 | tf_op jit(solution)/shard_map/ppermute | solution.py:158
  43.7 11.3 %collective-permute-start.3 = (bf16[120,896]{1,0:T(8,128)(2,1)S(1)}, bf16[120,896]{1,0:T(8,128)(2,1)S(1)}, u32[]{:S(2)}, u32[]{:S(2)}) collective-permute-start(bf16[120,896]{1,0:T(8,128)(2,1)S(1)} %collective-permute-done.2), channel_id=1, source_target_pairs={{0,16},{4,116},{16,32},{20,4},{32,48},{36,20},{48,64},{52,36},{64,... | collective-permute-start | bytes 645128 | tf_op jit(solution)/shard_map/ppermute | solution.py:158
  51.7 11.4 %collective-permute-start.6 = (bf16[120,896]{1,0:T(8,128)(2,1)S(1)}, bf16[120,896]{1,0:T(8,128)(2,1)S(1)}, u32[]{:S(2)}, u32[]{:S(2)}) collective-permute-start(bf16[120,896]{1,0:T(8,128)(2,1)S(1)} %collective-permute-done.4.refs_2_), channel_id=1, source_target_pairs={{0,16},{4,116},{16,32},{20,4},{32,48},{36,20},{48,64},{52,36},{64,... | collective-permute-start | bytes 645128 | tf_op jit(solution)/shard_map/ppermute | solution.py:158
  54.9 14.5 %collective-permute-start.5 = (bf16[120,896]{1,0:T(8,128)(2,1)S(1)}, bf16[120,896]{1,0:T(8,128)(2,1)S(1)}, u32[]{:S(2)}, u32[]{:S(2)}) collective-permute-start(bf16[120,896]{1,0:T(8,128)(2,1)S(1)} %collective-permute-done.3.refs_1_), channel_id=1, source_target_pairs={{0,16},{4,116},{16,32},{20,4},{32,48},{36,20},{48,64},{52,36},{64,... | collective-permute-start | bytes 645128 | tf_op jit(solution)/shard_map/ppermute | solution.py:158
  63.1 12.9 %collective-permute-start.8 = (bf16[120,896]{1,0:T(8,128)(2,1)S(1)}, bf16[120,896]{1,0:T(8,128)(2,1)S(1)}, u32[]{:S(2)}, u32[]{:S(2)}) collective-permute-start(bf16[120,896]{1,0:T(8,128)(2,1)S(1)} %collective-permute-done.6.refs_4_), channel_id=1, source_target_pairs={{0,16},{4,116},{16,32},{20,4},{32,48},{36,20},{48,64},{52,36},{64,... | collective-permute-start | bytes 645128 | tf_op jit(solution)/shard_map/ppermute | solution.py:158
  69.4 11.3 %collective-permute-start.7 = (bf16[120,896]{1,0:T(8,128)(2,1)S(1)}, bf16[120,896]{1,0:T(8,128)(2,1)S(1)}, u32[]{:S(2)}, u32[]{:S(2)}) collective-permute-start(bf16[120,896]{1,0:T(8,128)(2,1)S(1)} %collective-permute-done.5.refs_3_), channel_id=1, source_target_pairs={{0,16},{4,116},{16,32},{20,4},{32,48},{36,20},{48,64},{52,36},{64,... | collective-permute-start | bytes 645128 | tf_op jit(solution)/shard_map/ppermute | solution.py:158
  74.7 6.0 %copy-start.6 = (bf16[32,32,384]{2,1,0:T(8,128)(2,1)}, bf16[32,32,384]{2,1,0:T(8,128)(2,1)S(1)}, u32[]{:S(2)}) copy-start(bf16[32,32,384]{2,1,0:T(8,128)(2,1)S(1)} %all-to-all-done.keys) | copy-start | bytes 2359300
  85.8 11.1 %copy-start.7 = (bf16[26,4,896]{2,1,0:T(4,128)(2,1)S(1)}, bf16[26,4,896]{2,1,0:T(4,128)(2,1)}, u32[]{:S(2)}) copy-start(bf16[26,4,896]{2,1,0:T(4,128)(2,1)} %param.13) | copy-start | bytes 559108
  85.8 11.5 %copy-start.9 = (f32[896]{0:T(1024)S(1)}, f32[896]{0:T(1024)}, u32[]{:S(2)}) copy-start(f32[896]{0:T(1024)} %param.15) | copy-start | bytes 10756
  85.8 39.1 %all-to-all-start.1 = ((bf16[64,16,1024]{2,1,0:T(8,128)(2,1)}), bf16[64,16,1024]{2,1,0:T(8,128)(2,1)S(1)}, u32[]{:S(2)}, u32[]{:S(2)}) async-start(bf16[64,16,1024]{2,1,0:T(8,128)(2,1)} %shard_map.113), calls=%async_computation.1 | async-start | bytes 4194304 | tf_op jit(solution)/shard_map/all_to_all | solution.py:263
  97.3 1.9 %copy-start.1 = (bf16[1792,896]{1,0:T(8,128)(2,1)S(1)}, bf16[1792,896]{1,0:T(8,128)(2,1)}, u32[]{:S(2)}) copy-start(bf16[1792,896]{1,0:T(8,128)(2,1)} %all-gather.3.cloned.1.call-done) | copy-start | bytes 9633796
  100.0 0.9 copy-start.2
  101.0 0.9 copy-start.4
  124.9 1.2 copy-start.3
  126.1 1.1 copy-start.5
Sparse Core Ops, SparseCore 0:
  10.1 55.6 all-gather.2

commit v5 on v4

--- a/solution.py
+++ b/solution.py
@@ -25,6 +25,7 @@
 KEYPAD = 32
 WIDE = E + 128
 LIMIT = 24 * 2**20
+LAYER_LIMIT = 50 * 2**20
 SERVE_LIMIT = 52 * 2**20
 LOW = -1.0e38
 SPLIT = ("x", "zh", "zl", "core", "pb")
@@ -210,7 +211,14 @@
     quarter = lax.dynamic_slice_in_dim(slab, y * SLAB_ROWS, SLAB_ROWS, 0).astype(BF)
     numbers = jnp.pad(jnp.stack([owner, local]).astype(BF), ((0, KEYPAD - SLAB_ROWS - 2), (0, KEY - PAIRS)))
     pair = jnp.concatenate([quarter, numbers], axis=0)
+    pair, w_query, w_key, w_value, w_out = lax.optimization_barrier((pair, w_query, w_key, w_value, w_out))
     pair = lax.ppermute(pair, "zl", [(0, 1), (1, 0)])
+    packed = pl.pallas_call(
+        pack_kernel,
+        out_shape=jax.ShapeDtypeStruct((2 * w_query.shape[0], E), BF),
+        in_specs=vmem(4),
+        out_specs=pl.BlockSpec(memory_space=pltpu.VMEM),
+    )(w_query, w_key, w_value, w_out)
     token = lax.dynamic_index_in_dim(table, y, axis=1, keepdims=False)
     both = jnp.concatenate([quarter, pair[:SLAB_ROWS]], axis=1)
     both = jnp.pad(both, ((0, 0), (0, E - 2 * KEY)))
@@ -222,12 +230,6 @@
         others.append(ring_moved(others[-1]))
     far = ring_moved(ours[3])
     pieces = [ours[1], others[1], ours[2], others[2], ours[3], others[3], ours[0], far]
-    packed = pl.pallas_call(
-        pack_kernel,
-        out_shape=jax.ShapeDtypeStruct((2 * w_query.shape[0], E), BF),
-        in_specs=vmem(4),
-        out_specs=pl.BlockSpec(memory_space=pltpu.VMEM),
-    )(w_query, w_key, w_value, w_out)
     whole = lax.all_gather(packed, "pb", axis=0, tiled=False)
     code, own = marks_of(owner, local, zh, zl)
     partner = pair[SLAB_ROWS : SLAB_ROWS + 2, :PAIRS].astype(jnp.int32)
@@ -282,7 +284,7 @@
         ),
         in_specs=vmem(7),
         out_specs=tuple(vmem(2)),
-        compiler_params=pltpu.CompilerParams(vmem_limit_bytes=LIMIT),
+        compiler_params=pltpu.CompilerParams(vmem_limit_bytes=LAYER_LIMIT),
     )(place, got, keyed, valued, w_q, w_o, norm_gain.reshape(1, E))
     return best.T, encoded
 

time: 139 us -> 139 us (level)
  local copies, waits for them, and re-layouts: 10.1 us -> 6.65 us
  waiting for transfers between devices: 37.7 us -> 39.5 us
  Pallas kernels: 12.1 us -> 13.7 us
    unnamed x23 -> x15, local copies, waits for them, and re-layouts: 6.15 us -> 1.96 us
    all_to_all x1, waiting for transfers between devices: 23 us -> 24.8 us  [per_device(): got = lax.all_to_all(served, NEAR, split_axis=0, concat_axis=0, tiled=True)]
    pallas_call x1, Pallas kernels: 3.88 us -> 5.51 us  [per_device(): pl.pallas_call(layer_kernel, out_shape=(jax.ShapeDtypeStruct((2, GROUPS),...]
where the time goes in v5:
time: 139 us; the launch traced here: 138 us
  starting transfers between devices  63.1 us (45%)
  waiting for transfers between devices  39.5 us (28%)
  between operations  14.4 us (10%)
  Pallas kernels  13.7 us (10%)
  local copies, waits for them, and re-layouts  6.65 us (5%)
    ppermute x7, starting transfers between devices, ring_moved(): return lax.ppermute(piece, ('zh', 'core'), pairs)  30.1 us
    all_to_all x1, waiting for transfers between devices, per_device(): got = lax.all_to_all(served, NEAR, split_axis=0, concat_axis=0, tiled=True)  24.8 us
    ppermute x7, waiting for transfers between devices, ring_moved(): return lax.ppermute(piece, ('zh', 'core'), pairs)  13.5 us
    all_to_all x1, starting transfers between devices, per_device(): got = lax.all_to_all(served, NEAR, split_axis=0, concat_axis=0, tiled=True)  11.2 us
    all_to_all x1, starting transfers between devices, per_device(): asked = lax.all_to_all(sent, FLAT, split_axis=0, concat_axis=0, tiled=True)  9.45 us
    ppermute x1, starting transfers between devices, per_device(): others = [lax.ppermute(piece, 'core', [(0, 1), (1, 0)])]  8.44 us
    pallas_call x1, Pallas kernels, per_device(): pl.pallas_call(layer_kernel, out_shape=(jax.ShapeDtypeStruct((2, GROUPS),...  5.51 us
    pallas_call x1, Pallas kernels, per_device(): pl.pallas_call(serve_kernel, out_shape=jax.ShapeDtypeStruct((SERVERS, SLO...  5.05 us
  transfers between devices with their start and end apart: 12, of which 8 were waited for; matrix products, arithmetic and copies ran while one was open for 3% of the time, Pallas kernels for 4%

profile of v5, /device:TPU:6, one launch (start us, length us, event | category | flops | bytes accessed | tf_op | source)
XLA Modules:
  0.0 138.1 jit_solution(3974794928493543596)
XLA Ops:
  7.2 0.0 copy-start
  7.2 0.0 copy-start.6
  7.2 0.0 copy-start.4
  7.2 0.0 all-gather.3.cloned.1.call-start
  7.3 0.8 reshape.215
  8.1 0.8 dynamic-slice_convert_fusion
  8.9 2.3 %shard_map.114 = bf16[448,896]{1,0:T(8,128)(2,1)} custom-call(bf16[224,448]{1,0:T(8,128)(2,1)} %w_query, bf16[224,448]{1,0:T(8,128)(2,1)} %w_key, bf16[224,448]{1,0:T(8,128)(2,1)} %w_value, bf16[112,896]{1,0:T(8,128)(2,1)} %w_out), custom_call_target="tpu_custom_call" | custom-call | tf_op jit(solution)/shard_map/pallas_call | solution.py:216
  11.2 0.0 all-gather.3.cloned.1.call-update
  11.2 3.8 %collective-permute-start = (bf16[32,384]{1,0:T(8,128)(2,1)S(1)}, bf16[32,384]{1,0:T(8,128)(2,1)S(1)}, u32[]{:S(2)}, u32[]{:S(2)}) collective-permute-start(bf16[32,384]{1,0:T(8,128)(2,1)S(1)} %pad_maximum_fusion.1), channel_id=1, source_target_pairs={{0,8},{8,0},{1,9},{9,1},{2,10},{10,2},{3,11},{11,3},{4,12},{12,4},... | collective-permute-start | bytes 73736 | tf_op jit(solution)/shard_map/ppermute | solution.py:215
  15.1 0.0 copy-done.6
  15.1 0.1 reshape.214
  15.2 0.2 select_reduce_fusion.3
  15.4 0.0 copy-done
  15.4 0.4 constant_dynamic-slice_fusion
  15.8 0.0 copy-done.4
  15.8 1.1 collective-permute-done
  17.0 0.2 select_reduce_fusion.1
  17.2 0.1 select_reduce_fusion.2
  17.3 0.1 convert_element_type.49
  17.4 0.1 convert_element_type.53
  17.6 1.0 broadcast_in_dim.62
  18.5 9.4 %all-to-all-start = ((bf16[32,32,384]{2,1,0:T(8,128)(2,1)}), bf16[32,32,384]{2,1,0:T(8,128)(2,1)S(1)}, u32[]{:S(2)}, u32[]{:S(2)}) async-start(bf16[32,32,384]{2,1,0:T(8,128)(2,1)} %bitcast.6), calls=%async_computation | async-start | bytes 1572864 | tf_op jit(solution)/shard_map/all_to_all | solution.py:245
  28.1 3.3 %collective-permute-start.1 = (bf16[120,896]{1,0:T(8,128)(2,1)S(1)}, bf16[120,896]{1,0:T(8,128)(2,1)S(1)}, u32[]{:S(2)}, u32[]{:S(2)}) collective-permute-start(bf16[120,896]{1,0:T(8,128)(2,1)S(1)} %pad_maximum_fusion.refs_6_), channel_id=1, source_target_pairs={{0,16},{4,116},{16,32},{20,4},{32,48},{36,20},{48,64},{52,36},{64,... | collective-permute-start | bytes 645128 | tf_op jit(solution)/shard_map/ppermute | solution.py:159
  31.4 8.4 %collective-permute-start.2 = (bf16[120,896]{1,0:T(8,128)(2,1)S(1)}, bf16[120,896]{1,0:T(8,128)(2,1)S(1)}, u32[]{:S(2)}, u32[]{:S(2)}) collective-permute-start(bf16[120,896]{1,0:T(8,128)(2,1)S(1)} %pad_maximum_fusion.refs_6_), channel_id=1, source_target_pairs={{0,4},{4,0},{1,5},{5,1},{2,6},{6,2},{3,7},{7,3},{8,12},{12,8},{9,1... | collective-permute-start | bytes 645128 | tf_op jit(solution)/shard_map/ppermute | solution.py:227
  39.8 2.6 %collective-permute-done.1.refs_0_ = bf16[120,896]{1,0:T(8,128)(2,1)S(1)} collective-permute-done((bf16[120,896]{1,0:T(8,128)(2,1)S(1)}, bf16[120,896]{1,0:T(8,128)(2,1)S(1)}, u32[]{:S(2)}, u32[]{:S(2)}) %collective-permute-start.1) | collective-permute-done | bytes 215072 | tf_op jit(solution)/shard_map/ppermute | solution.py:159
  42.4 1.9 %collective-permute-start.4 = (bf16[120,896]{1,0:T(8,128)(2,1)S(1)}, bf16[120,896]{1,0:T(8,128)(2,1)S(1)}, u32[]{:S(2)}, u32[]{:S(2)}) collective-permute-start(bf16[120,896]{1,0:T(8,128)(2,1)S(1)} %collective-permute-done.1.refs_0_), channel_id=1, source_target_pairs={{0,16},{4,116},{16,32},{20,4},{32,48},{36,20},{48,64},{52,36},{64,... | collective-permute-start | bytes 645128 | tf_op jit(solution)/shard_map/ppermute | solution.py:159
  44.4 0.0 collective-permute-done.2
  44.4 5.6 %collective-permute-start.3 = (bf16[120,896]{1,0:T(8,128)(2,1)S(1)}, bf16[120,896]{1,0:T(8,128)(2,1)S(1)}, u32[]{:S(2)}, u32[]{:S(2)}) collective-permute-start(bf16[120,896]{1,0:T(8,128)(2,1)S(1)} %collective-permute-done.2), channel_id=1, source_target_pairs={{0,16},{4,116},{16,32},{20,4},{32,48},{36,20},{48,64},{52,36},{64,... | collective-permute-start | bytes 645128 | tf_op jit(solution)/shard_map/ppermute | solution.py:159
  49.9 2.5 %collective-permute-done.4.refs_2_ = bf16[120,896]{1,0:T(8,128)(2,1)S(1)} collective-permute-done((bf16[120,896]{1,0:T(8,128)(2,1)S(1)}, bf16[120,896]{1,0:T(8,128)(2,1)S(1)}, u32[]{:S(2)}, u32[]{:S(2)}) %collective-permute-start.4) | collective-permute-done | bytes 215072 | tf_op jit(solution)/shard_map/ppermute | solution.py:159
  52.4 3.2 %collective-permute-start.6 = (bf16[120,896]{1,0:T(8,128)(2,1)S(1)}, bf16[120,896]{1,0:T(8,128)(2,1)S(1)}, u32[]{:S(2)}, u32[]{:S(2)}) collective-permute-start(bf16[120,896]{1,0:T(8,128)(2,1)S(1)} %collective-permute-done.4.refs_2_), channel_id=1, source_target_pairs={{0,16},{4,116},{16,32},{20,4},{32,48},{36,20},{48,64},{52,36},{64,... | collective-permute-start | bytes 645128 | tf_op jit(solution)/shard_map/ppermute | solution.py:159
  55.6 0.0 collective-permute-done.3.refs_1_
  55.6 6.5 %collective-permute-start.5 = (bf16[120,896]{1,0:T(8,128)(2,1)S(1)}, bf16[120,896]{1,0:T(8,128)(2,1)S(1)}, u32[]{:S(2)}, u32[]{:S(2)}) collective-permute-start(bf16[120,896]{1,0:T(8,128)(2,1)S(1)} %collective-permute-done.3.refs_1_), channel_id=1, source_target_pairs={{0,16},{4,116},{16,32},{20,4},{32,48},{36,20},{48,64},{52,36},{64,... | collective-permute-start | bytes 645128 | tf_op jit(solution)/shard_map/ppermute | solution.py:159
  62.1 1.7 %collective-permute-done.6.refs_4_ = bf16[120,896]{1,0:T(8,128)(2,1)S(1)} collective-permute-done((bf16[120,896]{1,0:T(8,128)(2,1)S(1)}, bf16[120,896]{1,0:T(8,128)(2,1)S(1)}, u32[]{:S(2)}, u32[]{:S(2)}) %collective-permute-start.6) | collective-permute-done | bytes 215072 | tf_op jit(solution)/shard_map/ppermute | solution.py:159
  63.9 4.4 %collective-permute-start.8 = (bf16[120,896]{1,0:T(8,128)(2,1)S(1)}, bf16[120,896]{1,0:T(8,128)(2,1)S(1)}, u32[]{:S(2)}, u32[]{:S(2)}) collective-permute-start(bf16[120,896]{1,0:T(8,128)(2,1)S(1)} %collective-permute-done.6.refs_4_), channel_id=1, source_target_pairs={{0,16},{4,116},{16,32},{20,4},{32,48},{36,20},{48,64},{52,36},{64,... | collective-permute-start | bytes 645128 | tf_op jit(solution)/shard_map/ppermute | solution.py:159
  68.3 1.9 %collective-permute-done.5.refs_3_ = bf16[120,896]{1,0:T(8,128)(2,1)S(1)} collective-permute-done((bf16[120,896]{1,0:T(8,128)(2,1)S(1)}, bf16[120,896]{1,0:T(8,128)(2,1)S(1)}, u32[]{:S(2)}, u32[]{:S(2)}) %collective-permute-start.5) | collective-permute-done | bytes 215072 | tf_op jit(solution)/shard_map/ppermute | solution.py:159
  70.1 5.2 %collective-permute-start.7 = (bf16[120,896]{1,0:T(8,128)(2,1)S(1)}, bf16[120,896]{1,0:T(8,128)(2,1)S(1)}, u32[]{:S(2)}, u32[]{:S(2)}) collective-permute-start(bf16[120,896]{1,0:T(8,128)(2,1)S(1)} %collective-permute-done.5.refs_3_), channel_id=1, source_target_pairs={{0,16},{4,116},{16,32},{20,4},{32,48},{36,20},{48,64},{52,36},{64,... | collective-permute-start | bytes 645128 | tf_op jit(solution)/shard_map/ppermute | solution.py:159
  75.4 0.0 all-to-all-done.keys
  75.4 0.0 copy-start.2
  75.5 1.1 select_n.123.code
  76.6 0.2 collective-permute-done.8.refs_7_
  76.8 4.7 %collective-permute-done.7.refs_5_ = bf16[120,896]{1,0:T(8,128)(2,1)S(1)} collective-permute-done((bf16[120,896]{1,0:T(8,128)(2,1)S(1)}, bf16[120,896]{1,0:T(8,128)(2,1)S(1)}, u32[]{:S(2)}, u32[]{:S(2)}) %collective-permute-start.7) | collective-permute-done | bytes 215072 | tf_op jit(solution)/shard_map/ppermute | solution.py:159
  81.4 0.0 copy-done.2
  81.4 5.0 %shard_map.113 = bf16[64,16,1024]{2,1,0:T(8,128)(2,1)} custom-call(s32[1,1,128]{2,1,0:T(1,128)S(1)} %broadcast_in_dim.57.parity, s32[1024,1]{1,0:T(8,128)} %select_n.123.code, bf16[32,32,384]{2,1,0:T(8,128)(2,1)} %copy-done.2, bf16[120,896]{1,0:T(8,128)(2,1)S(1)} %collective-permute-done.1.refs_0_, bf16[120,896]{1,0:T(8,128)(2,1)S(1)} %collective-permute-done.3.refs_1_, ...), custom_call_target="tpu_custom_call" | custom-call | tf_op jit(solution)/shard_map/pallas_call | solution.py:251
  86.5 0.0 all-gather.3.cloned.1.call-done
  86.5 0.0 copy-start.3
  86.5 0.0 copy-start.5
  86.5 11.2 %all-to-all-start.1 = ((bf16[64,16,1024]{2,1,0:T(8,128)(2,1)}), bf16[64,16,1024]{2,1,0:T(8,128)(2,1)}, u32[]{:S(2)}, u32[]{:S(2)}) async-start(bf16[64,16,1024]{2,1,0:T(8,128)(2,1)} %shard_map.113), calls=%async_computation.1 | async-start | bytes 4194304 | tf_op jit(solution)/shard_map/all_to_all | solution.py:265
  97.8 0.1 reduce_max.23
  97.8 0.0 copy-done.3
  97.9 0.1 copy.22
  98.0 0.1 broadcast_add_fusion
  98.1 0.1 add.211.place
  98.2 0.0 copy-done.5
  98.2 0.0 copy-start.1
  98.2 1.9 %copy-done.1 = bf16[1792,896]{1,0:T(8,128)(2,1)S(1)} copy-done((bf16[1792,896]{1,0:T(8,128)(2,1)S(1)}, bf16[1792,896]{1,0:T(8,128)(2,1)}, u32[]{:S(2)}) %copy-start.1) | copy-done | bytes 3211288
  100.1 0.8 shard_map.115
  100.9 24.8 %all-to-all-done.1.got = bf16[64,16,1024]{2,1,0:T(8,128)(2,1)} async-done(((bf16[64,16,1024]{2,1,0:T(8,128)(2,1)}), bf16[64,16,1024]{2,1,0:T(8,128)(2,1)}, u32[]{:S(2)}, u32[]{:S(2)}) %all-to-all-start.1) | async-done | bytes 2097184 | tf_op jit(solution)/shard_map/all_to_all | solution.py:265
  125.7 5.5 %shard_map.116 = (f32[2,26]{1,0:T(2,128)}, bf16[26,2,4,896]{3,2,1,0:T(4,128)(2,1)}) custom-call(s32[208,1]{1,0:T(8,128)S(1)} %add.211.place, bf16[64,16,1024]{2,1,0:T(8,128)(2,1)} %all-to-all-done.1.got, bf16[104,448]{1,0:T(8,128)(2,1)S(1)} %get-tuple-element.22.keyed, bf16[104,448]{1,0:T(8,128)(2,1)S(1)} %get-tuple-element.23.valued, ...), custom_call_target="tpu_custom_call" | custom-call | tf_op jit(solution)/shard_map/pallas_call | solution.py:279
  (29 shorter events, 0.4 us)
Async XLA Ops:
  7.2 8.2 %copy-start = (bf16[96,4,896]{2,1,0:T(4,128)(2,1)S(1)}, bf16[96,4,896]{2,1,0:T(4,128)(2,1)}, u32[]{:S(2)}) copy-start(bf16[96,4,896]{2,1,0:T(4,128)(2,1)} %param.14) | copy-start | bytes 2064388
  7.2 7.9 %copy-start.6 = (s32[26,2]{0,1:T(2,128)S(1)}, s32[26,2]{0,1:T(2,128)}, u32[]{:S(2)}) copy-start(s32[26,2]{0,1:T(2,128)} %param.12) | copy-start | bytes 628
  7.2 8.6 %copy-start.4 = (f32[26,384]{1,0:T(8,128)S(1)}, f32[26,384]{1,0:T(8,128)}, u32[]{:S(2)}) copy-start(f32[26,384]{1,0:T(8,128)} %param.10) | copy-start | bytes 119812
  7.2 79.3 %all-gather.3.cloned.1.call-start = ((), (), s32[]{:S(2)}) async-start(), calls=%async_computation.2 | async-start | bytes 4014080 | tf_op jit(solution)/shard_map/all_gather | solution.py:233
  11.2 5.7 %collective-permute-start = (bf16[32,384]{1,0:T(8,128)(2,1)S(1)}, bf16[32,384]{1,0:T(8,128)(2,1)S(1)}, u32[]{:S(2)}, u32[]{:S(2)}) collective-permute-start(bf16[32,384]{1,0:T(8,128)(2,1)S(1)} %pad_maximum_fusion.1), channel_id=1, source_target_pairs={{0,8},{8,0},{1,9},{9,1},{2,10},{10,2},{3,11},{11,3},{4,12},{12,4},... | collective-permute-start | bytes 73736 | tf_op jit(solution)/shard_map/ppermute | solution.py:215
  18.5 56.8 %all-to-all-start = ((bf16[32,32,384]{2,1,0:T(8,128)(2,1)}), bf16[32,32,384]{2,1,0:T(8,128)(2,1)S(1)}, u32[]{:S(2)}, u32[]{:S(2)}) async-start(bf16[32,32,384]{2,1,0:T(8,128)(2,1)} %bitcast.6), calls=%async_computation | async-start | bytes 1572864 | tf_op jit(solution)/shard_map/all_to_all | solution.py:245
  28.1 14.4 %collective-permute-start.1 = (bf16[120,896]{1,0:T(8,128)(2,1)S(1)}, bf16[120,896]{1,0:T(8,128)(2,1)S(1)}, u32[]{:S(2)}, u32[]{:S(2)}) collective-permute-start(bf16[120,896]{1,0:T(8,128)(2,1)S(1)} %pad_maximum_fusion.refs_6_), channel_id=1, source_target_pairs={{0,16},{4,116},{16,32},{20,4},{32,48},{36,20},{48,64},{52,36},{64,... | collective-permute-start | bytes 645128 | tf_op jit(solution)/shard_map/ppermute | solution.py:159
  31.4 13.0 %collective-permute-start.2 = (bf16[120,896]{1,0:T(8,128)(2,1)S(1)}, bf16[120,896]{1,0:T(8,128)(2,1)S(1)}, u32[]{:S(2)}, u32[]{:S(2)}) collective-permute-start(bf16[120,896]{1,0:T(8,128)(2,1)S(1)} %pad_maximum_fusion.refs_6_), channel_id=1, source_target_pairs={{0,4},{4,0},{1,5},{5,1},{2,6},{6,2},{3,7},{7,3},{8,12},{12,8},{9,1... | collective-permute-start | bytes 645128 | tf_op jit(solution)/shard_map/ppermute | solution.py:227
  42.4 10.0 %collective-permute-start.4 = (bf16[120,896]{1,0:T(8,128)(2,1)S(1)}, bf16[120,896]{1,0:T(8,128)(2,1)S(1)}, u32[]{:S(2)}, u32[]{:S(2)}) collective-permute-start(bf16[120,896]{1,0:T(8,128)(2,1)S(1)} %collective-permute-done.1.refs_0_), channel_id=1, source_target_pairs={{0,16},{4,116},{16,32},{20,4},{32,48},{36,20},{48,64},{52,36},{64,... | collective-permute-start | bytes 645128 | tf_op jit(solution)/shard_map/ppermute | solution.py:159
  44.4 11.3 %collective-permute-start.3 = (bf16[120,896]{1,0:T(8,128)(2,1)S(1)}, bf16[120,896]{1,0:T(8,128)(2,1)S(1)}, u32[]{:S(2)}, u32[]{:S(2)}) collective-permute-start(bf16[120,896]{1,0:T(8,128)(2,1)S(1)} %collective-permute-done.2), channel_id=1, source_target_pairs={{0,16},{4,116},{16,32},{20,4},{32,48},{36,20},{48,64},{52,36},{64,... | collective-permute-start | bytes 645128 | tf_op jit(solution)/shard_map/ppermute | solution.py:159
  52.4 11.4 %collective-permute-start.6 = (bf16[120,896]{1,0:T(8,128)(2,1)S(1)}, bf16[120,896]{1,0:T(8,128)(2,1)S(1)}, u32[]{:S(2)}, u32[]{:S(2)}) collective-permute-start(bf16[120,896]{1,0:T(8,128)(2,1)S(1)} %collective-permute-done.4.refs_2_), channel_id=1, source_target_pairs={{0,16},{4,116},{16,32},{20,4},{32,48},{36,20},{48,64},{52,36},{64,... | collective-permute-start | bytes 645128 | tf_op jit(solution)/shard_map/ppermute | solution.py:159
  55.6 14.5 %collective-permute-start.5 = (bf16[120,896]{1,0:T(8,128)(2,1)S(1)}, bf16[120,896]{1,0:T(8,128)(2,1)S(1)}, u32[]{:S(2)}, u32[]{:S(2)}) collective-permute-start(bf16[120,896]{1,0:T(8,128)(2,1)S(1)} %collective-permute-done.3.refs_1_), channel_id=1, source_target_pairs={{0,16},{4,116},{16,32},{20,4},{32,48},{36,20},{48,64},{52,36},{64,... | collective-permute-start | bytes 645128 | tf_op jit(solution)/shard_map/ppermute | solution.py:159
  63.9 12.9 %collective-permute-start.8 = (bf16[120,896]{1,0:T(8,128)(2,1)S(1)}, bf16[120,896]{1,0:T(8,128)(2,1)S(1)}, u32[]{:S(2)}, u32[]{:S(2)}) collective-permute-start(bf16[120,896]{1,0:T(8,128)(2,1)S(1)} %collective-permute-done.6.refs_4_), channel_id=1, source_target_pairs={{0,16},{4,116},{16,32},{20,4},{32,48},{36,20},{48,64},{52,36},{64,... | collective-permute-start | bytes 645128 | tf_op jit(solution)/shard_map/ppermute | solution.py:159
  70.1 11.3 %collective-permute-start.7 = (bf16[120,896]{1,0:T(8,128)(2,1)S(1)}, bf16[120,896]{1,0:T(8,128)(2,1)S(1)}, u32[]{:S(2)}, u32[]{:S(2)}) collective-permute-start(bf16[120,896]{1,0:T(8,128)(2,1)S(1)} %collective-permute-done.5.refs_3_), channel_id=1, source_target_pairs={{0,16},{4,116},{16,32},{20,4},{32,48},{36,20},{48,64},{52,36},{64,... | collective-permute-start | bytes 645128 | tf_op jit(solution)/shard_map/ppermute | solution.py:159
  75.4 6.0 %copy-start.2 = (bf16[32,32,384]{2,1,0:T(8,128)(2,1)}, bf16[32,32,384]{2,1,0:T(8,128)(2,1)S(1)}, u32[]{:S(2)}) copy-start(bf16[32,32,384]{2,1,0:T(8,128)(2,1)S(1)} %all-to-all-done.keys) | copy-start | bytes 2359300
  86.5 11.3 %copy-start.3 = (bf16[26,4,896]{2,1,0:T(4,128)(2,1)S(1)}, bf16[26,4,896]{2,1,0:T(4,128)(2,1)}, u32[]{:S(2)}) copy-start(bf16[26,4,896]{2,1,0:T(4,128)(2,1)} %param.13) | copy-start | bytes 559108
  86.5 11.7 %copy-start.5 = (f32[896]{0:T(1024)S(1)}, f32[896]{0:T(1024)}, u32[]{:S(2)}) copy-start(f32[896]{0:T(1024)} %param.15) | copy-start | bytes 10756
  86.5 39.2 %all-to-all-start.1 = ((bf16[64,16,1024]{2,1,0:T(8,128)(2,1)}), bf16[64,16,1024]{2,1,0:T(8,128)(2,1)}, u32[]{:S(2)}, u32[]{:S(2)}) async-start(bf16[64,16,1024]{2,1,0:T(8,128)(2,1)} %shard_map.113), calls=%async_computation.1 | async-start | bytes 4194304 | tf_op jit(solution)/shard_map/all_to_all | solution.py:265
  98.2 1.9 %copy-start.1 = (bf16[1792,896]{1,0:T(8,128)(2,1)S(1)}, bf16[1792,896]{1,0:T(8,128)(2,1)}, u32[]{:S(2)}) copy-start(bf16[1792,896]{1,0:T(8,128)(2,1)} %all-gather.3.cloned.1.call-done) | copy-start | bytes 9633796
Sparse Core Ops, SparseCore 0:
  11.4 55.1 all-gather.2

commit v6 on v5

--- a/solution.py
+++ b/solution.py
@@ -151,11 +151,11 @@
     return [pl.BlockSpec(memory_space=pltpu.VMEM)] * count
 
 
-def ring_moved(piece):
+def ring_moved(piece, crossed=0):
     pairs = []
     for at in range(RING):
-        pairs.append((2 * at, 2 * ((at + 1) % RING)))
-        pairs.append((2 * at + 1, 2 * ((at - 1) % RING) + 1))
+        pairs.append((2 * at + crossed, 2 * ((at + 1) % RING)))
+        pairs.append((2 * at + 1 - crossed, 2 * ((at - 1) % RING) + 1))
     return lax.ppermute(piece, ("zh", "core"), pairs)
 
 
@@ -224,10 +224,10 @@
     both = jnp.pad(both, ((0, 0), (0, E - 2 * KEY)))
     piece = jnp.concatenate([token, both], axis=0)
     ours = [piece]
-    others = [lax.ppermute(piece, "core", [(0, 1), (1, 0)])]
-    for _ in range(3):
+    others = [piece]
+    for k in range(3):
         ours.append(ring_moved(ours[-1]))
-        others.append(ring_moved(others[-1]))
+        others.append(ring_moved(others[-1], crossed=1 if k == 0 else 0))
     far = ring_moved(ours[3])
     pieces = [ours[1], others[1], ours[2], others[2], ours[3], others[3], ours[0], far]
     whole = lax.all_gather(packed, "pb", axis=0, tiled=False)

time: 139 us -> 135 us (0.971)
  starting transfers between devices: 63.1 us -> 53.7 us
  waiting for transfers between devices: 39.5 us -> 44.7 us
    ppermute x1 -> x0, starting transfers between devices: 8.44 us -> none  [per_device(): others = [lax.ppermute(piece, 'core', [(0, 1), (1, 0)])]]
    ppermute x7, waiting for transfers between devices: 13.5 us -> 18.8 us  [ring_moved(): return lax.ppermute(piece, ('zh', 'core'), pairs)]
  transfers between devices with their start and end apart: 12 -> 11, of which waited for: 8 -> 8; matrix products, arithmetic and copies ran while one was open for 3% -> 3% of each run, Pallas kernels for 4% -> 4%
where the time goes in v6:
time: 135 us; the launch traced here: 134 us
  starting transfers between devices  53.7 us (40%)
  waiting for transfers between devices  44.7 us (33%)
  between operations  14.4 us (11%)
  Pallas kernels  13.6 us (10%)
  local copies, waits for them, and re-layouts  6.64 us (5%)
    ppermute x7, starting transfers between devices, ring_moved(): return lax.ppermute(piece, ('zh', 'core'), pairs)  28.9 us
    all_to_all x1, waiting for transfers between devices, per_device(): got = lax.all_to_all(served, NEAR, split_axis=0, concat_axis=0, tiled=True)  24.8 us
    ppermute x7, waiting for transfers between devices, ring_moved(): return lax.ppermute(piece, ('zh', 'core'), pairs)  18.8 us
    all_to_all x1, starting transfers between devices, per_device(): got = lax.all_to_all(served, NEAR, split_axis=0, concat_axis=0, tiled=True)  11.5 us
    all_to_all x1, starting transfers between devices, per_device(): asked = lax.all_to_all(sent, FLAT, split_axis=0, concat_axis=0, tiled=True)  9.45 us
    pallas_call x1, Pallas kernels, per_device(): pl.pallas_call(layer_kernel, out_shape=(jax.ShapeDtypeStruct((2, GROUPS),...  5.51 us
    pallas_call x1, Pallas kernels, per_device(): pl.pallas_call(serve_kernel, out_shape=jax.ShapeDtypeStruct((SERVERS, SLO...  5.03 us
    ppermute x1, starting transfers between devices, per_device(): pair = lax.ppermute(pair, 'zl', [(0, 1), (1, 0)])  3.83 us
  transfers between devices with their start and end apart: 11, of which 8 were waited for; matrix products, arithmetic and copies ran while one was open for 3% of the time, Pallas kernels for 4%

profile of v6, /device:TPU:6, one launch (start us, length us, event | category | flops | bytes accessed | tf_op | source)
XLA Modules:
  0.0 133.9 jit_solution(9039342078864985338)
XLA Ops:
  7.2 0.0 copy-start
  7.2 0.0 copy-start.6
  7.2 0.0 copy-start.4
  7.2 0.0 all-gather.3.cloned.1.call-start
  7.3 0.8 reshape.215
  8.1 0.8 dynamic-slice_convert_fusion
  8.9 2.3 %shard_map.114 = bf16[448,896]{1,0:T(8,128)(2,1)} custom-call(bf16[224,448]{1,0:T(8,128)(2,1)} %w_query, bf16[224,448]{1,0:T(8,128)(2,1)} %w_key, bf16[224,448]{1,0:T(8,128)(2,1)} %w_value, bf16[112,896]{1,0:T(8,128)(2,1)} %w_out), custom_call_target="tpu_custom_call" | custom-call | tf_op jit(solution)/shard_map/pallas_call | solution.py:216
  11.2 0.0 all-gather.3.cloned.1.call-update
  11.2 3.8 %collective-permute-start = (bf16[32,384]{1,0:T(8,128)(2,1)S(1)}, bf16[32,384]{1,0:T(8,128)(2,1)S(1)}, u32[]{:S(2)}, u32[]{:S(2)}) collective-permute-start(bf16[32,384]{1,0:T(8,128)(2,1)S(1)} %pad_maximum_fusion.1), channel_id=1, source_target_pairs={{0,8},{8,0},{1,9},{9,1},{2,10},{10,2},{3,11},{11,3},{4,12},{12,4},... | collective-permute-start | bytes 73736 | tf_op jit(solution)/shard_map/ppermute | solution.py:215
  15.1 0.0 copy-done.6
  15.1 0.1 reshape.214
  15.2 0.2 select_reduce_fusion.3
  15.4 0.0 copy-done
  15.4 0.4 constant_dynamic-slice_fusion
  15.8 0.0 copy-done.4
  15.8 1.1 collective-permute-done
  17.0 0.2 select_reduce_fusion.1
  17.2 0.1 select_reduce_fusion.2
  17.3 0.1 convert_element_type.49
  17.4 0.1 convert_element_type.53
  17.5 1.0 broadcast_in_dim.62
  18.5 9.4 %all-to-all-start = ((bf16[32,32,384]{2,1,0:T(8,128)(2,1)}), bf16[32,32,384]{2,1,0:T(8,128)(2,1)S(1)}, u32[]{:S(2)}, u32[]{:S(2)}) async-start(bf16[32,32,384]{2,1,0:T(8,128)(2,1)} %bitcast.6), calls=%async_computation | async-start | bytes 1572864 | tf_op jit(solution)/shard_map/all_to_all | solution.py:245
  28.0 3.3 %collective-permute-start.1 = (bf16[120,896]{1,0:T(8,128)(2,1)S(1)}, bf16[120,896]{1,0:T(8,128)(2,1)S(1)}, u32[]{:S(2)}, u32[]{:S(2)}) collective-permute-start(bf16[120,896]{1,0:T(8,128)(2,1)S(1)} %pad_maximum_fusion.refs_6_), channel_id=1, source_target_pairs={{0,16},{4,116},{16,32},{20,4},{32,48},{36,20},{48,64},{52,36},{64,... | collective-permute-start | bytes 645128 | tf_op jit(solution)/shard_map/ppermute | solution.py:159
  31.3 9.5 %collective-permute-start.2 = (bf16[120,896]{1,0:T(8,128)(2,1)S(1)}, bf16[120,896]{1,0:T(8,128)(2,1)S(1)}, u32[]{:S(2)}, u32[]{:S(2)}) collective-permute-start(bf16[120,896]{1,0:T(8,128)(2,1)S(1)} %pad_maximum_fusion.refs_6_), channel_id=1, source_target_pairs={{4,16},{0,116},{20,32},{16,4},{36,48},{32,20},{52,64},{48,36},{68,... | collective-permute-start | bytes 645128 | tf_op jit(solution)/shard_map/ppermute | solution.py:159
  40.8 1.9 %collective-permute-done.1.refs_0_ = bf16[120,896]{1,0:T(8,128)(2,1)S(1)} collective-permute-done((bf16[120,896]{1,0:T(8,128)(2,1)S(1)}, bf16[120,896]{1,0:T(8,128)(2,1)S(1)}, u32[]{:S(2)}, u32[]{:S(2)}) %collective-permute-start.1) | collective-permute-done | bytes 215072 | tf_op jit(solution)/shard_map/ppermute | solution.py:159
  42.7 1.9 %collective-permute-start.3 = (bf16[120,896]{1,0:T(8,128)(2,1)S(1)}, bf16[120,896]{1,0:T(8,128)(2,1)S(1)}, u32[]{:S(2)}, u32[]{:S(2)}) collective-permute-start(bf16[120,896]{1,0:T(8,128)(2,1)S(1)} %collective-permute-done.1.refs_0_), channel_id=1, source_target_pairs={{0,16},{4,116},{16,32},{20,4},{32,48},{36,20},{48,64},{52,36},{64,... | collective-permute-start | bytes 645128 | tf_op jit(solution)/shard_map/ppermute | solution.py:159
  44.6 2.8 %collective-permute-done.2.refs_1_ = bf16[120,896]{1,0:T(8,128)(2,1)S(1)} collective-permute-done((bf16[120,896]{1,0:T(8,128)(2,1)S(1)}, bf16[120,896]{1,0:T(8,128)(2,1)S(1)}, u32[]{:S(2)}, u32[]{:S(2)}) %collective-permute-start.2) | collective-permute-done | bytes 215072 | tf_op jit(solution)/shard_map/ppermute | solution.py:159
  47.5 4.2 %collective-permute-start.4 = (bf16[120,896]{1,0:T(8,128)(2,1)S(1)}, bf16[120,896]{1,0:T(8,128)(2,1)S(1)}, u32[]{:S(2)}, u32[]{:S(2)}) collective-permute-start(bf16[120,896]{1,0:T(8,128)(2,1)S(1)} %collective-permute-done.2.refs_1_), channel_id=1, source_target_pairs={{0,16},{4,116},{16,32},{20,4},{32,48},{36,20},{48,64},{52,36},{64,... | collective-permute-start | bytes 645128 | tf_op jit(solution)/shard_map/ppermute | solution.py:159
  51.6 1.3 collective-permute-done.3.refs_2_
  52.9 2.1 %collective-permute-start.5 = (bf16[120,896]{1,0:T(8,128)(2,1)S(1)}, bf16[120,896]{1,0:T(8,128)(2,1)S(1)}, u32[]{:S(2)}, u32[]{:S(2)}) collective-permute-start(bf16[120,896]{1,0:T(8,128)(2,1)S(1)} %collective-permute-done.3.refs_2_), channel_id=1, source_target_pairs={{0,16},{4,116},{16,32},{20,4},{32,48},{36,20},{48,64},{52,36},{64,... | collective-permute-start | bytes 645128 | tf_op jit(solution)/shard_map/ppermute | solution.py:159
  55.0 2.4 %collective-permute-done.4.refs_3_ = bf16[120,896]{1,0:T(8,128)(2,1)S(1)} collective-permute-done((bf16[120,896]{1,0:T(8,128)(2,1)S(1)}, bf16[120,896]{1,0:T(8,128)(2,1)S(1)}, u32[]{:S(2)}, u32[]{:S(2)}) %collective-permute-start.4) | collective-permute-done | bytes 215072 | tf_op jit(solution)/shard_map/ppermute | solution.py:159
  57.4 4.6 %collective-permute-start.6 = (bf16[120,896]{1,0:T(8,128)(2,1)S(1)}, bf16[120,896]{1,0:T(8,128)(2,1)S(1)}, u32[]{:S(2)}, u32[]{:S(2)}) collective-permute-start(bf16[120,896]{1,0:T(8,128)(2,1)S(1)} %collective-permute-done.4.refs_3_), channel_id=1, source_target_pairs={{0,16},{4,116},{16,32},{20,4},{32,48},{36,20},{48,64},{52,36},{64,... | collective-permute-start | bytes 645128 | tf_op jit(solution)/shard_map/ppermute | solution.py:159
  62.0 2.8 %collective-permute-done.5.refs_4_ = bf16[120,896]{1,0:T(8,128)(2,1)S(1)} collective-permute-done((bf16[120,896]{1,0:T(8,128)(2,1)S(1)}, bf16[120,896]{1,0:T(8,128)(2,1)S(1)}, u32[]{:S(2)}, u32[]{:S(2)}) %collective-permute-start.5) | collective-permute-done | bytes 215072 | tf_op jit(solution)/shard_map/ppermute | solution.py:159
  64.8 3.4 %collective-permute-start.7 = (bf16[120,896]{1,0:T(8,128)(2,1)S(1)}, bf16[120,896]{1,0:T(8,128)(2,1)S(1)}, u32[]{:S(2)}, u32[]{:S(2)}) collective-permute-start(bf16[120,896]{1,0:T(8,128)(2,1)S(1)} %collective-permute-done.5.refs_4_), channel_id=1, source_target_pairs={{0,16},{4,116},{16,32},{20,4},{32,48},{36,20},{48,64},{52,36},{64,... | collective-permute-start | bytes 645128 | tf_op jit(solution)/shard_map/ppermute | solution.py:159
  68.2 0.0 all-to-all-done.keys
  68.2 0.0 copy-start.2
  68.3 1.1 select_n.123.code
  69.4 0.0 collective-permute-done.6.refs_5_
  69.4 7.5 %collective-permute-done.7.refs_7_ = bf16[120,896]{1,0:T(8,128)(2,1)S(1)} collective-permute-done((bf16[120,896]{1,0:T(8,128)(2,1)S(1)}, bf16[120,896]{1,0:T(8,128)(2,1)S(1)}, u32[]{:S(2)}, u32[]{:S(2)}) %collective-permute-start.7) | collective-permute-done | bytes 215072 | tf_op jit(solution)/shard_map/ppermute | solution.py:159
  77.0 0.0 copy-done.2
  77.0 5.0 %shard_map.113 = bf16[64,16,1024]{2,1,0:T(8,128)(2,1)} custom-call(s32[1,1,128]{2,1,0:T(1,128)S(1)} %broadcast_in_dim.57.parity, s32[1024,1]{1,0:T(8,128)} %select_n.123.code, bf16[32,32,384]{2,1,0:T(8,128)(2,1)} %copy-done.2, bf16[120,896]{1,0:T(8,128)(2,1)S(1)} %collective-permute-done.1.refs_0_, bf16[120,896]{1,0:T(8,128)(2,1)S(1)} %collective-permute-done.2.refs_1_, ...), custom_call_target="tpu_custom_call" | custom-call | tf_op jit(solution)/shard_map/pallas_call | solution.py:251
  82.0 0.0 all-gather.3.cloned.1.call-done
  82.0 0.0 copy-start.3
  82.0 0.0 copy-start.5
  82.1 11.5 %all-to-all-start.1 = ((bf16[64,16,1024]{2,1,0:T(8,128)(2,1)}), bf16[64,16,1024]{2,1,0:T(8,128)(2,1)}, u32[]{:S(2)}, u32[]{:S(2)}) async-start(bf16[64,16,1024]{2,1,0:T(8,128)(2,1)} %shard_map.113), calls=%async_computation.1 | async-start | bytes 4194304 | tf_op jit(solution)/shard_map/all_to_all | solution.py:265
  93.6 0.1 reduce_max.23
  93.6 0.0 copy-done.3
  93.7 0.1 copy.22
  93.8 0.1 broadcast_add_fusion
  93.9 0.1 add.211.place
  94.0 0.0 copy-done.5
  94.0 0.0 copy-start.1
  94.1 1.9 %copy-done.1 = bf16[1792,896]{1,0:T(8,128)(2,1)S(1)} copy-done((bf16[1792,896]{1,0:T(8,128)(2,1)S(1)}, bf16[1792,896]{1,0:T(8,128)(2,1)}, u32[]{:S(2)}) %copy-start.1) | copy-done | bytes 3211288
  96.0 0.8 shard_map.115
  96.7 24.8 %all-to-all-done.1.got = bf16[64,16,1024]{2,1,0:T(8,128)(2,1)} async-done(((bf16[64,16,1024]{2,1,0:T(8,128)(2,1)}), bf16[64,16,1024]{2,1,0:T(8,128)(2,1)}, u32[]{:S(2)}, u32[]{:S(2)}) %all-to-all-start.1) | async-done | bytes 2097184 | tf_op jit(solution)/shard_map/all_to_all | solution.py:265
  121.5 5.5 %shard_map.116 = (f32[2,26]{1,0:T(2,128)}, bf16[26,2,4,896]{3,2,1,0:T(4,128)(2,1)}) custom-call(s32[208,1]{1,0:T(8,128)S(1)} %add.211.place, bf16[64,16,1024]{2,1,0:T(8,128)(2,1)} %all-to-all-done.1.got, bf16[104,448]{1,0:T(8,128)(2,1)S(1)} %get-tuple-element.22.keyed, bf16[104,448]{1,0:T(8,128)(2,1)S(1)} %get-tuple-element.23.valued, ...), custom_call_target="tpu_custom_call" | custom-call | tf_op jit(solution)/shard_map/pallas_call | solution.py:279
  (29 shorter events, 0.4 us)
Async XLA Ops:
  7.2 8.2 %copy-start = (bf16[96,4,896]{2,1,0:T(4,128)(2,1)S(1)}, bf16[96,4,896]{2,1,0:T(4,128)(2,1)}, u32[]{:S(2)}) copy-start(bf16[96,4,896]{2,1,0:T(4,128)(2,1)} %param.14) | copy-start | bytes 2064388
  7.2 7.9 %copy-start.6 = (s32[26,2]{0,1:T(2,128)S(1)}, s32[26,2]{0,1:T(2,128)}, u32[]{:S(2)}) copy-start(s32[26,2]{0,1:T(2,128)} %param.12) | copy-start | bytes 628
  7.2 8.6 %copy-start.4 = (f32[26,384]{1,0:T(8,128)S(1)}, f32[26,384]{1,0:T(8,128)}, u32[]{:S(2)}) copy-start(f32[26,384]{1,0:T(8,128)} %param.10) | copy-start | bytes 119812
  7.2 74.8 %all-gather.3.cloned.1.call-start = ((), (), s32[]{:S(2)}) async-start(), calls=%async_computation.2 | async-start | bytes 4014080 | tf_op jit(solution)/shard_map/all_gather | solution.py:233
  11.2 5.7 %collective-permute-start = (bf16[32,384]{1,0:T(8,128)(2,1)S(1)}, bf16[32,384]{1,0:T(8,128)(2,1)S(1)}, u32[]{:S(2)}, u32[]{:S(2)}) collective-permute-start(bf16[32,384]{1,0:T(8,128)(2,1)S(1)} %pad_maximum_fusion.1), channel_id=1, source_target_pairs={{0,8},{8,0},{1,9},{9,1},{2,10},{10,2},{3,11},{11,3},{4,12},{12,4},... | collective-permute-start | bytes 73736 | tf_op jit(solution)/shard_map/ppermute | solution.py:215
  18.5 49.7 %all-to-all-start = ((bf16[32,32,384]{2,1,0:T(8,128)(2,1)}), bf16[32,32,384]{2,1,0:T(8,128)(2,1)S(1)}, u32[]{:S(2)}, u32[]{:S(2)}) async-start(bf16[32,32,384]{2,1,0:T(8,128)(2,1)} %bitcast.6), calls=%async_computation | async-start | bytes 1572864 | tf_op jit(solution)/shard_map/all_to_all | solution.py:245
  28.0 14.7 %collective-permute-start.1 = (bf16[120,896]{1,0:T(8,128)(2,1)S(1)}, bf16[120,896]{1,0:T(8,128)(2,1)S(1)}, u32[]{:S(2)}, u32[]{:S(2)}) collective-permute-start(bf16[120,896]{1,0:T(8,128)(2,1)S(1)} %pad_maximum_fusion.refs_6_), channel_id=1, source_target_pairs={{0,16},{4,116},{16,32},{20,4},{32,48},{36,20},{48,64},{52,36},{64,... | collective-permute-start | bytes 645128 | tf_op jit(solution)/shard_map/ppermute | solution.py:159
  31.3 16.1 %collective-permute-start.2 = (bf16[120,896]{1,0:T(8,128)(2,1)S(1)}, bf16[120,896]{1,0:T(8,128)(2,1)S(1)}, u32[]{:S(2)}, u32[]{:S(2)}) collective-permute-start(bf16[120,896]{1,0:T(8,128)(2,1)S(1)} %pad_maximum_fusion.refs_6_), channel_id=1, source_target_pairs={{4,16},{0,116},{20,32},{16,4},{36,48},{32,20},{52,64},{48,36},{68,... | collective-permute-start | bytes 645128 | tf_op jit(solution)/shard_map/ppermute | solution.py:159
  42.7 10.3 %collective-permute-start.3 = (bf16[120,896]{1,0:T(8,128)(2,1)S(1)}, bf16[120,896]{1,0:T(8,128)(2,1)S(1)}, u32[]{:S(2)}, u32[]{:S(2)}) collective-permute-start(bf16[120,896]{1,0:T(8,128)(2,1)S(1)} %collective-permute-done.1.refs_0_), channel_id=1, source_target_pairs={{0,16},{4,116},{16,32},{20,4},{32,48},{36,20},{48,64},{52,36},{64,... | collective-permute-start | bytes 645128 | tf_op jit(solution)/shard_map/ppermute | solution.py:159
  47.5 10.0 %collective-permute-start.4 = (bf16[120,896]{1,0:T(8,128)(2,1)S(1)}, bf16[120,896]{1,0:T(8,128)(2,1)S(1)}, u32[]{:S(2)}, u32[]{:S(2)}) collective-permute-start(bf16[120,896]{1,0:T(8,128)(2,1)S(1)} %collective-permute-done.2.refs_1_), channel_id=1, source_target_pairs={{0,16},{4,116},{16,32},{20,4},{32,48},{36,20},{48,64},{52,36},{64,... | collective-permute-start | bytes 645128 | tf_op jit(solution)/shard_map/ppermute | solution.py:159
  52.9 11.8 %collective-permute-start.5 = (bf16[120,896]{1,0:T(8,128)(2,1)S(1)}, bf16[120,896]{1,0:T(8,128)(2,1)S(1)}, u32[]{:S(2)}, u32[]{:S(2)}) collective-permute-start(bf16[120,896]{1,0:T(8,128)(2,1)S(1)} %collective-permute-done.3.refs_2_), channel_id=1, source_target_pairs={{0,16},{4,116},{16,32},{20,4},{32,48},{36,20},{48,64},{52,36},{64,... | collective-permute-start | bytes 645128 | tf_op jit(solution)/shard_map/ppermute | solution.py:159
  57.4 12.0 %collective-permute-start.6 = (bf16[120,896]{1,0:T(8,128)(2,1)S(1)}, bf16[120,896]{1,0:T(8,128)(2,1)S(1)}, u32[]{:S(2)}, u32[]{:S(2)}) collective-permute-start(bf16[120,896]{1,0:T(8,128)(2,1)S(1)} %collective-permute-done.4.refs_3_), channel_id=1, source_target_pairs={{0,16},{4,116},{16,32},{20,4},{32,48},{36,20},{48,64},{52,36},{64,... | collective-permute-start | bytes 645128 | tf_op jit(solution)/shard_map/ppermute | solution.py:159
  64.8 12.2 %collective-permute-start.7 = (bf16[120,896]{1,0:T(8,128)(2,1)S(1)}, bf16[120,896]{1,0:T(8,128)(2,1)S(1)}, u32[]{:S(2)}, u32[]{:S(2)}) collective-permute-start(bf16[120,896]{1,0:T(8,128)(2,1)S(1)} %collective-permute-done.5.refs_4_), channel_id=1, source_target_pairs={{0,16},{4,116},{16,32},{20,4},{32,48},{36,20},{48,64},{52,36},{64,... | collective-permute-start | bytes 645128 | tf_op jit(solution)/shard_map/ppermute | solution.py:159
  68.2 8.8 %copy-start.2 = (bf16[32,32,384]{2,1,0:T(8,128)(2,1)}, bf16[32,32,384]{2,1,0:T(8,128)(2,1)S(1)}, u32[]{:S(2)}) copy-start(bf16[32,32,384]{2,1,0:T(8,128)(2,1)S(1)} %all-to-all-done.keys) | copy-start | bytes 2359300
  82.0 11.6 %copy-start.3 = (bf16[26,4,896]{2,1,0:T(4,128)(2,1)S(1)}, bf16[26,4,896]{2,1,0:T(4,128)(2,1)}, u32[]{:S(2)}) copy-start(bf16[26,4,896]{2,1,0:T(4,128)(2,1)} %param.13) | copy-start | bytes 559108
  82.0 12.0 %copy-start.5 = (f32[896]{0:T(1024)S(1)}, f32[896]{0:T(1024)}, u32[]{:S(2)}) copy-start(f32[896]{0:T(1024)} %param.15) | copy-start | bytes 10756
  82.1 39.5 %all-to-all-start.1 = ((bf16[64,16,1024]{2,1,0:T(8,128)(2,1)}), bf16[64,16,1024]{2,1,0:T(8,128)(2,1)}, u32[]{:S(2)}, u32[]{:S(2)}) async-start(bf16[64,16,1024]{2,1,0:T(8,128)(2,1)} %shard_map.113), calls=%async_computation.1 | async-start | bytes 4194304 | tf_op jit(solution)/shard_map/all_to_all | solution.py:265
  94.0 1.9 %copy-start.1 = (bf16[1792,896]{1,0:T(8,128)(2,1)S(1)}, bf16[1792,896]{1,0:T(8,128)(2,1)}, u32[]{:S(2)}) copy-start(bf16[1792,896]{1,0:T(8,128)(2,1)} %all-gather.3.cloned.1.call-done) | copy-start | bytes 9633796
Sparse Core Ops, SparseCore 0:
  11.4 55.1 all-gather.2

commit v7 on v6

--- a/solution.py
+++ b/solution.py
@@ -159,7 +159,15 @@
     return lax.ppermute(piece, ("zh", "core"), pairs)
 
 
-def pack_kernel(w_query, w_key, w_value, w_out, packed):
+def pack_kernel(y, ids, slab, w_query, w_key, w_value, w_out, pair, packed, held):
+    rows = pl.ds(pl.multiple_of(y[0] * SLAB_ROWS, 8), SLAB_ROWS)
+    held[...] = jnp.zeros_like(held)
+    held[:SLAB_ROWS, :] = slab[rows, :]
+    flat = ids[...].astype(F32)
+    owner = jnp.floor((flat + 0.5) * (1.0 / ROWS))
+    held[SLAB_ROWS : SLAB_ROWS + 2, :GROUPS] = owner
+    held[SLAB_ROWS + 2 : SLAB_ROWS + 4, :GROUPS] = flat - owner * ROWS
+    pair[...] = held[...].astype(BF)
     part = w_query.shape[0]
     half = part // 2
     packed[:part, :HD] = w_query[...]
@@ -208,17 +216,18 @@
     flat = neighbour_ids.T.reshape(PAIRS)
     owner = lax.div(flat, ROWS)
     local = flat - owner * ROWS
-    quarter = lax.dynamic_slice_in_dim(slab, y * SLAB_ROWS, SLAB_ROWS, 0).astype(BF)
-    numbers = jnp.pad(jnp.stack([owner, local]).astype(BF), ((0, KEYPAD - SLAB_ROWS - 2), (0, KEY - PAIRS)))
-    pair = jnp.concatenate([quarter, numbers], axis=0)
-    pair, w_query, w_key, w_value, w_out = lax.optimization_barrier((pair, w_query, w_key, w_value, w_out))
-    pair = lax.ppermute(pair, "zl", [(0, 1), (1, 0)])
-    packed = pl.pallas_call(
+    mine, packed = pl.pallas_call(
         pack_kernel,
-        out_shape=jax.ShapeDtypeStruct((2 * w_query.shape[0], E), BF),
-        in_specs=vmem(4),
-        out_specs=pl.BlockSpec(memory_space=pltpu.VMEM),
-    )(w_query, w_key, w_value, w_out)
+        out_shape=(
+            jax.ShapeDtypeStruct((KEYPAD, KEY), BF),
+            jax.ShapeDtypeStruct((2 * w_query.shape[0], E), BF),
+        ),
+        in_specs=[pl.BlockSpec(memory_space=pltpu.SMEM), *vmem(6)],
+        out_specs=tuple(vmem(2)),
+        scratch_shapes=[pltpu.VMEM((KEYPAD, KEY), F32)],
+    )(y.reshape(1).astype(jnp.int32), neighbour_ids.T, slab, w_query, w_key, w_value, w_out)
+    quarter = mine[:SLAB_ROWS]
+    pair = lax.ppermute(mine, "zl", [(0, 1), (1, 0)])
     token = lax.dynamic_index_in_dim(table, y, axis=1, keepdims=False)
     both = jnp.concatenate([quarter, pair[:SLAB_ROWS]], axis=1)
     both = jnp.pad(both, ((0, 0), (0, E - 2 * KEY)))
@@ -232,8 +241,8 @@
     pieces = [ours[1], others[1], ours[2], others[2], ours[3], others[3], ours[0], far]
     whole = lax.all_gather(packed, "pb", axis=0, tiled=False)
     code, own = marks_of(owner, local, zh, zl)
-    partner = pair[SLAB_ROWS : SLAB_ROWS + 2, :PAIRS].astype(jnp.int32)
-    _, other = marks_of(partner[0], partner[1], zh, zl)
+    partner = pair[SLAB_ROWS : SLAB_ROWS + 4, :GROUPS].astype(jnp.int32)
+    _, other = marks_of(partner[:2].reshape(PAIRS), partner[2:].reshape(PAIRS), zh, zl)
     place = (code >> 7) * (PLANE * SLOTS) + (code & 127)
     place = place.reshape(2, GROUPS).T.reshape(GROUPS, 2, 1) + lax.iota(jnp.int32, NT) * 128
     place = place.reshape(PAIRS * NT, 1)

time: 135 us -> 134 us (level)
  transfers between devices with their start and end apart: 11 -> 11, of which waited for: 8 -> 7; matrix products, arithmetic and copies ran while one was open for 3% -> 4% of each run, Pallas kernels for 4% -> 4%
where the time goes in v7:
time: 134 us; the launch traced here: 133 us
  starting transfers between devices  53.6 us (40%)
  waiting for transfers between devices  43.6 us (33%)
  between operations  14.4 us (11%)
  Pallas kernels  13.7 us (10%)
  local copies, waits for them, and re-layouts  6.62 us (5%)
    ppermute x7, starting transfers between devices, ring_moved(): return lax.ppermute(piece, ('zh', 'core'), pairs)  28.9 us
    all_to_all x1, waiting for transfers between devices, per_device(): got = lax.all_to_all(served, NEAR, split_axis=0, concat_axis=0, tiled=True)  24.8 us
    ppermute x7, waiting for transfers between devices, ring_moved(): return lax.ppermute(piece, ('zh', 'core'), pairs)  18.8 us
    all_to_all x1, starting transfers between devices, per_device(): got = lax.all_to_all(served, NEAR, split_axis=0, concat_axis=0, tiled=True)  11.5 us
    all_to_all x1, starting transfers between devices, per_device(): asked = lax.all_to_all(sent, FLAT, split_axis=0, concat_axis=0, tiled=True)  9.39 us
    pallas_call x1, Pallas kernels, per_device(): pl.pallas_call(layer_kernel, out_shape=(jax.ShapeDtypeStruct((2, GROUPS),...  5.5 us
    pallas_call x1, Pallas kernels, per_device(): pl.pallas_call(serve_kernel, out_shape=jax.ShapeDtypeStruct((SERVERS, SLO...  5.05 us
    ppermute x1, starting transfers between devices, per_device(): pair = lax.ppermute(mine, 'zl', [(0, 1), (1, 0)])  3.83 us
  transfers between devices with their start and end apart: 11, of which 7 were waited for; matrix products, arithmetic and copies ran while one was open for 4% of the time, Pallas kernels for 4%

profile of v7, /device:TPU:6, one launch (start us, length us, event | category | flops | bytes accessed | tf_op | source)
XLA Modules:
  0.0 132.8 jit_solution(17885664071737790301)
XLA Ops:
  7.2 0.0 copy-start
  7.2 0.0 copy-start.4
  7.2 0.0 all-gather.3.cloned.1.call-start
  7.2 2.4 %shard_map.113 = (bf16[32,384]{1,0:T(8,128)(2,1)}, bf16[448,896]{1,0:T(8,128)(2,1)}) custom-call(s32[1]{0:T(128)} %bitcast.2.y, s32[2,26]{1,0:T(2,128)} %bitcast.19, f32[96,384]{1,0:T(8,128)} %slab.1, bf16[224,448]{1,0:T(8,128)(2,1)} %w_query.1, bf16[224,448]{1,0:T(8,128)(2,1)} %w_key.1, bf16[224,448]{1,0:T(8,128)(2,1)} %w_value.1, bf16[112,896]{1,0:T(8,128)(2,1)} %w_out.1), custom_call_target="tpu_custom_call" | custom-call | tf_op jit(solution)/shard_map/pallas_call | solution.py:219
  9.7 0.0 all-gather.3.cloned.1.call-update
  9.7 3.8 %collective-permute-start = (bf16[32,384]{1,0:T(8,128)(2,1)}, bf16[32,384]{1,0:T(8,128)(2,1)S(1)}, u32[]{:S(2)}, u32[]{:S(2)}) collective-permute-start(bf16[32,384]{1,0:T(8,128)(2,1)} %get-tuple-element.12), channel_id=1, source_target_pairs={{0,8},{8,0},{1,9},{9,1},{2,10},{10,2},{3,11},{11,3},{4,12},{12,4},... | collective-permute-start | bytes 73736 | tf_op jit(solution)/shard_map/ppermute | solution.py:230
  13.5 0.8 reshape.252
  14.3 0.2 select_reduce_fusion.3
  14.5 0.0 copy-done
  14.5 0.4 constant_dynamic-slice_fusion
  14.9 0.7 slice.32
  15.6 0.0 copy-done.4
  15.7 0.0 collective-permute-done
  15.7 0.1 reshape.254
  15.8 0.1 add.227
  15.9 0.2 select_reduce_fusion.1
  16.1 0.1 select_reduce_fusion.2
  16.2 0.1 convert_element_type.43
  16.3 0.1 convert_element_type.46
  16.4 1.0 broadcast_in_dim.59
  17.4 9.4 %all-to-all-start = ((bf16[32,32,384]{2,1,0:T(8,128)(2,1)}), bf16[32,32,384]{2,1,0:T(8,128)(2,1)S(1)}, u32[]{:S(2)}, u32[]{:S(2)}) async-start(bf16[32,32,384]{2,1,0:T(8,128)(2,1)} %bitcast.3), calls=%async_computation | async-start | bytes 1572864 | tf_op jit(solution)/shard_map/all_to_all | solution.py:254
  26.9 3.4 %collective-permute-start.1 = (bf16[120,896]{1,0:T(8,128)(2,1)S(1)}, bf16[120,896]{1,0:T(8,128)(2,1)S(1)}, u32[]{:S(2)}, u32[]{:S(2)}) collective-permute-start(bf16[120,896]{1,0:T(8,128)(2,1)S(1)} %pad_maximum_fusion.refs_6_), channel_id=1, source_target_pairs={{0,16},{4,116},{16,32},{20,4},{32,48},{36,20},{48,64},{52,36},{64,... | collective-permute-start | bytes 645128 | tf_op jit(solution)/shard_map/ppermute | solution.py:159
  30.2 9.4 %collective-permute-start.2 = (bf16[120,896]{1,0:T(8,128)(2,1)S(1)}, bf16[120,896]{1,0:T(8,128)(2,1)S(1)}, u32[]{:S(2)}, u32[]{:S(2)}) collective-permute-start(bf16[120,896]{1,0:T(8,128)(2,1)S(1)} %pad_maximum_fusion.refs_6_), channel_id=1, source_target_pairs={{4,16},{0,116},{20,32},{16,4},{36,48},{32,20},{52,64},{48,36},{68,... | collective-permute-start | bytes 645128 | tf_op jit(solution)/shard_map/ppermute | solution.py:159
  39.7 1.9 %collective-permute-done.1.refs_0_ = bf16[120,896]{1,0:T(8,128)(2,1)S(1)} collective-permute-done((bf16[120,896]{1,0:T(8,128)(2,1)S(1)}, bf16[120,896]{1,0:T(8,128)(2,1)S(1)}, u32[]{:S(2)}, u32[]{:S(2)}) %collective-permute-start.1) | collective-permute-done | bytes 215072 | tf_op jit(solution)/shard_map/ppermute | solution.py:159
  41.5 1.9 %collective-permute-start.3 = (bf16[120,896]{1,0:T(8,128)(2,1)S(1)}, bf16[120,896]{1,0:T(8,128)(2,1)S(1)}, u32[]{:S(2)}, u32[]{:S(2)}) collective-permute-start(bf16[120,896]{1,0:T(8,128)(2,1)S(1)} %collective-permute-done.1.refs_0_), channel_id=1, source_target_pairs={{0,16},{4,116},{16,32},{20,4},{32,48},{36,20},{48,64},{52,36},{64,... | collective-permute-start | bytes 645128 | tf_op jit(solution)/shard_map/ppermute | solution.py:159
  43.5 2.8 %collective-permute-done.2.refs_1_ = bf16[120,896]{1,0:T(8,128)(2,1)S(1)} collective-permute-done((bf16[120,896]{1,0:T(8,128)(2,1)S(1)}, bf16[120,896]{1,0:T(8,128)(2,1)S(1)}, u32[]{:S(2)}, u32[]{:S(2)}) %collective-permute-start.2) | collective-permute-done | bytes 215072 | tf_op jit(solution)/shard_map/ppermute | solution.py:159
  46.3 4.2 %collective-permute-start.4 = (bf16[120,896]{1,0:T(8,128)(2,1)S(1)}, bf16[120,896]{1,0:T(8,128)(2,1)S(1)}, u32[]{:S(2)}, u32[]{:S(2)}) collective-permute-start(bf16[120,896]{1,0:T(8,128)(2,1)S(1)} %collective-permute-done.2.refs_1_), channel_id=1, source_target_pairs={{0,16},{4,116},{16,32},{20,4},{32,48},{36,20},{48,64},{52,36},{64,... | collective-permute-start | bytes 645128 | tf_op jit(solution)/shard_map/ppermute | solution.py:159
  50.5 1.3 collective-permute-done.3.refs_2_
  51.8 2.1 %collective-permute-start.5 = (bf16[120,896]{1,0:T(8,128)(2,1)S(1)}, bf16[120,896]{1,0:T(8,128)(2,1)S(1)}, u32[]{:S(2)}, u32[]{:S(2)}) collective-permute-start(bf16[120,896]{1,0:T(8,128)(2,1)S(1)} %collective-permute-done.3.refs_2_), channel_id=1, source_target_pairs={{0,16},{4,116},{16,32},{20,4},{32,48},{36,20},{48,64},{52,36},{64,... | collective-permute-start | bytes 645128 | tf_op jit(solution)/shard_map/ppermute | solution.py:159
  53.9 2.4 %collective-permute-done.4.refs_3_ = bf16[120,896]{1,0:T(8,128)(2,1)S(1)} collective-permute-done((bf16[120,896]{1,0:T(8,128)(2,1)S(1)}, bf16[120,896]{1,0:T(8,128)(2,1)S(1)}, u32[]{:S(2)}, u32[]{:S(2)}) %collective-permute-start.4) | collective-permute-done | bytes 215072 | tf_op jit(solution)/shard_map/ppermute | solution.py:159
  56.3 4.6 %collective-permute-start.6 = (bf16[120,896]{1,0:T(8,128)(2,1)S(1)}, bf16[120,896]{1,0:T(8,128)(2,1)S(1)}, u32[]{:S(2)}, u32[]{:S(2)}) collective-permute-start(bf16[120,896]{1,0:T(8,128)(2,1)S(1)} %collective-permute-done.4.refs_3_), channel_id=1, source_target_pairs={{0,16},{4,116},{16,32},{20,4},{32,48},{36,20},{48,64},{52,36},{64,... | collective-permute-start | bytes 645128 | tf_op jit(solution)/shard_map/ppermute | solution.py:159
  60.8 2.8 %collective-permute-done.5.refs_4_ = bf16[120,896]{1,0:T(8,128)(2,1)S(1)} collective-permute-done((bf16[120,896]{1,0:T(8,128)(2,1)S(1)}, bf16[120,896]{1,0:T(8,128)(2,1)S(1)}, u32[]{:S(2)}, u32[]{:S(2)}) %collective-permute-start.5) | collective-permute-done | bytes 215072 | tf_op jit(solution)/shard_map/ppermute | solution.py:159
  63.6 3.4 %collective-permute-start.7 = (bf16[120,896]{1,0:T(8,128)(2,1)S(1)}, bf16[120,896]{1,0:T(8,128)(2,1)S(1)}, u32[]{:S(2)}, u32[]{:S(2)}) collective-permute-start(bf16[120,896]{1,0:T(8,128)(2,1)S(1)} %collective-permute-done.5.refs_4_), channel_id=1, source_target_pairs={{0,16},{4,116},{16,32},{20,4},{32,48},{36,20},{48,64},{52,36},{64,... | collective-permute-start | bytes 645128 | tf_op jit(solution)/shard_map/ppermute | solution.py:159
  67.0 0.0 all-to-all-done.keys
  67.1 0.0 copy-start.2
  67.2 1.1 select_n.128.code
  68.3 0.0 collective-permute-done.6.refs_5_
  68.3 7.6 %collective-permute-done.7.refs_7_ = bf16[120,896]{1,0:T(8,128)(2,1)S(1)} collective-permute-done((bf16[120,896]{1,0:T(8,128)(2,1)S(1)}, bf16[120,896]{1,0:T(8,128)(2,1)S(1)}, u32[]{:S(2)}, u32[]{:S(2)}) %collective-permute-start.7) | collective-permute-done | bytes 215072 | tf_op jit(solution)/shard_map/ppermute | solution.py:159
  75.8 0.0 copy-done.2
  75.8 5.0 %shard_map.114 = bf16[64,16,1024]{2,1,0:T(8,128)(2,1)} custom-call(s32[1,1,128]{2,1,0:T(1,128)S(1)} %broadcast_in_dim.55.parity, s32[1024,1]{1,0:T(8,128)} %select_n.128.code, bf16[32,32,384]{2,1,0:T(8,128)(2,1)} %copy-done.2, bf16[120,896]{1,0:T(8,128)(2,1)S(1)} %collective-permute-done.1.refs_0_, bf16[120,896]{1,0:T(8,128)(2,1)S(1)} %collective-permute-done.2.refs_1_, ...), custom_call_target="tpu_custom_call" | custom-call | tf_op jit(solution)/shard_map/pallas_call | solution.py:260
  80.9 0.0 all-gather.3.cloned.1.call-done
  80.9 0.0 copy-start.3
  80.9 0.0 copy-start.6
  80.9 0.0 copy-start.5
  80.9 11.5 %all-to-all-start.1 = ((bf16[64,16,1024]{2,1,0:T(8,128)(2,1)}), bf16[64,16,1024]{2,1,0:T(8,128)(2,1)}, u32[]{:S(2)}, u32[]{:S(2)}) async-start(bf16[64,16,1024]{2,1,0:T(8,128)(2,1)} %shard_map.114), calls=%async_computation.1 | async-start | bytes 4194304 | tf_op jit(solution)/shard_map/all_to_all | solution.py:274
  92.4 0.1 reduce_max.21
  92.5 0.0 copy-done.3
  92.6 0.0 copy-done.6
  92.6 0.1 copy.22
  92.7 0.1 broadcast_add_fusion
  92.8 0.1 add.232.place
  92.9 0.0 copy-done.5
  92.9 0.0 copy-start.1
  92.9 1.9 %copy-done.1 = bf16[1792,896]{1,0:T(8,128)(2,1)S(1)} copy-done((bf16[1792,896]{1,0:T(8,128)(2,1)S(1)}, bf16[1792,896]{1,0:T(8,128)(2,1)}, u32[]{:S(2)}) %copy-start.1) | copy-done | bytes 3211288
  94.8 0.8 shard_map.115
  95.6 24.8 %all-to-all-done.1.got = bf16[64,16,1024]{2,1,0:T(8,128)(2,1)} async-done(((bf16[64,16,1024]{2,1,0:T(8,128)(2,1)}), bf16[64,16,1024]{2,1,0:T(8,128)(2,1)}, u32[]{:S(2)}, u32[]{:S(2)}) %all-to-all-start.1) | async-done | bytes 2097184 | tf_op jit(solution)/shard_map/all_to_all | solution.py:274
  120.4 5.5 %shard_map.116 = (f32[2,26]{1,0:T(2,128)}, bf16[26,2,4,896]{3,2,1,0:T(4,128)(2,1)}) custom-call(s32[208,1]{1,0:T(8,128)S(1)} %add.232.place, bf16[64,16,1024]{2,1,0:T(8,128)(2,1)} %all-to-all-done.1.got, bf16[104,448]{1,0:T(8,128)(2,1)S(1)} %get-tuple-element.16.keyed, bf16[104,448]{1,0:T(8,128)(2,1)S(1)} %get-tuple-element.17.valued, ...), custom_call_target="tpu_custom_call" | custom-call | tf_op jit(solution)/shard_map/pallas_call | solution.py:288
  (24 shorter events, 0.4 us)
Async XLA Ops:
  7.2 7.3 %copy-start = (bf16[96,4,896]{2,1,0:T(4,128)(2,1)S(1)}, bf16[96,4,896]{2,1,0:T(4,128)(2,1)}, u32[]{:S(2)}) copy-start(bf16[96,4,896]{2,1,0:T(4,128)(2,1)} %param.14) | copy-start | bytes 2064388
  7.2 8.4 %copy-start.4 = (f32[26,384]{1,0:T(8,128)S(1)}, f32[26,384]{1,0:T(8,128)}, u32[]{:S(2)}) copy-start(f32[26,384]{1,0:T(8,128)} %param.10) | copy-start | bytes 119812
  7.2 73.7 %all-gather.3.cloned.1.call-start = ((), (), s32[]{:S(2)}) async-start(), calls=%async_computation.2 | async-start | bytes 4014080 | tf_op jit(solution)/shard_map/all_gather | solution.py:242
  9.7 6.0 %collective-permute-start = (bf16[32,384]{1,0:T(8,128)(2,1)}, bf16[32,384]{1,0:T(8,128)(2,1)S(1)}, u32[]{:S(2)}, u32[]{:S(2)}) collective-permute-start(bf16[32,384]{1,0:T(8,128)(2,1)} %get-tuple-element.12), channel_id=1, source_target_pairs={{0,8},{8,0},{1,9},{9,1},{2,10},{10,2},{3,11},{11,3},{4,12},{12,4},... | collective-permute-start | bytes 73736 | tf_op jit(solution)/shard_map/ppermute | solution.py:230
  17.4 49.6 %all-to-all-start = ((bf16[32,32,384]{2,1,0:T(8,128)(2,1)}), bf16[32,32,384]{2,1,0:T(8,128)(2,1)S(1)}, u32[]{:S(2)}, u32[]{:S(2)}) async-start(bf16[32,32,384]{2,1,0:T(8,128)(2,1)} %bitcast.3), calls=%async_computation | async-start | bytes 1572864 | tf_op jit(solution)/shard_map/all_to_all | solution.py:254
  26.9 14.7 %collective-permute-start.1 = (bf16[120,896]{1,0:T(8,128)(2,1)S(1)}, bf16[120,896]{1,0:T(8,128)(2,1)S(1)}, u32[]{:S(2)}, u32[]{:S(2)}) collective-permute-start(bf16[120,896]{1,0:T(8,128)(2,1)S(1)} %pad_maximum_fusion.refs_6_), channel_id=1, source_target_pairs={{0,16},{4,116},{16,32},{20,4},{32,48},{36,20},{48,64},{52,36},{64,... | collective-permute-start | bytes 645128 | tf_op jit(solution)/shard_map/ppermute | solution.py:159
  30.2 16.1 %collective-permute-start.2 = (bf16[120,896]{1,0:T(8,128)(2,1)S(1)}, bf16[120,896]{1,0:T(8,128)(2,1)S(1)}, u32[]{:S(2)}, u32[]{:S(2)}) collective-permute-start(bf16[120,896]{1,0:T(8,128)(2,1)S(1)} %pad_maximum_fusion.refs_6_), channel_id=1, source_target_pairs={{4,16},{0,116},{20,32},{16,4},{36,48},{32,20},{52,64},{48,36},{68,... | collective-permute-start | bytes 645128 | tf_op jit(solution)/shard_map/ppermute | solution.py:159
  41.5 10.3 %collective-permute-start.3 = (bf16[120,896]{1,0:T(8,128)(2,1)S(1)}, bf16[120,896]{1,0:T(8,128)(2,1)S(1)}, u32[]{:S(2)}, u32[]{:S(2)}) collective-permute-start(bf16[120,896]{1,0:T(8,128)(2,1)S(1)} %collective-permute-done.1.refs_0_), channel_id=1, source_target_pairs={{0,16},{4,116},{16,32},{20,4},{32,48},{36,20},{48,64},{52,36},{64,... | collective-permute-start | bytes 645128 | tf_op jit(solution)/shard_map/ppermute | solution.py:159
  46.3 10.0 %collective-permute-start.4 = (bf16[120,896]{1,0:T(8,128)(2,1)S(1)}, bf16[120,896]{1,0:T(8,128)(2,1)S(1)}, u32[]{:S(2)}, u32[]{:S(2)}) collective-permute-start(bf16[120,896]{1,0:T(8,128)(2,1)S(1)} %collective-permute-done.2.refs_1_), channel_id=1, source_target_pairs={{0,16},{4,116},{16,32},{20,4},{32,48},{36,20},{48,64},{52,36},{64,... | collective-permute-start | bytes 645128 | tf_op jit(solution)/shard_map/ppermute | solution.py:159
  51.8 11.8 %collective-permute-start.5 = (bf16[120,896]{1,0:T(8,128)(2,1)S(1)}, bf16[120,896]{1,0:T(8,128)(2,1)S(1)}, u32[]{:S(2)}, u32[]{:S(2)}) collective-permute-start(bf16[120,896]{1,0:T(8,128)(2,1)S(1)} %collective-permute-done.3.refs_2_), channel_id=1, source_target_pairs={{0,16},{4,116},{16,32},{20,4},{32,48},{36,20},{48,64},{52,36},{64,... | collective-permute-start | bytes 645128 | tf_op jit(solution)/shard_map/ppermute | solution.py:159
  56.3 12.0 %collective-permute-start.6 = (bf16[120,896]{1,0:T(8,128)(2,1)S(1)}, bf16[120,896]{1,0:T(8,128)(2,1)S(1)}, u32[]{:S(2)}, u32[]{:S(2)}) collective-permute-start(bf16[120,896]{1,0:T(8,128)(2,1)S(1)} %collective-permute-done.4.refs_3_), channel_id=1, source_target_pairs={{0,16},{4,116},{16,32},{20,4},{32,48},{36,20},{48,64},{52,36},{64,... | collective-permute-start | bytes 645128 | tf_op jit(solution)/shard_map/ppermute | solution.py:159
  63.6 12.2 %collective-permute-start.7 = (bf16[120,896]{1,0:T(8,128)(2,1)S(1)}, bf16[120,896]{1,0:T(8,128)(2,1)S(1)}, u32[]{:S(2)}, u32[]{:S(2)}) collective-permute-start(bf16[120,896]{1,0:T(8,128)(2,1)S(1)} %collective-permute-done.5.refs_4_), channel_id=1, source_target_pairs={{0,16},{4,116},{16,32},{20,4},{32,48},{36,20},{48,64},{52,36},{64,... | collective-permute-start | bytes 645128 | tf_op jit(solution)/shard_map/ppermute | solution.py:159
  67.1 8.8 %copy-start.2 = (bf16[32,32,384]{2,1,0:T(8,128)(2,1)}, bf16[32,32,384]{2,1,0:T(8,128)(2,1)S(1)}, u32[]{:S(2)}) copy-start(bf16[32,32,384]{2,1,0:T(8,128)(2,1)S(1)} %all-to-all-done.keys) | copy-start | bytes 2359300
  80.9 11.6 %copy-start.3 = (bf16[26,4,896]{2,1,0:T(4,128)(2,1)S(1)}, bf16[26,4,896]{2,1,0:T(4,128)(2,1)}, u32[]{:S(2)}) copy-start(bf16[26,4,896]{2,1,0:T(4,128)(2,1)} %param.13) | copy-start | bytes 559108
  80.9 11.7 %copy-start.6 = (s32[26,2]{0,1:T(2,128)S(1)}, s32[26,2]{0,1:T(2,128)}, u32[]{:S(2)}) copy-start(s32[26,2]{0,1:T(2,128)} %param.12) | copy-start | bytes 628
  80.9 12.0 %copy-start.5 = (f32[896]{0:T(1024)S(1)}, f32[896]{0:T(1024)}, u32[]{:S(2)}) copy-start(f32[896]{0:T(1024)} %param.15) | copy-start | bytes 10756
  80.9 39.5 %all-to-all-start.1 = ((bf16[64,16,1024]{2,1,0:T(8,128)(2,1)}), bf16[64,16,1024]{2,1,0:T(8,128)(2,1)}, u32[]{:S(2)}, u32[]{:S(2)}) async-start(bf16[64,16,1024]{2,1,0:T(8,128)(2,1)} %shard_map.114), calls=%async_computation.1 | async-start | bytes 4194304 | tf_op jit(solution)/shard_map/all_to_all | solution.py:274
  92.9 1.9 %copy-start.1 = (bf16[1792,896]{1,0:T(8,128)(2,1)S(1)}, bf16[1792,896]{1,0:T(8,128)(2,1)}, u32[]{:S(2)}) copy-start(bf16[1792,896]{1,0:T(8,128)(2,1)} %all-gather.3.cloned.1.call-done) | copy-start | bytes 9633796
Sparse Core Ops, SparseCore 0:
  10.1 55.2 all-gather.2

commit v8 on v7

--- a/solution.py
+++ b/solution.py
@@ -54,6 +54,17 @@
         for part in range(2):
             at = (2 * k + part) * SLAB_ROWS
             slab[at : at + SLAB_ROWS, :] = extra[:, part * KEY : (part + 1) * KEY].astype(F32)
+    step = 256
+    n = step // SLOTS
+    copies = []
+    for i in range(SERVERS * SLOTS // step):
+        label = lax.broadcasted_iota(jnp.int32, (step, RING * ROWS), 1)
+        pick = (code[i * step : (i + 1) * step, :] == label).astype(F32).astype(BF)
+        found = jnp.dot(pick, held[...], preferred_element_type=F32).astype(BF)
+        out[i * n : (i + 1) * n, :, :E] = found.reshape(n, SLOTS, E)
+        block = pl.ds(i * n, n)
+        copies.append(pltpu.make_async_copy(out.at[block, :, pl.ds(0, E)], sent.at[block, :, pl.ds(0, E)], sems.at[i]))
+        copies[-1].start()
     wide = 512
     n = wide // KEYPAD
     rows = slab[...].astype(BF)
@@ -92,17 +103,9 @@
         for z in range(2):
             at = z * PLANE + i * n
             out[at : at + n, :, E:] = jnp.where(mine == z, total, none).astype(BF)
-    step = 256
-    n = step // SLOTS
-    copies = []
-    for i in range(SERVERS * SLOTS // step):
-        label = lax.broadcasted_iota(jnp.int32, (step, RING * ROWS), 1)
-        pick = (code[i * step : (i + 1) * step, :] == label).astype(F32).astype(BF)
-        found = jnp.dot(pick, held[...], preferred_element_type=F32).astype(BF)
-        out[i * n : (i + 1) * n, :, :E] = found.reshape(n, SLOTS, E)
-        block = pl.ds(i * n, n)
-        copies.append(pltpu.make_async_copy(out.at[block], sent.at[block], sems.at[i]))
-        copies[-1].start()
+    lanes = pl.ds(E, WIDE - E)
+    copies.append(pltpu.make_async_copy(out.at[:, :, lanes], sent.at[:, :, lanes], sems.at[4]))
+    copies[-1].start()
     for copy in copies:
         copy.wait()
 
@@ -266,7 +269,7 @@
             pltpu.VMEM((RING * ROWS, E), BF),
             pltpu.VMEM((RING * 2 * SLAB_ROWS, KEY), F32),
             pltpu.VMEM((SERVERS, SLOTS, WIDE), BF),
-            pltpu.SemaphoreType.DMA((4,)),
+            pltpu.SemaphoreType.DMA((5,)),
         ],
         compiler_params=pltpu.CompilerParams(vmem_limit_bytes=SERVE_LIMIT),
     )(parity, wanted, asked, *pieces)

time: 134 us -> 134 us (level)
  no operation moved by 1% of the time
where the time goes in v8:
time: 134 us; the launch traced here: 133 us
  starting transfers between devices  53.6 us (40%)
  waiting for transfers between devices  43.6 us (33%)
  between operations  14.4 us (11%)
  Pallas kernels  13.7 us (10%)
  local copies, waits for them, and re-layouts  6.62 us (5%)
    ppermute x7, starting transfers between devices, ring_moved(): return lax.ppermute(piece, ('zh', 'core'), pairs)  28.9 us
    all_to_all x1, waiting for transfers between devices, per_device(): got = lax.all_to_all(served, NEAR, split_axis=0, concat_axis=0, tiled=True)  24.8 us
    ppermute x7, waiting for transfers between devices, ring_moved(): return lax.ppermute(piece, ('zh', 'core'), pairs)  18.8 us
    all_to_all x1, starting transfers between devices, per_device(): got = lax.all_to_all(served, NEAR, split_axis=0, concat_axis=0, tiled=True)  11.5 us
    all_to_all x1, starting transfers between devices, per_device(): asked = lax.all_to_all(sent, FLAT, split_axis=0, concat_axis=0, tiled=True)  9.39 us
    pallas_call x1, Pallas kernels, per_device(): pl.pallas_call(layer_kernel, out_shape=(jax.ShapeDtypeStruct((2, GROUPS),...  5.52 us
    pallas_call x1, Pallas kernels, per_device(): pl.pallas_call(serve_kernel, out_shape=jax.ShapeDtypeStruct((SERVERS, SLO...  4.99 us
    ppermute x1, starting transfers between devices, per_device(): pair = lax.ppermute(mine, 'zl', [(0, 1), (1, 0)])  3.83 us
  transfers between devices with their start and end apart: 11, of which 7 were waited for; matrix products, arithmetic and copies ran while one was open for 4% of the time, Pallas kernels for 4%

profile of v8, /device:TPU:6, one launch (start us, length us, event | category | flops | bytes accessed | tf_op | source)
XLA Modules:
  0.0 132.7 jit_solution(5081809968711913453)
XLA Ops:
  7.2 0.0 copy-start
  7.2 0.0 copy-start.4
  7.2 0.0 all-gather.3.cloned.1.call-start
  7.2 2.4 %shard_map.113 = (bf16[32,384]{1,0:T(8,128)(2,1)}, bf16[448,896]{1,0:T(8,128)(2,1)}) custom-call(s32[1]{0:T(128)} %bitcast.2.y, s32[2,26]{1,0:T(2,128)} %bitcast.19, f32[96,384]{1,0:T(8,128)} %slab.1, bf16[224,448]{1,0:T(8,128)(2,1)} %w_query.1, bf16[224,448]{1,0:T(8,128)(2,1)} %w_key.1, bf16[224,448]{1,0:T(8,128)(2,1)} %w_value.1, bf16[112,896]{1,0:T(8,128)(2,1)} %w_out.1), custom_call_target="tpu_custom_call" | custom-call | tf_op jit(solution)/shard_map/pallas_call | solution.py:222
  9.7 0.0 all-gather.3.cloned.1.call-update
  9.7 3.8 %collective-permute-start = (bf16[32,384]{1,0:T(8,128)(2,1)}, bf16[32,384]{1,0:T(8,128)(2,1)S(1)}, u32[]{:S(2)}, u32[]{:S(2)}) collective-permute-start(bf16[32,384]{1,0:T(8,128)(2,1)} %get-tuple-element.12), channel_id=1, source_target_pairs={{0,8},{8,0},{1,9},{9,1},{2,10},{10,2},{3,11},{11,3},{4,12},{12,4},... | collective-permute-start | bytes 73736 | tf_op jit(solution)/shard_map/ppermute | solution.py:233
  13.5 0.8 reshape.252
  14.3 0.2 select_reduce_fusion.3
  14.5 0.0 copy-done
  14.5 0.4 constant_dynamic-slice_fusion
  14.9 0.7 slice.32
  15.6 0.0 copy-done.4
  15.7 0.0 collective-permute-done
  15.7 0.1 reshape.254
  15.8 0.1 add.227
  15.9 0.2 select_reduce_fusion.1
  16.1 0.1 select_reduce_fusion.2
  16.2 0.1 convert_element_type.43
  16.3 0.1 convert_element_type.46
  16.4 1.0 broadcast_in_dim.59
  17.4 9.4 %all-to-all-start = ((bf16[32,32,384]{2,1,0:T(8,128)(2,1)}), bf16[32,32,384]{2,1,0:T(8,128)(2,1)S(1)}, u32[]{:S(2)}, u32[]{:S(2)}) async-start(bf16[32,32,384]{2,1,0:T(8,128)(2,1)} %bitcast.3), calls=%async_computation | async-start | bytes 1572864 | tf_op jit(solution)/shard_map/all_to_all | solution.py:257
  26.9 3.4 %collective-permute-start.1 = (bf16[120,896]{1,0:T(8,128)(2,1)S(1)}, bf16[120,896]{1,0:T(8,128)(2,1)S(1)}, u32[]{:S(2)}, u32[]{:S(2)}) collective-permute-start(bf16[120,896]{1,0:T(8,128)(2,1)S(1)} %pad_maximum_fusion.refs_6_), channel_id=1, source_target_pairs={{0,16},{4,116},{16,32},{20,4},{32,48},{36,20},{48,64},{52,36},{64,... | collective-permute-start | bytes 645128 | tf_op jit(solution)/shard_map/ppermute | solution.py:162
  30.2 9.4 %collective-permute-start.2 = (bf16[120,896]{1,0:T(8,128)(2,1)S(1)}, bf16[120,896]{1,0:T(8,128)(2,1)S(1)}, u32[]{:S(2)}, u32[]{:S(2)}) collective-permute-start(bf16[120,896]{1,0:T(8,128)(2,1)S(1)} %pad_maximum_fusion.refs_6_), channel_id=1, source_target_pairs={{4,16},{0,116},{20,32},{16,4},{36,48},{32,20},{52,64},{48,36},{68,... | collective-permute-start | bytes 645128 | tf_op jit(solution)/shard_map/ppermute | solution.py:162
  39.7 1.9 %collective-permute-done.1.refs_0_ = bf16[120,896]{1,0:T(8,128)(2,1)S(1)} collective-permute-done((bf16[120,896]{1,0:T(8,128)(2,1)S(1)}, bf16[120,896]{1,0:T(8,128)(2,1)S(1)}, u32[]{:S(2)}, u32[]{:S(2)}) %collective-permute-start.1) | collective-permute-done | bytes 215072 | tf_op jit(solution)/shard_map/ppermute | solution.py:162
  41.5 1.9 %collective-permute-start.3 = (bf16[120,896]{1,0:T(8,128)(2,1)S(1)}, bf16[120,896]{1,0:T(8,128)(2,1)S(1)}, u32[]{:S(2)}, u32[]{:S(2)}) collective-permute-start(bf16[120,896]{1,0:T(8,128)(2,1)S(1)} %collective-permute-done.1.refs_0_), channel_id=1, source_target_pairs={{0,16},{4,116},{16,32},{20,4},{32,48},{36,20},{48,64},{52,36},{64,... | collective-permute-start | bytes 645128 | tf_op jit(solution)/shard_map/ppermute | solution.py:162
  43.5 2.8 %collective-permute-done.2.refs_1_ = bf16[120,896]{1,0:T(8,128)(2,1)S(1)} collective-permute-done((bf16[120,896]{1,0:T(8,128)(2,1)S(1)}, bf16[120,896]{1,0:T(8,128)(2,1)S(1)}, u32[]{:S(2)}, u32[]{:S(2)}) %collective-permute-start.2) | collective-permute-done | bytes 215072 | tf_op jit(solution)/shard_map/ppermute | solution.py:162
  46.3 4.2 %collective-permute-start.4 = (bf16[120,896]{1,0:T(8,128)(2,1)S(1)}, bf16[120,896]{1,0:T(8,128)(2,1)S(1)}, u32[]{:S(2)}, u32[]{:S(2)}) collective-permute-start(bf16[120,896]{1,0:T(8,128)(2,1)S(1)} %collective-permute-done.2.refs_1_), channel_id=1, source_target_pairs={{0,16},{4,116},{16,32},{20,4},{32,48},{36,20},{48,64},{52,36},{64,... | collective-permute-start | bytes 645128 | tf_op jit(solution)/shard_map/ppermute | solution.py:162
  50.5 1.3 collective-permute-done.3.refs_2_
  51.8 2.1 %collective-permute-start.5 = (bf16[120,896]{1,0:T(8,128)(2,1)S(1)}, bf16[120,896]{1,0:T(8,128)(2,1)S(1)}, u32[]{:S(2)}, u32[]{:S(2)}) collective-permute-start(bf16[120,896]{1,0:T(8,128)(2,1)S(1)} %collective-permute-done.3.refs_2_), channel_id=1, source_target_pairs={{0,16},{4,116},{16,32},{20,4},{32,48},{36,20},{48,64},{52,36},{64,... | collective-permute-start | bytes 645128 | tf_op jit(solution)/shard_map/ppermute | solution.py:162
  53.9 2.4 %collective-permute-done.4.refs_3_ = bf16[120,896]{1,0:T(8,128)(2,1)S(1)} collective-permute-done((bf16[120,896]{1,0:T(8,128)(2,1)S(1)}, bf16[120,896]{1,0:T(8,128)(2,1)S(1)}, u32[]{:S(2)}, u32[]{:S(2)}) %collective-permute-start.4) | collective-permute-done | bytes 215072 | tf_op jit(solution)/shard_map/ppermute | solution.py:162
  56.3 4.6 %collective-permute-start.6 = (bf16[120,896]{1,0:T(8,128)(2,1)S(1)}, bf16[120,896]{1,0:T(8,128)(2,1)S(1)}, u32[]{:S(2)}, u32[]{:S(2)}) collective-permute-start(bf16[120,896]{1,0:T(8,128)(2,1)S(1)} %collective-permute-done.4.refs_3_), channel_id=1, source_target_pairs={{0,16},{4,116},{16,32},{20,4},{32,48},{36,20},{48,64},{52,36},{64,... | collective-permute-start | bytes 645128 | tf_op jit(solution)/shard_map/ppermute | solution.py:162
  60.8 2.8 %collective-permute-done.5.refs_4_ = bf16[120,896]{1,0:T(8,128)(2,1)S(1)} collective-permute-done((bf16[120,896]{1,0:T(8,128)(2,1)S(1)}, bf16[120,896]{1,0:T(8,128)(2,1)S(1)}, u32[]{:S(2)}, u32[]{:S(2)}) %collective-permute-start.5) | collective-permute-done | bytes 215072 | tf_op jit(solution)/shard_map/ppermute | solution.py:162
  63.6 3.4 %collective-permute-start.7 = (bf16[120,896]{1,0:T(8,128)(2,1)S(1)}, bf16[120,896]{1,0:T(8,128)(2,1)S(1)}, u32[]{:S(2)}, u32[]{:S(2)}) collective-permute-start(bf16[120,896]{1,0:T(8,128)(2,1)S(1)} %collective-permute-done.5.refs_4_), channel_id=1, source_target_pairs={{0,16},{4,116},{16,32},{20,4},{32,48},{36,20},{48,64},{52,36},{64,... | collective-permute-start | bytes 645128 | tf_op jit(solution)/shard_map/ppermute | solution.py:162
  67.0 0.0 all-to-all-done.keys
  67.1 0.0 copy-start.2
  67.2 1.1 select_n.128.code
  68.3 0.0 collective-permute-done.6.refs_5_
  68.3 7.6 %collective-permute-done.7.refs_7_ = bf16[120,896]{1,0:T(8,128)(2,1)S(1)} collective-permute-done((bf16[120,896]{1,0:T(8,128)(2,1)S(1)}, bf16[120,896]{1,0:T(8,128)(2,1)S(1)}, u32[]{:S(2)}, u32[]{:S(2)}) %collective-permute-start.7) | collective-permute-done | bytes 215072 | tf_op jit(solution)/shard_map/ppermute | solution.py:162
  75.8 0.0 copy-done.2
  75.8 5.0 %shard_map.114 = bf16[64,16,1024]{2,1,0:T(8,128)(2,1)} custom-call(s32[1,1,128]{2,1,0:T(1,128)S(1)} %broadcast_in_dim.55.parity, s32[1024,1]{1,0:T(8,128)} %select_n.128.code, bf16[32,32,384]{2,1,0:T(8,128)(2,1)} %copy-done.2, bf16[120,896]{1,0:T(8,128)(2,1)S(1)} %collective-permute-done.1.refs_0_, bf16[120,896]{1,0:T(8,128)(2,1)S(1)} %collective-permute-done.2.refs_1_, ...), custom_call_target="tpu_custom_call" | custom-call | tf_op jit(solution)/shard_map/pallas_call | solution.py:263
  80.8 0.0 all-gather.3.cloned.1.call-done
  80.8 0.0 copy-start.3
  80.8 0.0 copy-start.6
  80.9 0.0 copy-start.5
  80.9 11.5 %all-to-all-start.1 = ((bf16[64,16,1024]{2,1,0:T(8,128)(2,1)}), bf16[64,16,1024]{2,1,0:T(8,128)(2,1)}, u32[]{:S(2)}, u32[]{:S(2)}) async-start(bf16[64,16,1024]{2,1,0:T(8,128)(2,1)} %shard_map.114), calls=%async_computation.1 | async-start | bytes 4194304 | tf_op jit(solution)/shard_map/all_to_all | solution.py:277
  92.4 0.1 reduce_max.21
  92.5 0.0 copy-done.3
  92.5 0.0 copy-done.6
  92.5 0.1 copy.22
  92.7 0.1 broadcast_add_fusion
  92.7 0.1 add.232.place
  92.8 0.0 copy-done.5
  92.9 0.0 copy-start.1
  92.9 1.9 %copy-done.1 = bf16[1792,896]{1,0:T(8,128)(2,1)S(1)} copy-done((bf16[1792,896]{1,0:T(8,128)(2,1)S(1)}, bf16[1792,896]{1,0:T(8,128)(2,1)}, u32[]{:S(2)}) %copy-start.1) | copy-done | bytes 3211288
  94.8 0.8 shard_map.115
  95.6 24.8 %all-to-all-done.1.got = bf16[64,16,1024]{2,1,0:T(8,128)(2,1)} async-done(((bf16[64,16,1024]{2,1,0:T(8,128)(2,1)}), bf16[64,16,1024]{2,1,0:T(8,128)(2,1)}, u32[]{:S(2)}, u32[]{:S(2)}) %all-to-all-start.1) | async-done | bytes 2097184 | tf_op jit(solution)/shard_map/all_to_all | solution.py:277
  120.3 5.5 %shard_map.116 = (f32[2,26]{1,0:T(2,128)}, bf16[26,2,4,896]{3,2,1,0:T(4,128)(2,1)}) custom-call(s32[208,1]{1,0:T(8,128)S(1)} %add.232.place, bf16[64,16,1024]{2,1,0:T(8,128)(2,1)} %all-to-all-done.1.got, bf16[104,448]{1,0:T(8,128)(2,1)S(1)} %get-tuple-element.16.keyed, bf16[104,448]{1,0:T(8,128)(2,1)S(1)} %get-tuple-element.17.valued, ...), custom_call_target="tpu_custom_call" | custom-call | tf_op jit(solution)/shard_map/pallas_call | solution.py:291
  (24 shorter events, 0.4 us)
Async XLA Ops:
  7.2 7.3 %copy-start = (bf16[96,4,896]{2,1,0:T(4,128)(2,1)S(1)}, bf16[96,4,896]{2,1,0:T(4,128)(2,1)}, u32[]{:S(2)}) copy-start(bf16[96,4,896]{2,1,0:T(4,128)(2,1)} %param.14) | copy-start | bytes 2064388
  7.2 8.4 %copy-start.4 = (f32[26,384]{1,0:T(8,128)S(1)}, f32[26,384]{1,0:T(8,128)}, u32[]{:S(2)}) copy-start(f32[26,384]{1,0:T(8,128)} %param.10) | copy-start | bytes 119812
  7.2 73.6 %all-gather.3.cloned.1.call-start = ((), (), s32[]{:S(2)}) async-start(), calls=%async_computation.2 | async-start | bytes 4014080 | tf_op jit(solution)/shard_map/all_gather | solution.py:245
  9.7 6.0 %collective-permute-start = (bf16[32,384]{1,0:T(8,128)(2,1)}, bf16[32,384]{1,0:T(8,128)(2,1)S(1)}, u32[]{:S(2)}, u32[]{:S(2)}) collective-permute-start(bf16[32,384]{1,0:T(8,128)(2,1)} %get-tuple-element.12), channel_id=1, source_target_pairs={{0,8},{8,0},{1,9},{9,1},{2,10},{10,2},{3,11},{11,3},{4,12},{12,4},... | collective-permute-start | bytes 73736 | tf_op jit(solution)/shard_map/ppermute | solution.py:233
  17.4 49.6 %all-to-all-start = ((bf16[32,32,384]{2,1,0:T(8,128)(2,1)}), bf16[32,32,384]{2,1,0:T(8,128)(2,1)S(1)}, u32[]{:S(2)}, u32[]{:S(2)}) async-start(bf16[32,32,384]{2,1,0:T(8,128)(2,1)} %bitcast.3), calls=%async_computation | async-start | bytes 1572864 | tf_op jit(solution)/shard_map/all_to_all | solution.py:257
  26.9 14.7 %collective-permute-start.1 = (bf16[120,896]{1,0:T(8,128)(2,1)S(1)}, bf16[120,896]{1,0:T(8,128)(2,1)S(1)}, u32[]{:S(2)}, u32[]{:S(2)}) collective-permute-start(bf16[120,896]{1,0:T(8,128)(2,1)S(1)} %pad_maximum_fusion.refs_6_), channel_id=1, source_target_pairs={{0,16},{4,116},{16,32},{20,4},{32,48},{36,20},{48,64},{52,36},{64,... | collective-permute-start | bytes 645128 | tf_op jit(solution)/shard_map/ppermute | solution.py:162
  30.2 16.1 %collective-permute-start.2 = (bf16[120,896]{1,0:T(8,128)(2,1)S(1)}, bf16[120,896]{1,0:T(8,128)(2,1)S(1)}, u32[]{:S(2)}, u32[]{:S(2)}) collective-permute-start(bf16[120,896]{1,0:T(8,128)(2,1)S(1)} %pad_maximum_fusion.refs_6_), channel_id=1, source_target_pairs={{4,16},{0,116},{20,32},{16,4},{36,48},{32,20},{52,64},{48,36},{68,... | collective-permute-start | bytes 645128 | tf_op jit(solution)/shard_map/ppermute | solution.py:162
  41.5 10.3 %collective-permute-start.3 = (bf16[120,896]{1,0:T(8,128)(2,1)S(1)}, bf16[120,896]{1,0:T(8,128)(2,1)S(1)}, u32[]{:S(2)}, u32[]{:S(2)}) collective-permute-start(bf16[120,896]{1,0:T(8,128)(2,1)S(1)} %collective-permute-done.1.refs_0_), channel_id=1, source_target_pairs={{0,16},{4,116},{16,32},{20,4},{32,48},{36,20},{48,64},{52,36},{64,... | collective-permute-start | bytes 645128 | tf_op jit(solution)/shard_map/ppermute | solution.py:162
  46.3 10.0 %collective-permute-start.4 = (bf16[120,896]{1,0:T(8,128)(2,1)S(1)}, bf16[120,896]{1,0:T(8,128)(2,1)S(1)}, u32[]{:S(2)}, u32[]{:S(2)}) collective-permute-start(bf16[120,896]{1,0:T(8,128)(2,1)S(1)} %collective-permute-done.2.refs_1_), channel_id=1, source_target_pairs={{0,16},{4,116},{16,32},{20,4},{32,48},{36,20},{48,64},{52,36},{64,... | collective-permute-start | bytes 645128 | tf_op jit(solution)/shard_map/ppermute | solution.py:162
  51.8 11.8 %collective-permute-start.5 = (bf16[120,896]{1,0:T(8,128)(2,1)S(1)}, bf16[120,896]{1,0:T(8,128)(2,1)S(1)}, u32[]{:S(2)}, u32[]{:S(2)}) collective-permute-start(bf16[120,896]{1,0:T(8,128)(2,1)S(1)} %collective-permute-done.3.refs_2_), channel_id=1, source_target_pairs={{0,16},{4,116},{16,32},{20,4},{32,48},{36,20},{48,64},{52,36},{64,... | collective-permute-start | bytes 645128 | tf_op jit(solution)/shard_map/ppermute | solution.py:162
  56.3 12.0 %collective-permute-start.6 = (bf16[120,896]{1,0:T(8,128)(2,1)S(1)}, bf16[120,896]{1,0:T(8,128)(2,1)S(1)}, u32[]{:S(2)}, u32[]{:S(2)}) collective-permute-start(bf16[120,896]{1,0:T(8,128)(2,1)S(1)} %collective-permute-done.4.refs_3_), channel_id=1, source_target_pairs={{0,16},{4,116},{16,32},{20,4},{32,48},{36,20},{48,64},{52,36},{64,... | collective-permute-start | bytes 645128 | tf_op jit(solution)/shard_map/ppermute | solution.py:162
  63.6 12.2 %collective-permute-start.7 = (bf16[120,896]{1,0:T(8,128)(2,1)S(1)}, bf16[120,896]{1,0:T(8,128)(2,1)S(1)}, u32[]{:S(2)}, u32[]{:S(2)}) collective-permute-start(bf16[120,896]{1,0:T(8,128)(2,1)S(1)} %collective-permute-done.5.refs_4_), channel_id=1, source_target_pairs={{0,16},{4,116},{16,32},{20,4},{32,48},{36,20},{48,64},{52,36},{64,... | collective-permute-start | bytes 645128 | tf_op jit(solution)/shard_map/ppermute | solution.py:162
  67.1 8.8 %copy-start.2 = (bf16[32,32,384]{2,1,0:T(8,128)(2,1)}, bf16[32,32,384]{2,1,0:T(8,128)(2,1)S(1)}, u32[]{:S(2)}) copy-start(bf16[32,32,384]{2,1,0:T(8,128)(2,1)S(1)} %all-to-all-done.keys) | copy-start | bytes 2359300
  80.8 11.6 %copy-start.3 = (bf16[26,4,896]{2,1,0:T(4,128)(2,1)S(1)}, bf16[26,4,896]{2,1,0:T(4,128)(2,1)}, u32[]{:S(2)}) copy-start(bf16[26,4,896]{2,1,0:T(4,128)(2,1)} %param.13) | copy-start | bytes 559108
  80.8 11.7 %copy-start.6 = (s32[26,2]{0,1:T(2,128)S(1)}, s32[26,2]{0,1:T(2,128)}, u32[]{:S(2)}) copy-start(s32[26,2]{0,1:T(2,128)} %param.12) | copy-start | bytes 628
  80.9 12.0 %copy-start.5 = (f32[896]{0:T(1024)S(1)}, f32[896]{0:T(1024)}, u32[]{:S(2)}) copy-start(f32[896]{0:T(1024)} %param.15) | copy-start | bytes 10756
  80.9 39.5 %all-to-all-start.1 = ((bf16[64,16,1024]{2,1,0:T(8,128)(2,1)}), bf16[64,16,1024]{2,1,0:T(8,128)(2,1)}, u32[]{:S(2)}, u32[]{:S(2)}) async-start(bf16[64,16,1024]{2,1,0:T(8,128)(2,1)} %shard_map.114), calls=%async_computation.1 | async-start | bytes 4194304 | tf_op jit(solution)/shard_map/all_to_all | solution.py:277
  92.9 1.9 %copy-start.1 = (bf16[1792,896]{1,0:T(8,128)(2,1)S(1)}, bf16[1792,896]{1,0:T(8,128)(2,1)}, u32[]{:S(2)}) copy-start(bf16[1792,896]{1,0:T(8,128)(2,1)} %all-gather.3.cloned.1.call-done) | copy-start | bytes 9633796
Sparse Core Ops, SparseCore 0:
  10.1 55.2 all-gather.2
